TPU v7x, 32 devices: a whole 2x2x4 slice. The times are simulated.
32 devices in a mesh: blk: 2 (over y), ctx: 4 (over x, core), tp: 4 (over z).
Axes of the slice: x: 2, y: 2, z: 4, core: 2. Of those that a mesh axis runs over, the one named last changes fastest.
Arguments:
- inputs: bfloat16 [2, 1024, 1024], P(None, ('blk', 'ctx')), may hold values from -6 to 6
- cotangent: bfloat16 [2, 1024, 1024], P(None, ('blk', 'ctx')), may hold values from -6 to 6
- matrices: float32 [192, 65536], P('tp', 'blk')
- momenta: float32 [192, 65536], P('tp', 'blk'), may hold values from -80 to 80
- small: float32 [13312], replicated
- small_first: float32 [13312], replicated, may hold values from -28 to 28
- small_second: float32 [13312], replicated, may hold values from 20.48 to 409.6
- segments: int32 [2, 1024], replicated, may hold values from 0 to 1023, as said below
- positions: int32 [2, 1024], P(None, ('blk', 'ctx')), may hold values from 0 to 2046, as said below
Outputs:
- block_output: float32 [2, 1024, 1024], P(None, ('blk', 'ctx'))
- input_grad: float32 [2, 1024, 1024], P(None, ('blk', 'ctx'))
- matrix_grads: float32 [192, 65536], P('tp', 'blk')
- new_matrices: float32 [192, 65536], P('tp', 'blk')
- new_momenta: float32 [192, 65536], P('tp', 'blk')
- small_grads: float32 [13312], replicated
- new_first: float32 [13312], replicated
- new_second: float32 [13312], replicated
- new_small: float32 [13312], replicated
Inputs may be any that keep to these rules, and one draw needn't show every extreme that they name: `segments`: along a sequence the numbers never fall; each token's number is the index of its document's first token; the last token of a sequence starts a document of its own. Within a document positions rise by one from token to token; the first token of a sequence has 0.
All inputs are finite; a program needn't handle non-finite values.
Results may differ from a plain program's by a relative error of at most 0.012.
Values may be sent and summed in bfloat16 or wider, within the bound.
No kernel may reach another device: no remote copies, remote signals or barrier semaphores. Data moves between devices by JAX's collectives and lax.ppermute only.
A program may use at most 256 MiB of HBM per device.

v0:
```python
import jax
import jax.numpy as jnp
from jax import lax
from jax.sharding import PartitionSpec as P

MODEL_DIM = 1024
H = 16
HD = 64
FF = 4096
ROTARY = 16
NEWTON = 5
STEP = 10


norm_epsilon = 1e-05
rope_base = 10000.0
masked_score = -1e30
momentum_decay = 0.95
muon_rate = 0.2
weight_decay = 0.01
muon_epsilon = 1e-07
quintic = (3.4445, -4.775, 2.0315)
adam_first = 0.9
adam_second = 0.95
adam_epsilon = 1e-08
small_rate = 0.2


def passed_along(x, axis, by):
    devices = lax.axis_size(axis)
    pairs = [(i, i + by) for i in range(devices) if 0 <= i + by < devices]
    return lax.ppermute(x, axis, pairs)


def shifted(x, axis, by):
    devices = lax.axis_size(axis)
    return lax.ppermute(x, axis, [(i, (i + by) % devices) for i in range(devices)])


def as_sent(x):

    def short(part):
        return part.astype(jnp.bfloat16) if part.dtype == jnp.float32 else part

    return jax.tree.map(short, x)


def layer_norm(values, scaling, offset):
    centre = jnp.mean(values, axis=-1, keepdims=True)
    centred = values - centre
    spread = jnp.mean(centred * centred, axis=-1, keepdims=True)
    return centred * lax.rsqrt(spread + norm_epsilon) * scaling + offset


def rope_tables(positions):
    halfway = ROTARY // 2
    frequency = rope_base ** (-2.0 * jnp.arange(halfway, dtype=jnp.float32) / ROTARY)
    angles = positions.astype(jnp.float32)[..., None] * frequency
    return (jnp.cos(angles)[:, :, None, :], jnp.sin(angles)[:, :, None, :])


def rotate(values, cosine, sine):
    halfway = ROTARY // 2
    former = values[..., :halfway]
    latter = values[..., halfway:ROTARY]
    return jnp.concatenate(
        [former * cosine - latter * sine, latter * cosine + former * sine, values[..., ROTARY:]],
        axis=-1,
    )


def exact_gelu(values):
    return jax.nn.gelu(values, approximate=False)


def newton_schulz(blocks):
    frobenius = jnp.sqrt(jnp.sum(blocks * blocks, axis=(1, 2), keepdims=True))
    current = blocks / (frobenius + muon_epsilon)
    linear_term, square_term, cubic_term = quintic
    for iteration in range(NEWTON):
        gram_matrix = jnp.einsum("mde,mdf->mef", current, current, precision=lax.Precision.HIGHEST)
        polynomial = square_term * gram_matrix + cubic_term * jnp.einsum(
            "mef,mfg->meg", gram_matrix, gram_matrix, precision=lax.Precision.HIGHEST
        )
        current = linear_term * current + jnp.einsum(
            "mde,mef->mdf", current, polynomial, precision=lax.Precision.HIGHEST
        )
    return current


def to_heads(values):
    return lax.all_to_all(values, "ctx", split_axis=3, concat_axis=1, tiled=True)


def to_positions(values):
    return lax.all_to_all(values, "ctx", split_axis=1, concat_axis=3, tiled=True)


def pass_keys(pair):
    return passed_along(pair, "blk", 1)


def pass_grads(pair_grad):
    return shifted(pair_grad.astype(jnp.bfloat16), "blk", 1).astype(pair_grad.dtype)


def allowed_pairs(segments, query_block, key_block, block_rows):
    query_place = query_block * block_rows + jnp.arange(block_rows, dtype=jnp.int32)
    key_place = key_block * block_rows + jnp.arange(block_rows, dtype=jnp.int32)
    query_doc = lax.dynamic_slice_in_dim(segments, query_block * block_rows, block_rows, 1)
    key_doc = lax.dynamic_slice_in_dim(segments, key_block * block_rows, block_rows, 1)
    causal = key_place[None, :] <= query_place[:, None]
    return (causal[None] & (query_doc[:, :, None] == key_doc[:, None, :]))[:, None]


def masked_scores(queries, keys, allowed):
    score_scale = HD ** (-0.5)
    scores = (
        jnp.einsum("sqhe,skhe->shqk", queries, keys, preferred_element_type=jnp.float32)
        * score_scale
    )
    return jnp.where(allowed, scores, masked_score)


def on_device(
    inputs, cotangent, matrices, momenta, small, small_first, small_second, segments, positions
):
    tensor_size = lax.axis_size("tp")
    cycle_size = lax.axis_size("blk")
    context_size = lax.axis_size("ctx")
    tensor_index = lax.axis_index("tp")
    cycle_index = lax.axis_index("blk")
    sequences, local_rows, model_width = inputs.shape
    per_group = matrices.shape[0]
    head_count = H // tensor_size
    unit_blocks = FF // HD // tensor_size
    block_rows = local_rows * context_size
    gathered = lax.all_gather(matrices.astype(jnp.bfloat16), "blk", axis=1, tiled=True).reshape(
        per_group, model_width, HD
    )
    query_key_value_weight = gathered[: 3 * head_count]
    projection_out_weight = gathered[3 * head_count : 4 * head_count]
    input_weight = gathered[4 * head_count : 4 * head_count + unit_blocks]
    down_projection_weight = gathered[4 * head_count + unit_blocks :]
    qkv_start = 6 * model_width + tensor_index * head_count * 3 * HD
    query_key_value_bias = lax.dynamic_slice_in_dim(small, qkv_start, head_count * 3 * HD).reshape(
        head_count, 3, HD
    )
    unit_start = 6 * model_width + H * 3 * HD + tensor_index * unit_blocks * HD
    hidden_unit_bias = lax.dynamic_slice_in_dim(small, unit_start, unit_blocks * HD).reshape(
        unit_blocks, HD
    )
    residual = inputs.astype(jnp.float32)

    def both_norms(values, gain_one, offset_one, gain_two, offset_two):
        return (layer_norm(values, gain_one, offset_one), layer_norm(values, gain_two, offset_two))

    (normed_one, normed_two), norm_back = jax.vjp(
        both_norms,
        residual,
        small[0:model_width],
        small[model_width : 2 * model_width],
        small[2 * model_width : 3 * model_width],
        small[3 * model_width : 4 * model_width],
    )
    first_input = normed_one.astype(jnp.bfloat16)
    second_input = normed_two.astype(jnp.bfloat16)
    projected = jnp.einsum(
        "pgk,jka->pgja", first_input, query_key_value_weight, preferred_element_type=jnp.float32
    )
    projected = projected.reshape(sequences, local_rows, 3, head_count, HD) + jnp.transpose(
        query_key_value_bias, (1, 0, 2)
    )
    cosine, sine = rope_tables(positions)

    def turn_pair(query_pre, key_pre):
        return (rotate(query_pre, cosine, sine), rotate(key_pre, cosine, sine))

    (query_turned, key_turned), turn_back = jax.vjp(
        turn_pair, projected[:, :, 0], projected[:, :, 1]
    )
    stacked = jnp.stack([query_turned, key_turned, projected[:, :, 2]], axis=2).astype(jnp.bfloat16)
    by_heads = to_heads(stacked)
    queries = by_heads[:, :, 0]
    head_local = queries.shape[2]

    def forward_visit(state, pair, source):
        row_max, row_total, weighted = state
        allowed = allowed_pairs(segments, cycle_index, source, block_rows)
        scores = masked_scores(queries, pair[:, :, 0], allowed)
        new_max = jnp.maximum(row_max, jnp.max(scores, axis=-1))
        weights = jnp.where(allowed, jnp.exp(scores - new_max[..., None]), 0.0)
        rescale = jnp.exp(row_max - new_max)
        row_total = row_total * rescale + jnp.sum(weights, axis=-1)
        weighted = weighted * rescale[..., None] + jnp.einsum(
            "shqk,skhe->shqe",
            weights.astype(jnp.bfloat16),
            pair[:, :, 1],
            preferred_element_type=jnp.float32,
        )
        return (new_max, row_total, weighted)

    def forward_hop(hop_index, carry):
        pair, state = carry
        source = (cycle_index - hop_index) % cycle_size
        state = forward_visit(state, pair, source)
        return (pass_keys(pair), state)

    start_state = (
        jnp.full((sequences, head_local, block_rows), masked_score, jnp.float32),
        jnp.zeros((sequences, head_local, block_rows), jnp.float32),
        jnp.zeros((sequences, head_local, block_rows, HD), jnp.float32),
    )
    pair, state = lax.fori_loop(0, cycle_size - 1, forward_hop, (by_heads[:, :, 1:], start_state))
    row_max, row_total, weighted = forward_visit(state, pair, (cycle_index + 1) % cycle_size)
    log_total = row_max + jnp.log(row_total)
    attended_rows = jnp.transpose(weighted / row_total[..., None], (0, 2, 1, 3))
    attention_result = to_positions(attended_rows.astype(jnp.bfloat16)[:, :, None])[:, :, 0]
    attention_branch = jnp.einsum(
        "roxu,xcu->roc", attention_result, projection_out_weight, preferred_element_type=jnp.float32
    )
    hidden_preactivation = (
        jnp.einsum("ptr,kra->ptka", second_input, input_weight, preferred_element_type=jnp.float32)
        + hidden_unit_bias
    )
    activated_hidden, gelu_back = jax.vjp(exact_gelu, hidden_preactivation)
    activated_reduced = activated_hidden.astype(jnp.bfloat16)
    perceptron_branch = jnp.einsum(
        "xkzp,zop->xko",
        activated_reduced,
        down_projection_weight,
        preferred_element_type=jnp.float32,
    )
    branches = lax.psum((attention_branch + perceptron_branch).astype(jnp.bfloat16), "tp").astype(
        jnp.float32
    )
    block_output = (
        residual
        + branches
        + small[4 * model_width : 5 * model_width]
        + small[5 * model_width : 6 * model_width]
    )
    act_grad = jnp.einsum(
        "ptr,kra->ptka", cotangent, down_projection_weight, preferred_element_type=jnp.float32
    )
    hidden_gradient = gelu_back(act_grad)[0].astype(jnp.bfloat16)
    down_grad = jnp.einsum(
        "gup,guzb->zpb", cotangent, activated_reduced, preferred_element_type=jnp.float32
    )
    in_grad = jnp.einsum(
        "gup,guzb->zpb", second_input, hidden_gradient, preferred_element_type=jnp.float32
    )
    second_grad = jnp.einsum(
        "xkzp,zop->xko", hidden_gradient, input_weight, preferred_element_type=jnp.float32
    )
    attended_grad = jnp.einsum(
        "pgk,jka->pgja", cotangent, projection_out_weight, preferred_element_type=jnp.float32
    ).astype(jnp.bfloat16)
    outproj_grad = jnp.einsum(
        "ztu,ztqi->qui", cotangent, attention_result, preferred_element_type=jnp.float32
    )
    grad_heads = to_heads(attended_grad[:, :, None])[:, :, 0]
    row_delta = jnp.transpose(
        jnp.sum(grad_heads.astype(jnp.float32) * attended_rows, axis=-1), (0, 2, 1)
    )

    def backward_visit(query_grad, pair, source):
        allowed = allowed_pairs(segments, cycle_index, source, block_rows)
        scores = masked_scores(queries, pair[:, :, 0], allowed)
        probabilities = jnp.where(allowed, jnp.exp(scores - log_total[..., None]), 0.0)
        value_grad = jnp.einsum(
            "shqk,sqhe->skhe",
            probabilities.astype(jnp.bfloat16),
            grad_heads,
            preferred_element_type=jnp.float32,
        )
        prob_grad = jnp.einsum(
            "sqhe,skhe->shqk", grad_heads, pair[:, :, 1], preferred_element_type=jnp.float32
        )
        score_grad = (probabilities * (prob_grad - row_delta[..., None])).astype(jnp.bfloat16)
        score_scale = HD ** (-0.5)
        query_grad = (
            query_grad
            + jnp.einsum(
                "shqk,skhe->sqhe", score_grad, pair[:, :, 0], preferred_element_type=jnp.float32
            )
            * score_scale
        )
        key_grad = (
            jnp.einsum("shqk,sqhe->skhe", score_grad, queries, preferred_element_type=jnp.float32)
            * score_scale
        )
        return (query_grad, jnp.stack([key_grad, value_grad], axis=2))

    def backward_hop(hop_index, carry):
        pair, pair_grad, query_grad = carry
        source = (cycle_index - hop_index) % cycle_size
        query_grad, visit_grad = backward_visit(query_grad, pair, source)
        return (pass_keys(pair), pass_grads(pair_grad + visit_grad), query_grad)

    zero_pair = jnp.zeros(by_heads[:, :, 1:].shape, jnp.float32)
    pair, pair_grad, query_grad = lax.fori_loop(
        0,
        cycle_size - 1,
        backward_hop,
        (by_heads[:, :, 1:], zero_pair, jnp.zeros(queries.shape, jnp.float32)),
    )
    query_grad, visit_grad = backward_visit(query_grad, pair, (cycle_index + 1) % cycle_size)
    pair_grad = pass_grads(pair_grad + visit_grad)
    head_grads = jnp.concatenate([query_grad[:, :, None], pair_grad], axis=2).astype(jnp.bfloat16)
    position_grads = to_positions(head_grads).astype(jnp.float32)
    query_pre_grad, key_pre_grad = turn_back((position_grads[:, :, 0], position_grads[:, :, 1]))
    projected_grad = jnp.stack(
        [query_pre_grad, key_pre_grad, position_grads[:, :, 2]], axis=2
    ).astype(jnp.bfloat16)
    flattened_gradient = projected_grad.reshape(sequences, local_rows, 3 * head_count, HD)
    query_key_value_gradient = jnp.einsum(
        "ztu,ztqi->qui", first_input, flattened_gradient, preferred_element_type=jnp.float32
    )
    first_grad = jnp.einsum(
        "roxu,xcu->roc",
        flattened_gradient,
        query_key_value_weight,
        preferred_element_type=jnp.float32,
    )
    input_part, gain_one_grad, offset_one_grad, gain_two_grad, offset_two_grad = norm_back(
        (first_grad, second_grad)
    )
    input_grad = cotangent.astype(jnp.float32) + lax.psum(
        input_part.astype(jnp.bfloat16), "tp"
    ).astype(jnp.float32)
    owner_share = jnp.where(tensor_index == 0, 1.0, 0.0).astype(jnp.float32)
    bias_grad = jnp.sum(cotangent.astype(jnp.float32), axis=(0, 1)) * owner_share
    qkv_bias_grad = jnp.transpose(
        jnp.sum(projected_grad.astype(jnp.float32), axis=(0, 1)), (1, 0, 2)
    ).reshape(-1)
    unit_bias_grad = jnp.sum(hidden_gradient.astype(jnp.float32), axis=(0, 1)).reshape(-1)
    local_small = jnp.concatenate(
        [
            gain_one_grad,
            offset_one_grad,
            gain_two_grad,
            offset_two_grad,
            bias_grad,
            bias_grad,
            jnp.zeros((small.shape[0] - 6 * model_width,), jnp.float32),
        ]
    )
    local_small = lax.dynamic_update_slice_in_dim(local_small, qkv_bias_grad, qkv_start, 0)
    local_small = lax.dynamic_update_slice_in_dim(local_small, unit_bias_grad, unit_start, 0)
    small_grads = lax.psum(local_small, ("blk", "ctx", "tp"))
    local_grad = jnp.concatenate(
        [query_key_value_gradient, outproj_grad, in_grad, down_grad], axis=0
    ).reshape(per_group, -1)
    shares = lax.psum_scatter(
        local_grad.astype(jnp.bfloat16), "blk", scatter_dimension=1, tiled=True
    )
    matrix_grads = lax.psum(shares, "ctx").astype(jnp.float32)
    new_momenta = momentum_decay * momenta + matrix_grads
    update = matrix_grads + momentum_decay * new_momenta
    per_owner = per_group // cycle_size
    sectioned = update.reshape(cycle_size, per_owner, update.shape[1])
    pieces = lax.all_to_all(
        sectioned.astype(jnp.bfloat16), "blk", split_axis=0, concat_axis=2, tiled=True
    ).astype(sectioned.dtype)
    piece_count = pieces.shape[1]
    settled_blocks = newton_schulz(pieces.reshape(piece_count, MODEL_DIM, HD)).reshape(
        1, piece_count, MODEL_DIM * HD
    )
    settled = lax.all_to_all(
        as_sent(settled_blocks), "blk", split_axis=2, concat_axis=0, tiled=True
    ).astype(settled_blocks.dtype)
    orthogonal_all = settled.reshape(per_group, -1)
    muon_scale = max(1.0, MODEL_DIM / HD) ** 0.5
    new_matrices = matrices - muon_rate * (muon_scale * orthogonal_all + weight_decay * matrices)
    new_first = adam_first * small_first + (1.0 - adam_first) * small_grads
    new_second = adam_second * small_second + (1.0 - adam_second) * small_grads * small_grads
    corrected = new_first / (1.0 - adam_first**STEP)
    spread = jnp.sqrt(new_second / (1.0 - adam_second**STEP))
    new_small = small - small_rate * corrected / (spread + adam_epsilon)
    return (
        block_output,
        input_grad,
        matrix_grads,
        new_matrices,
        new_momenta,
        small_grads,
        new_first,
        new_second,
        new_small,
    )


def solution(mesh):
    in_specs = (
        P(None, ("blk", "ctx"), None),
        P(None, ("blk", "ctx"), None),
        P("tp", "blk"),
        P("tp", "blk"),
        P(),
        P(),
        P(),
        P(),
        P(None, ("blk", "ctx")),
    )
    out_specs = (
        P(None, ("blk", "ctx"), None),
        P(None, ("blk", "ctx"), None),
        P("tp", "blk"),
        P("tp", "blk"),
        P("tp", "blk"),
        P(),
        P(),
        P(),
        P(),
    )
    return jax.shard_map(
        on_device, mesh=mesh, in_specs=in_specs, out_specs=out_specs, check_vma=False
    )
```

profile of v0, /device:TPU:0, one launch (start us, length us, event | category | flops | bytes accessed | tf_op | source)
XLA Modules:
  0.0 1227.2 jit_solution(8957831343607342331)
XLA Ops:
  17.0 78.4 %all-gather.2.cloned.1.call-done = bf16[48,65536]{1,0:T(8,128)(2,1)} async-done(((bf16[48,32768]{1,0:T(8,128)(2,1)}), bf16[48,65536]{1,0:T(8,128)(2,1)}) %all-gather.2.cloned.1.call-update) | async-done | bytes 6291472 | tf_op jit(solution)/shard_map/all_gather | solution.py:138
  216.6 12.0 copy.267
  228.6 12.9 %convert_element_type.219 = bf16[48,65536]{1,0:T(8,128)(2,1)} reshape(bf16[48,1024,64]{2,1,0:T(8,128)(2,1)} %copy.267) | data formatting | bytes 12582912 | tf_op jit(solution)/shard_map/convert_element_type | solution.py:356
  242.2 75.8 %reduce-scatter.2.cloned.1.call-done = bf16[48,32768]{1,0:T(8,128)(2,1)} async-done(((bf16[48,65536]{1,0:T(8,128)(2,1)}), bf16[48,32768]{1,0:T(8,128)(2,1)}) %reduce-scatter.2.cloned.1.call-update) | async-done | bytes 3145744 | tf_op jit(solution)/shard_map/reduce_scatter | solution.py:355
  331.0 58.0 %all-reduce.10.cloned.1.call-done = bf16[48,32768]{1,0:T(8,128)(2,1)} async-done(((bf16[48,32768]{1,0:T(8,128)(2,1)}), bf16[48,32768]{1,0:T(8,128)(2,1)}) %all-reduce.10.cloned.1.call-update) | async-done | bytes 3145744 | tf_op jit(solution)/shard_map/psum | solution.py:358
  389.0 10.8 add_convert_fusion.1
  409.9 30.1 %all-to-all-done.4 = bf16[2,24,32768]{2,1,0:T(8,128)(2,1)S(1)} async-done(((bf16[2,24,32768]{2,1,0:T(8,128)(2,1)}), bf16[2,24,32768]{2,1,0:T(8,128)(2,1)S(1)}, u32[]{:S(2)}, u32[]{:S(2)}) %all-to-all-start.4) | async-done | bytes 3145760 | tf_op jit(solution)/shard_map/all_to_all | solution.py:363
  443.1 10.3 copy.268
  453.5 13.7 %reshape.522 = f32[24,1024,64]{2,1,0:T(8,128)} reshape(f32[1,24,2,32768]{3,2,1,0:T(2,128)} %copy.268) | data formatting | bytes 12582912 | tf_op jit(solution)/shard_map/convert_element_type | solution.py:365
  467.2 9.7 copy.269
  477.6 11.5 fusion.63
  490.2 7.2 multiply_add_fusion.3
  504.7 6.9 multiply_add_fusion.2
  518.8 6.9 multiply_add_fusion.1
  533.1 7.0 multiply_add_fusion
  558.1 6.5 convert_element_type.229
  564.6 49.2 %copy.276 = bf16[1,24,65536]{1,0,2:T(2,128)(2,1)} copy(bf16[1,24,65536]{2,1,0:T(8,128)(2,1)S(1)} %convert_element_type.229) | data formatting | bytes 6291456 | tf_op jit(solution)/shard_map/convert_element_type | solution.py:43
  614.3 355.9 %reduce.18 = bf16[65536,24]{1,0:T(8,128)(2,1)} reduce(bf16[65536,1,24]{2,1,0:T(2,128)(2,1)} %bitcast.296, bf16[]{:T(256)} %broadcast.393), dimensions={1}, to_apply=%bitcast.231.reduce_sub_computation | reduce | bytes 6291458
  970.2 31.5 %reshape.550 = bf16[2,2,393216]{2,1,0:T(2,128)(2,1)} reshape(bf16[65536,24]{1,0:T(8,128)(2,1)} %reduce.18) | data formatting | bytes 6291456
  1009.9 66.8 %psum.31 = f32[13312]{0:T(1024)S(1)} all-reduce(f32[13312]{0:T(1024)S(1)} %dynamic_update_slice.7), channel_id=1, replica_groups=mesh['blk'=2,'ctx'=4,'tp'=4] {'blk','ctx','tp'}, use_global_device_ids=true, to_apply=%region_23.24 | all-reduce | flops 13312 | bytes 106496 | tf_op jit(solution)/shard_map/psum | solution.py:351
  1079.7 58.4 %reshape.551 = bf16[65536,1,24]{2,1,0:T(2,128)(2,1)} reshape(bf16[2,2,393216]{2,1,0:T(2,128)(2,1)} %all-to-all-done.5) | data formatting | bytes 6291456
  1138.1 60.1 %copy.277 = bf16[1,24,65536]{2,1,0:T(8,128)(2,1)S(1)} copy(bf16[1,24,65536]{1,0,2:T(2,128)(2,1)} %bitcast.297) | data formatting | bytes 6291456 | tf_op jit(solution)/shard_map/all_to_all | solution.py:370
  1201.3 8.9 mul.599
  1210.2 6.6 copy.278
  (261 shorter events, 217.0 us)
Async XLA Ops:
  7.2 88.2 %all-gather.2.cloned.1.call-start = ((), (), s32[]{:S(2)}) async-start(), calls=%async_computation.7 | async-start | bytes 9437184 | tf_op jit(solution)/shard_map/all_gather | solution.py:138
  12.9 88.1 %copy-start.31 = (f32[1024]{0:T(1024)}, f32[1024]{0:T(1024)S(1)}, u32[]{:S(2)}) copy-start(f32[1024]{0:T(1024)S(1)} %get-tuple-element.122) | copy-start | bytes 12292
  14.4 86.6 %copy-start.28 = (f32[2,128]{1,0:T(2,128)}, f32[2,128]{1,0:T(2,128)S(1)}, u32[]{:S(2)}) copy-start(f32[2,128]{1,0:T(2,128)S(1)} %broadcast_multiply_fusion) | copy-start | bytes 3076
  15.2 85.8 %copy-start.33 = (f32[2,128]{1,0:T(2,128)}, f32[2,128]{1,0:T(2,128)S(1)}, u32[]{:S(2)}) copy-start(f32[2,128]{1,0:T(2,128)S(1)} %fusion.125) | copy-start | bytes 3076
  17.0 151.1 %copy-start.11 = (pred[512,512]{0,1:T(8,128)(4,1)}, pred[512,512]{0,1:T(8,128)(4,1)S(1)}, u32[]{:S(2)}) copy-start(pred[512,512]{0,1:T(8,128)(4,1)S(1)} %get-tuple-element.135) | copy-start | bytes 786436
  109.1 35.2 %all-to-all-start.2 = ((bf16[2,128,1,4,64]{1,4,0,2,3:T(8,128)(2,1)}), bf16[2,128,1,4,64]{1,4,0,2,3:T(8,128)(2,1)S(1)}, u32[]{:S(2)}, u32[]{:S(2)}) async-start(bf16[2,128,1,4,64]{1,4,0,2,3:T(8,128)(2,1)} %copy.251), calls=%async_computation.2 | async-start | bytes 262144 | tf_op jit(solution)/shard_map/all_to_all | solution.py:92
  144.3 10.9 all-to-all-start
  155.7 7.7 collective-permute-start
  171.1 7.8 collective-permute-start.1
  179.6 9.4 collective-permute-start.2
  184.3 10.3 all-to-all-start.1
  194.6 11.6 all-to-all-start.3
  198.7 119.3 %reduce-scatter.2.cloned.1.call-start = ((), (), s32[]{:S(2)}) async-start(), calls=%async_computation.8 | async-start | bytes 9437184 | tf_op jit(solution)/shard_map/reduce_scatter | solution.py:355
  241.5 76.6 %copy-start.14 = (bf16[2,128,16,64]{1,3,2,0:T(8,128)(2,1)S(1)}, bf16[2,128,16,64]{1,3,2,0:T(8,128)(2,1)}, u32[]{:S(2)}) copy-start(bf16[2,128,16,64]{1,3,2,0:T(8,128)(2,1)} %get-tuple-element.146) | copy-start | bytes 1572868
  241.5 147.5 %all-reduce.10.cloned.1.call-start = ((), (), s32[]{:S(2)}) async-start(), calls=%async_computation.9 | async-start | bytes 6291456 | tf_op jit(solution)/shard_map/psum | solution.py:358
  399.8 40.2 %all-to-all-start.4 = ((bf16[2,24,32768]{2,1,0:T(8,128)(2,1)}), bf16[2,24,32768]{2,1,0:T(8,128)(2,1)S(1)}, u32[]{:S(2)}, u32[]{:S(2)}) async-start(bf16[2,24,32768]{2,1,0:T(8,128)(2,1)} %bitcast.301), calls=%async_computation.5 | async-start | bytes 6291456 | tf_op jit(solution)/shard_map/all_to_all | solution.py:363
  403.8 603.3 %all-reduce.12.cloned.1.call-start = ((), (), s32[]{:S(2)}) async-start(), calls=%async_computation.10 | async-start | bytes 2097152 | tf_op jit(solution)/shard_map/psum | solution.py:234
  1001.7 75.1 %copy-start.1 = (bf16[2,128,1024]{2,1,0:T(8,128)(2,1)S(1)}, bf16[2,128,1024]{2,1,0:T(8,128)(2,1)}, u32[]{:S(2)}) copy-start(bf16[2,128,1024]{2,1,0:T(8,128)(2,1)} %param.9) | copy-start | bytes 1572868
  1001.7 75.1 %copy-start.37 = (f32[1024]{0:T(1024)S(1)}, f32[1024]{0:T(1024)}, u32[]{:S(2)}) copy-start(f32[1024]{0:T(1024)} %get-tuple-element.118) | copy-start | bytes 12292
  1001.7 75.1 %copy-start.38 = (f32[1024]{0:T(1024)S(1)}, f32[1024]{0:T(1024)}, u32[]{:S(2)}) copy-start(f32[1024]{0:T(1024)} %get-tuple-element.124) | copy-start | bytes 12292
  1001.7 77.3 %copy-start.21 = (f32[13312]{0:T(1024)S(1)}, f32[13312]{0:T(1024)}, u32[]{:S(2)}) copy-start(f32[13312]{0:T(1024)} %param.13) | copy-start | bytes 159748
  1001.7 77.3 %copy-start.26 = (f32[13312]{0:T(1024)S(1)}, f32[13312]{0:T(1024)}, u32[]{:S(2)}) copy-start(f32[13312]{0:T(1024)} %param.15) | copy-start | bytes 159748
  1001.7 77.3 %copy-start.27 = (f32[13312]{0:T(1024)S(1)}, f32[13312]{0:T(1024)}, u32[]{:S(2)}) copy-start(f32[13312]{0:T(1024)} %param.14) | copy-start | bytes 159748
  1001.7 78.0 %all-to-all-start.5 = ((bf16[2,2,393216]{2,1,0:T(2,128)(2,1)}), bf16[2,2,393216]{2,1,0:T(2,128)(2,1)}, u32[]{:S(2)}, u32[]{:S(2)}) async-start(bf16[2,2,393216]{2,1,0:T(2,128)(2,1)} %reshape.550), calls=%async_computation.6 | async-start | bytes 6291456 | tf_op jit(solution)/shard_map/all_to_all | solution.py:370
  (42 other events, 307.2 us)
Sparse Core Ops, SparseCore 0:
  12.2 83.1 all-gather.1
  241.6 76.3 reduce-scatter.1
  320.5 68.4 all-reduce.9
  410.0 52.7 all-reduce.11
where the time goes:
time: 1240 us; the launch traced here: 1230 us
  other arithmetic  406 us (33%)
  local copies, waits for them, and re-layouts  331 us (27%)
  waiting for transfers between devices  256 us (21%)
  matrix products  121 us (10%)
  blocking collectives  66.8 us (5%)
  starting transfers between devices  31.3 us (3%)
  between operations  15.2 us (1%)
    unnamed x5, other arithmetic  356 us
    unnamed x115, local copies, waits for them, and re-layouts  96.8 us
    all_gather x1, waiting for transfers between devices, on_device(): lax.all_gather(matrices.astype(jnp.bfloat16), 'blk', axis=1, tiled=True)  78.4 us
    reduce_scatter x1, waiting for transfers between devices, on_device(): lax.psum_scatter(local_grad.astype(jnp.bfloat16), 'blk', scatter_dimensio...  75.8 us
    psum x1, blocking collectives, on_device(): small_grads = lax.psum(local_small, ('blk', 'ctx', 'tp'))  66.8 us
    convert_element_type x3, local copies, waits for them, and re-layouts, short(): return part.astype(jnp.bfloat16) if part.dtype == jnp.float32 else part  60.2 us
    all_to_all x1, local copies, waits for them, and re-layouts, on_device(): lax.all_to_all(as_sent(settled_blocks), 'blk', split_axis=2, concat_axis=...  60.1 us
    psum x1, waiting for transfers between devices, on_device(): matrix_grads = lax.psum(shares, 'ctx').astype(jnp.float32)  58 us
  transfers between devices with their start and end apart: 13, of which 8 were waited for; matrix products, arithmetic and copies ran while one was open for 52% of the time, Pallas kernels for 0%

commit v1 on v0

--- a/solution.py
+++ b/solution.py
@@ -1,6 +1,10 @@
+import functools
+
 import jax
 import jax.numpy as jnp
 from jax import lax
+from jax.experimental import pallas as pl
+from jax.experimental.pallas import tpu as pltpu
 from jax.sharding import PartitionSpec as P
 
 MODEL_DIM = 1024
@@ -10,6 +14,7 @@
 ROTARY = 16
 NEWTON = 5
 STEP = 10
+SEQS = 2
 
 
 norm_epsilon = 1e-05
@@ -391,6 +396,604 @@
     )
 
 
+def native_view(array):
+    rows, columns = array.shape
+    tiled = array.reshape(rows // 8, 8, columns // 128, 128).transpose(0, 2, 1, 3)
+    return tiled.reshape(rows // 8, columns // 16, 128)
+
+
+def native_back(array):
+    groups, rows, _ = array.shape
+    return array.reshape(groups, rows // 8, 8, 128).transpose(0, 2, 1, 3).reshape(groups * 8, rows * 16)
+
+
+def piece_members(piece):
+    chunk, place = divmod(piece, 4)
+    if chunk == 0:
+        return [place, 4 + place, 8 + place, 12 + place]
+    return [16 * chunk + 4 * place + j for j in range(4)]
+
+
+def mem(kind=pltpu.VMEM):
+    return pl.BlockSpec(memory_space=kind)
+
+
+def limits(mebibytes):
+    return pltpu.CompilerParams(vmem_limit_bytes=mebibytes << 20)
+
+
+def low_lanes(rows):
+    return lax.broadcasted_iota(jnp.int32, (rows, 128), 1) < HD
+
+
+def dot(a, b, dims=((1,), (0,)), precision=None):
+    return lax.dot_general(
+        a, b, (dims, ((), ())), precision=precision, preferred_element_type=jnp.float32
+    )
+
+
+NT = ((1,), (1,))
+TN = ((0,), (0,))
+
+
+def relayout_kernel(n, src, out, scratch):
+    low = low_lanes(n)
+    for piece in range(12):
+        members = piece_members(piece)
+        for half in range(2):
+            k = 2 * piece + half
+            first, second = members[2 * half : 2 * half + 2]
+            a = src[first // 8, pl.ds(first % 8, n, stride=8), :]
+            b = src[second // 8, pl.ds(second % 8, n, stride=8), :]
+            scratch[k, pl.ds(0, n, stride=2), :] = jnp.where(low, a, pltpu.roll(b, 64, 1))
+            scratch[k, pl.ds(1, n, stride=2), :] = jnp.where(low, pltpu.roll(a, 64, 1), b)
+            out[piece, :, half * 128 : (half + 1) * 128] = scratch[k].astype(out.dtype)
+
+
+def relayout(array, dtype, n=32):
+    return pl.pallas_call(
+        functools.partial(relayout_kernel, n),
+        grid=(256 // n,),
+        in_specs=[pl.BlockSpec((6, 8 * n, 128), lambda i: (0, i, 0))],
+        out_specs=pl.BlockSpec((12, 2 * n, 256), lambda i: (0, i, 0)),
+        out_shape=jax.ShapeDtypeStruct((12, 512, 256), dtype),
+        scratch_shapes=[pltpu.VMEM((24, 2 * n, 128), jnp.float32)],
+        compiler_params=limits(40),
+        name="relayout",
+    )(native_view(array))
+
+
+def normalized(x):
+    centred = x - jnp.mean(x, axis=-1, keepdims=True)
+    spread = jnp.mean(centred * centred, axis=-1, keepdims=True)
+    root = lax.rsqrt(spread + norm_epsilon)
+    return centred * root, root
+
+
+def halves(values, first):
+    left, right = values[:, :512], values[:, 512:]
+    return jnp.where(first, left, right), jnp.where(first, right, left)
+
+
+def whole(own, other, first):
+    return jnp.concatenate([jnp.where(first, own, other), jnp.where(first, other, own)], axis=1)
+
+
+def norm_back(grad, hat, root, gain):
+    scaled = grad * gain
+    along = jnp.mean(scaled * hat, axis=-1, keepdims=True)
+    return root * (scaled - jnp.mean(scaled, axis=-1, keepdims=True) - hat * along)
+
+
+def turned(values, cosine, sine):
+    lane = lax.broadcasted_iota(jnp.int32, values.shape, 1) % HD
+    other = jnp.where(lane < 8, pltpu.roll(values, 120, 1), pltpu.roll(values, 8, 1))
+    return values * cosine + other * sine
+
+
+def project_kernel(scal, x, cot, norms, bias, cosine, sine, own, r0, r1, r2, r3, send, h1):
+    first = scal[0] == 0
+    hat, _ = normalized(x[...].astype(jnp.float32))
+    h = (hat * norms[0:1] + norms[1:2]).astype(jnp.bfloat16)
+    h1[...] = h
+    h_own, h_other = halves(h, first)
+    c_own, c_other = halves(cot[...], first)
+    tokens = h.shape[0]
+    low = low_lanes(tokens)
+    for r, other in enumerate((r0, r1, r2, r3)):
+        head = scal[1] ^ r
+        mine = own[head]
+        theirs = other[...]
+        pre = dot(h_own, mine) + dot(h_other, theirs) + bias[pl.ds(head, 1), :]
+        back = dot(c_own, mine[:, 128:]) + dot(c_other, theirs[:, 128:])
+        left = turned(pre[:, :128], cosine[...], sine[...]).astype(jnp.bfloat16)
+        right = jnp.where(low, pre[:, 128:], back).astype(jnp.bfloat16)
+        for s in range(2):
+            rows = slice(128 * s, 128 * s + 128)
+            send[4 * s + head, :, :128] = left[rows]
+            send[4 * s + head, :, 128:] = right[rows]
+
+
+def attention_kernel(rows_ref, seg, out, key_total, value_total):
+    key_total[...] = jnp.zeros_like(key_total)
+    value_total[...] = jnp.zeros_like(value_total)
+    step = 256
+    for block in range(rows_ref.shape[0] // step):
+        rows = slice(block * step, (block + 1) * step)
+        n = (block + 1) * step
+        query = rows_ref[rows, 0:HD] * jnp.bfloat16(0.125)
+        grad = rows_ref[rows, 3 * HD : 4 * HD]
+        keys = rows_ref[0:n, HD : 2 * HD]
+        values = rows_ref[0:n, 2 * HD : 3 * HD]
+        scores = dot(query, keys, NT)
+        query_place = block * step + lax.broadcasted_iota(jnp.int32, (step, n), 0)
+        key_place = lax.broadcasted_iota(jnp.int32, (step, n), 1)
+        allowed = (key_place <= query_place) & (key_place >= seg[rows, :])
+        scores = jnp.where(allowed, scores, masked_score)
+        weights = jnp.exp(scores - jnp.max(scores, axis=-1, keepdims=True))
+        weights = jnp.where(allowed, weights, 0.0)
+        weights = weights * (1.0 / jnp.sum(weights, axis=-1, keepdims=True))
+        short = weights.astype(jnp.bfloat16)
+        attended = dot(short, values)
+        weight_grad = dot(grad, values, NT)
+        delta = jnp.sum(weights * weight_grad, axis=-1, keepdims=True)
+        score_grad = (weights * (weight_grad - delta)).astype(jnp.bfloat16)
+        query_grad = dot(score_grad, keys) * 0.125
+        key_total[0:n, :] += dot(score_grad, query, TN)
+        value_total[0:n, :] += dot(short, grad, TN)
+        out[rows, 0:HD] = query_grad.astype(jnp.bfloat16)
+        out[rows, 3 * HD : 4 * HD] = attended.astype(jnp.bfloat16)
+    out[:, HD : 2 * HD] = key_total[...].astype(jnp.bfloat16)
+    out[:, 2 * HD : 3 * HD] = value_total[...].astype(jnp.bfloat16)
+
+
+def feed_forward_kernel(
+    scal, x, cot, norms, bias, own_in, own_down, r0, r1, r2, r3,
+    branch, input_part, keep, send, hidden_sums, norm_grads, cot_sums,
+):
+    first = scal[0] == 0
+    hat, root = normalized(x[...].astype(jnp.float32))
+    h = (hat * norms[2:3] + norms[3:4]).astype(jnp.bfloat16)
+    h_own, h_other = halves(h, first)
+    c_own, c_other = halves(cot[...], first)
+    cot_sums[...] = jnp.sum(cot[...].astype(jnp.float32), axis=0, keepdims=True)
+    outs = [0.0] * 4
+    for r, other in enumerate((r0, r1, r2, r3)):
+        piece = scal[1] ^ r
+        in_own, in_other = own_in[piece], other[0]
+        down_own, down_other = own_down[piece], other[1]
+        pre = dot(h_own, in_own) + dot(h_other, in_other) + bias[pl.ds(piece, 1), :]
+        cumulative = 0.5 * (1.0 + lax.erf(pre * 0.7071067811865476))
+        slope = cumulative + pre * (0.3989422804014327 * jnp.exp(-0.5 * pre * pre))
+        act = (pre * cumulative).astype(jnp.bfloat16)
+        act_grad = dot(c_own, down_own) + dot(c_other, down_other)
+        grad = (act_grad * slope).astype(jnp.bfloat16)
+        hidden_sums[pl.ds(piece, 1), :] = jnp.sum(
+            grad.astype(jnp.float32), axis=0, keepdims=True
+        )
+        outs[0] += dot(act, down_own, NT)
+        outs[1] += dot(act, down_other, NT)
+        outs[2] += dot(grad, in_own, NT)
+        outs[3] += dot(grad, in_other, NT)
+        target = send if r % 2 else keep
+        for side, (h_side, c_side) in enumerate(((h_own, c_own), (h_other, c_other))):
+            target[side, r // 2, 0] = dot(h_side, grad, TN).astype(jnp.bfloat16)
+            target[side, r // 2, 1] = dot(c_side, act, TN).astype(jnp.bfloat16)
+    branch[...] = whole(outs[0], outs[1], first)
+    second = whole(outs[2], outs[3], first)
+    norm_grads[0:1] = jnp.sum(second * hat, axis=0, keepdims=True)
+    norm_grads[1:2] = jnp.sum(second, axis=0, keepdims=True)
+    input_part[...] = norm_back(second, hat, root, norms[2:3])
+
+
+def gather_kernel(
+    scal, x, cot, norms, cosine, sine, back, h1, own, r0, r1, r2, r3, ff_branch, ff_part,
+    near, far, keep, send, sums, norm_grads, parts,
+):
+    first = scal[0] == 0
+    hat, root = normalized(x[...].astype(jnp.float32))
+    h_own, h_other = halves(h1[...], first)
+    c_own, c_other = halves(cot[...], first)
+    tokens = h_own.shape[0]
+    low = low_lanes(tokens)
+    outs = [0.0] * 4
+    for r, other in enumerate((r0, r1, r2, r3)):
+        head = scal[1] ^ r
+        mine, theirs = own[head], other[...]
+        grads = jnp.concatenate([back[head], back[4 + head]], axis=0)
+        left = turned(grads[:, :128].astype(jnp.float32), cosine[...], -sine[...])
+        right = grads[:, 128:].astype(jnp.float32)
+        value_grad = jnp.where(low, right, 0.0).astype(jnp.bfloat16)
+        attended = jnp.where(low, 0.0, right).astype(jnp.bfloat16)
+        pre_grad = jnp.concatenate([left.astype(jnp.bfloat16), value_grad], axis=1)
+        sums[pl.ds(head, 1), :] = jnp.sum(pre_grad.astype(jnp.float32), axis=0, keepdims=True)
+        outs[0] += dot(attended, mine[:, 128:], NT)
+        outs[1] += dot(attended, theirs[:, 128:], NT)
+        outs[2] += dot(pre_grad, mine, NT)
+        outs[3] += dot(pre_grad, theirs, NT)
+        target = send if r % 2 else keep
+        for side, (h_side, c_side) in enumerate(((h_own, c_own), (h_other, c_other))):
+            grad = dot(h_side, pre_grad, TN)
+            out_grad = dot(c_side, attended, TN)
+            target[side, r // 2, 0, :, :128] = grad[:, :128].astype(jnp.bfloat16)
+            target[side, r // 2, 0, :, 128:] = (grad[:, 128:] + out_grad).astype(jnp.bfloat16)
+    branch = ff_branch[...] + whole(outs[0], outs[1], first)
+    grad = whole(outs[2], outs[3], first)
+    norm_grads[0:1] = jnp.sum(grad * hat, axis=0, keepdims=True)
+    norm_grads[1:2] = jnp.sum(grad, axis=0, keepdims=True)
+    input_part = ff_part[...] + norm_back(grad, hat, root, norms[0:1])
+    for q in range(4):
+        parts[q, 0] = branch[64 * q : 64 * q + 64].astype(jnp.bfloat16)
+        parts[q, 1] = input_part[64 * q : 64 * q + 64].astype(jnp.bfloat16)
+    for r in range(4):
+        (far if r % 2 else near)[r // 2] = parts[scal[2] ^ r]
+
+
+def finish_rows_kernel(scal, x, cot, bias, r0, r1, r2, r3, block_output, input_grad):
+    for r, piece in enumerate((r0, r1, r2, r3)):
+        q = scal[2] ^ r
+        block_output[q] = x[q].astype(jnp.float32) + piece[0].astype(jnp.float32) + bias[...]
+        input_grad[q] = cot[q].astype(jnp.float32) + piece[1].astype(jnp.float32)
+
+
+def gram_kernel(place, own, a, b, c, momenta, grads, grams):
+    total = own[...].astype(jnp.float32) + a[...].astype(jnp.float32)
+    total = total + b[...].astype(jnp.float32) + c[...].astype(jnp.float32)
+    short = total.astype(jnp.bfloat16)
+    grads[...] = short
+    update = 1.95 * short[0].astype(jnp.float32) + 0.9025 * momenta[0]
+    gram = dot(update, update, TN, lax.Precision.HIGHEST)
+    for j in range(4):
+        cut = slice(j * HD, (j + 1) * HD)
+        grams[0, j] = gram[cut, cut]
+
+
+def gram_of(own, a, b, c, momenta, first_chunk, place):
+    chunks = own.shape[0]
+    piece = pl.BlockSpec((1, 512, 256), lambda i, s: (i, 0, 0))
+    return pl.pallas_call(
+        gram_kernel,
+        grid_spec=pltpu.PrefetchScalarGridSpec(
+            num_scalar_prefetch=1,
+            grid=(chunks,),
+            in_specs=[piece] * 4
+            + [pl.BlockSpec((1, 512, 256), lambda i, s: (4 * (first_chunk + i) + s[1], 0, 0))],
+            out_specs=[piece, pl.BlockSpec((1, 4, HD, HD), lambda i, s: (i, 0, 0, 0))],
+        ),
+        out_shape=[
+            jax.ShapeDtypeStruct((chunks, 512, 256), jnp.bfloat16),
+            jax.ShapeDtypeStruct((chunks, 4, HD, HD), jnp.float32),
+        ],
+        compiler_params=limits(32),
+        name="gram",
+    )(place, own, a, b, c, momenta)
+
+
+def newton_kernel(mine, theirs, out):
+    linear, square, cubic = quintic
+    shape = (HD, HD)
+    eye = lax.broadcasted_iota(jnp.int32, shape, 0) == lax.broadcasted_iota(jnp.int32, shape, 1)
+    high = lax.Precision.HIGHEST
+    chunks = mine.shape[0]
+    places = [(i, j) for i in range(chunks) for j in range(4)]
+    states = []
+    for i, j in places:
+        gram = mine[i, j] + theirs[i, j]
+        trace = jnp.sum(jnp.where(eye, gram, 0.0), axis=(0, 1), keepdims=True)
+        scale = 1.0 / (jnp.sqrt(trace) + muon_epsilon)
+        states.append([gram * scale * scale, None, scale])
+    for iteration in range(NEWTON):
+        squares = [dot(s[0], s[0], precision=high) for s in states]
+        steps = [
+            jnp.where(eye, linear, 0.0) + square * s[0] + cubic * sq
+            for s, sq in zip(states, squares)
+        ]
+        if iteration == 0:
+            halfway = [dot(s[0], m, precision=high) for s, m in zip(states, steps)]
+            for s, m in zip(states, steps):
+                s[1] = m
+        elif iteration < NEWTON - 1:
+            both = [
+                dot(jnp.concatenate([s[0], s[1]], axis=0), m, precision=high)
+                for s, m in zip(states, steps)
+            ]
+            halfway = [x[:HD] for x in both]
+            for s, x in zip(states, both):
+                s[1] = x[HD:]
+        else:
+            for s, m in zip(states, steps):
+                s[1] = dot(s[1], m, precision=high)
+        if iteration < NEWTON - 1:
+            for s, x, m in zip(states, halfway, steps):
+                s[0] = dot(x, m, precision=high)
+    for (i, j), s in zip(places, states):
+        out[i, j] = s[1] * s[2]
+
+
+def newton(mine, theirs):
+    return pl.pallas_call(
+        newton_kernel,
+        in_specs=[mem()] * 2,
+        out_specs=mem(),
+        out_shape=jax.ShapeDtypeStruct(mine.shape, jnp.float32),
+        compiler_params=limits(32),
+        name="newton",
+    )(mine, theirs)
+
+
+def update_kernel(
+    n, chunk_start, scal, g0, g1, g2, g3, q0, q1, q2, q3, momenta, native_momenta, native,
+    grads_in, weights_in, momenta_in, grads, weights, moved, mixing, first, second,
+):
+    if chunk_start == 0:
+        place_of = lambda p, j: (j // 2, 4 * (j % 2) + p)
+    else:
+        place_of = lambda p, j: (p // 2, 4 * (p % 2) + j)
+
+    @pl.when((pl.program_id(0) == 0) & (pl.program_id(1) == 0))
+    def _():
+        mixing[...] = jnp.zeros_like(mixing)
+
+    @pl.when(pl.program_id(1) == 0)
+    def _():
+        for r, q in enumerate((q0, q1, q2, q3)):
+            for j in range(4):
+                mixing[r, j * HD : (j + 1) * HD, j * HD : (j + 1) * HD] = q[0, j]
+
+    low = low_lanes(n)
+    for r, piece in enumerate((g0, g1, g2, g3)):
+        place = scal[1] ^ r
+        grad = piece[0].astype(jnp.float32)
+        update = 1.95 * grad + 0.9025 * momenta[place]
+        settled = dot(update, mixing[r], precision=lax.Precision.HIGHEST)
+        for half in range(2):
+            k = 2 * r + half
+            first[k] = grad[:, half * 128 : (half + 1) * 128]
+            second[k] = settled[:, half * 128 : (half + 1) * 128]
+            pairs = []
+            for s in (first, second):
+                even = s[k, pl.ds(0, n, stride=2), :]
+                odd = s[k, pl.ds(1, n, stride=2), :]
+                pairs.append(
+                    (
+                        jnp.where(low, even, pltpu.roll(odd, 64, 1)),
+                        jnp.where(low, pltpu.roll(even, 64, 1), odd),
+                    )
+                )
+            for w in range(2):
+                group, line = place_of(place, 2 * half + w)
+                rows = pl.ds(line, n, stride=8)
+                value, step = pairs[0][w], pairs[1][w]
+                grads[group, rows, :] = value
+                moved[group, rows, :] = momentum_decay * native_momenta[group, rows, :] + value
+                weight = native[group, rows, :]
+                weights[group, rows, :] = weight - muon_rate * (4.0 * step + weight_decay * weight)
+
+
+def update(chunk_start, chunks, scal, grads, mixes, momenta, native_momenta, native, before, n=32):
+    block = pl.BlockSpec((2, 8 * n, 128), lambda k, i: (chunk_start + k, i, 0))
+    piece = pl.BlockSpec((1, 2 * n, 256), lambda k, i: (k, i, 0))
+    mix = pl.BlockSpec((1, 4, HD, HD), lambda k, i: (k, 0, 0, 0))
+    full = jax.ShapeDtypeStruct((6, 2048, 128), jnp.float32)
+    kernel = functools.partial(update_kernel, n, chunk_start)
+    if before is None:
+        body = kernel
+        kernel = lambda *refs: body(*refs[:12], None, None, None, *refs[12:])
+        before = ()
+    return pl.pallas_call(
+        kernel,
+        grid=(chunks, 256 // n),
+        in_specs=[mem(pltpu.SMEM)]
+        + [piece] * 4
+        + [mix] * 4
+        + [pl.BlockSpec((4, 2 * n, 256), lambda k, i: (chunk_start + k, i, 0)), block, block]
+        + [mem(pl.ANY)] * len(before),
+        out_specs=[block] * 3,
+        out_shape=[full] * 3,
+        scratch_shapes=[
+            pltpu.VMEM((4, 256, 256), jnp.float32),
+            pltpu.VMEM((8, 2 * n, 128), jnp.float32),
+            pltpu.VMEM((8, 2 * n, 128), jnp.float32),
+        ],
+        input_output_aliases={12 + i: i for i in range(len(before))},
+        compiler_params=limits(40),
+        name="update",
+    )(scal, *grads, *mixes, momenta, native_momenta, native, *before)
+
+
+def whole_device(
+    inputs, cotangent, matrices, momenta, small, small_first, small_second, segments, positions
+):
+    blk_at = lax.axis_index("blk")
+    ctx_at = lax.axis_index("ctx")
+    tp_at = lax.axis_index("tp")
+    scal = jnp.stack([blk_at, ctx_at, tp_at]).astype(jnp.int32)
+    sequences, local_rows, width = inputs.shape
+    tokens = sequences * local_rows
+    both = ("blk", "ctx")
+    f32, bf16 = jnp.float32, jnp.bfloat16
+    shaped = jax.ShapeDtypeStruct
+
+    def hop(values, by):
+        return lax.ppermute(values, both, [(i, i ^ by) for i in range(8)])
+
+    def hop_tp(values, by):
+        return lax.ppermute(values, "tp", [(i, i ^ by) for i in range(4)])
+
+    x = inputs.reshape(tokens, width)
+    cot = cotangent.reshape(tokens, width)
+    norms = small[: 4 * width].reshape(4, width)
+    qkv_start = 6 * width + tp_at * 4 * 3 * HD
+    qkv_bias = lax.dynamic_slice_in_dim(small, qkv_start, 4 * 3 * HD).reshape(4, 3 * HD)
+    qkv_bias = jnp.pad(qkv_bias, ((0, 0), (0, HD)))
+    unit_start = 6 * width + H * 3 * HD + tp_at * 1024
+    unit_bias = lax.dynamic_slice_in_dim(small, unit_start, 1024).reshape(4, 256)
+    frequency = rope_base ** (-2.0 * jnp.arange(ROTARY // 2, dtype=f32) / ROTARY)
+    angles = positions.astype(f32).reshape(tokens, 1) * frequency
+    cos, sin = jnp.cos(angles), jnp.sin(angles)
+    rest = jnp.ones((tokens, HD - ROTARY), f32)
+    cosine = jnp.concatenate([cos, cos, rest, cos, cos, rest], axis=1)
+    sine = jnp.concatenate([-sin, sin, 0.0 * rest, -sin, sin, 0.0 * rest], axis=1)
+
+    weights = relayout(matrices, bf16)
+
+    def gathered(piece):
+        a = hop(piece, 4)
+        c = hop(a, 2)
+        return [a, hop(a, 1), c, hop(c, 1)]
+
+    by_chunk = weights.reshape(3, 4, 512, 256)
+    mine = lax.dynamic_index_in_dim(by_chunk, ctx_at, 1, keepdims=False)
+    others_head = gathered(mine[0])
+    others_unit = gathered(mine[1:])
+    piled = relayout(momenta, f32)
+
+    own_chunk = lambda k: pl.BlockSpec((4, 512, 256), lambda *_: (k, 0, 0))
+    send, h1 = pl.pallas_call(
+        project_kernel,
+        grid=(1,),
+        in_specs=[mem(pltpu.SMEM)] + [mem()] * 6 + [own_chunk(0)] + [mem()] * 4,
+        out_specs=[mem()] * 2,
+        out_shape=[shaped((8, local_rows, 256), bf16), shaped((tokens, width), bf16)],
+        compiler_params=limits(40),
+        name="project",
+    )(scal, x, cot, norms, qkv_bias, cosine, sine, weights, *others_head)
+
+    arrived = lax.all_to_all(send, both, split_axis=0, concat_axis=0, tiled=True)
+    documents = lax.dynamic_index_in_dim(segments, blk_at, 0, keepdims=False)
+    length = documents.shape[0]
+    attended = pl.pallas_call(
+        attention_kernel,
+        in_specs=[mem()] * 2,
+        out_specs=mem(),
+        out_shape=shaped((length, 256), bf16),
+        scratch_shapes=[pltpu.VMEM((length, HD), f32)] * 2,
+        compiler_params=limits(48),
+        name="attention",
+    )(arrived.reshape(length, 256), documents.reshape(length, 1))
+    back = lax.all_to_all(
+        attended.reshape(8, local_rows, 256), both, split_axis=0, concat_axis=0, tiled=True
+    )
+
+    ff_branch, ff_part, ff_keep, ff_send, unit_sums, norm_two, cot_sums = pl.pallas_call(
+        feed_forward_kernel,
+        grid=(1,),
+        in_specs=[mem(pltpu.SMEM)] + [mem()] * 4 + [own_chunk(1), own_chunk(2)] + [mem()] * 4,
+        out_specs=[mem()] * 7,
+        out_shape=[
+            shaped((tokens, width), f32),
+            shaped((tokens, width), f32),
+            shaped((2, 2, 2, 512, 256), bf16),
+            shaped((2, 2, 2, 512, 256), bf16),
+            shaped((4, 256), f32),
+            shaped((2, width), f32),
+            shaped((1, width), f32),
+        ],
+        compiler_params=limits(48),
+        name="feed_forward",
+    )(scal, x, cot, norms, unit_bias, weights, weights, *others_unit)
+
+    def reduced(keep, send):
+        came = hop(send, 1)
+        summed = (keep.astype(f32) + came.astype(f32)).astype(bf16)
+        return summed[0, 0], hop(summed[1, 0], 4), hop(summed[0, 1], 2), hop(summed[1, 1], 6)
+
+    def spread(piece):
+        c = hop(piece, 2)
+        return [piece, hop(piece, 1), c, hop(c, 1)]
+
+    def muon(keep, send, first_chunk, before):
+        grads, grams = gram_of(*reduced(keep, send), piled, first_chunk, scal)
+        pieces = spread(grads)
+        mixes = spread(newton(grams, hop(grams, 4)))
+        return update(
+            first_chunk, grads.shape[0], scal, pieces, mixes, piled, native_view(momenta),
+            native_view(matrices), before,
+        )
+
+    before = muon(ff_keep, ff_send, 1, None)
+
+    near, far, keep, send_back, qkv_sums, norm_one = pl.pallas_call(
+        gather_kernel,
+        grid=(1,),
+        in_specs=[mem(pltpu.SMEM)] + [mem()] * 7 + [own_chunk(0)] + [mem()] * 6,
+        out_specs=[mem()] * 6,
+        out_shape=[
+            shaped((2, 2, 64, width), bf16),
+            shaped((2, 2, 64, width), bf16),
+            shaped((2, 2, 1, 512, 256), bf16),
+            shaped((2, 2, 1, 512, 256), bf16),
+            shaped((4, 256), f32),
+            shaped((2, width), f32),
+        ],
+        scratch_shapes=[pltpu.VMEM((4, 2, 64, width), bf16)],
+        compiler_params=limits(48),
+        name="gather",
+    )(scal, x, cot, norms, cosine, sine, back, h1, weights, *others_head, ff_branch, ff_part)
+
+    outs = muon(keep, send_back, 0, before)
+
+    summed = (near.astype(f32) + hop_tp(far, 1).astype(f32)).astype(bf16)
+    total = (summed[0].astype(f32) + hop_tp(summed[1], 2).astype(f32)).astype(bf16)
+    beside = hop_tp(total, 2)
+    block_output, input_grad = pl.pallas_call(
+        finish_rows_kernel,
+        in_specs=[mem(pltpu.SMEM)] + [mem()] * 7,
+        out_specs=[mem()] * 2,
+        out_shape=[shaped((4, 64, width), f32)] * 2,
+        compiler_params=limits(32),
+        name="finish_rows",
+    )(
+        scal,
+        x.reshape(4, 64, width),
+        cot.reshape(4, 64, width),
+        (small[4 * width : 5 * width] + small[5 * width : 6 * width]).reshape(1, width),
+        total,
+        hop_tp(total, 1),
+        beside,
+        hop_tp(beside, 1),
+    )
+
+    share = jnp.where(tp_at == 0, 1.0, 0.0).astype(f32)
+    cot_total = cot_sums[0] * share
+    local = jnp.concatenate(
+        [
+            norm_one.reshape(-1),
+            norm_two.reshape(-1),
+            cot_total,
+            cot_total,
+            jnp.zeros((small.shape[0] - 6 * width,), f32),
+        ]
+    )
+    local = lax.dynamic_update_slice_in_dim(
+        local, qkv_sums[:, : 3 * HD].reshape(-1), qkv_start, 0
+    )
+    small_grads = lax.dynamic_update_slice_in_dim(local, unit_sums.reshape(-1), unit_start, 0)
+    for by in (1, 2, 4):
+        small_grads = small_grads + hop(small_grads, by)
+    for by in (1, 2):
+        small_grads = small_grads + hop_tp(small_grads, by)
+    new_matrices_at = native_back(outs[1])
+    return (
+        block_output.reshape(inputs.shape),
+        input_grad.reshape(inputs.shape),
+        native_back(outs[0]),
+        new_matrices_at,
+        native_back(outs[2]),
+        small_grads,
+        *small_step(small, small_first, small_second, small_grads),
+    )
+
+
+def small_step(small, small_first, small_second, small_grads):
+    new_first = adam_first * small_first + (1.0 - adam_first) * small_grads
+    new_second = adam_second * small_second + (1.0 - adam_second) * small_grads * small_grads
+    corrected = new_first / (1.0 - adam_first**STEP)
+    spread = jnp.sqrt(new_second / (1.0 - adam_second**STEP))
+    new_small = small - small_rate * corrected / (spread + adam_epsilon)
+    return new_first, new_second, new_small
+
+
 def solution(mesh):
     in_specs = (
         P(None, ("blk", "ctx"), None),
@@ -414,6 +1017,8 @@
         P(),
         P(),
     )
+    one_each = mesh.shape["blk"] == SEQS and mesh.shape["ctx"] * mesh.shape["tp"] == H
+    one_each = one_each and mesh.shape["tp"] == 4
     return jax.shard_map(
-        on_device, mesh=mesh, in_specs=in_specs, out_specs=out_specs, check_vma=False
-    )
+        whole_device if one_each else on_device, mesh=mesh, in_specs=in_specs, out_specs=out_specs, check_vma=False
+    )

time: 1240 us -> 229 us (0.18)
  other arithmetic: 406 us -> 5.49 us
  local copies, waits for them, and re-layouts: 331 us -> 15.6 us
  waiting for transfers between devices: 256 us -> 85.4 us
  matrix products: 121 us -> 0 us
  Pallas kernels: 0 us -> 74.9 us
  blocking collectives: 66.8 us -> 0 us
  starting transfers between devices: 31.3 us -> 45.6 us
  between operations: 15.2 us -> 1.09 us
    unnamed x5 -> x2, other arithmetic: 356 us -> 0.01 us
    dot_general x39 -> x0, matrix products: 121 us -> none  [the longest x5 36.4 us: newton_schulz(): jnp.einsum('mde,mdf->mef', current, current, precision=lax.Precision.HIGH...]
    convert_element_type x11 -> x0, local copies, waits for them, and re-layouts: 109 us -> none  [the longest x3 60.2 us: short(): return part.astype(jnp.bfloat16) if part.dtype == jnp.float32 else part]
    unnamed x115 -> x51, local copies, waits for them, and re-layouts: 96.8 us -> 10.3 us
    all_gather x1 -> x0, waiting for transfers between devices: 78.4 us -> none  [on_device(): lax.all_gather(matrices.astype(jnp.bfloat16), 'blk', axis=1, tiled=True)]
    reduce_scatter x1 -> x0, waiting for transfers between devices: 75.8 us -> none  [on_device(): lax.psum_scatter(local_grad.astype(jnp.bfloat16), 'blk', scatter_dimensio...]
    pallas_call x0 -> x13, Pallas kernels: none -> 74.9 us  [the longest x2 31.6 us: update(): pl.pallas_call(kernel, grid=(chunks, 256 // n), in_specs=[mem(pltpu.SMEM)...]
    ppermute x3 -> x40, waiting for transfers between devices: 6.23 us -> 76.5 us  [the longest x33 59.6 us: hop(): return lax.ppermute(values, both, [(i, i ^ by) for i in range(8)])]
  transfers between devices with their start and end apart: 13 -> 42, of which waited for: 8 -> 15; matrix products, arithmetic and copies ran while one was open for 52% -> 5% of each run, Pallas kernels for 0% -> 27%
where the time goes in v1:
time: 229 us; the launch traced here: 228 us
  waiting for transfers between devices  85.4 us (37%)
  Pallas kernels  74.9 us (33%)
  starting transfers between devices  45.6 us (20%)
  local copies, waits for them, and re-layouts  15.6 us (7%)
  other arithmetic  5.49 us (2%)
    ppermute x33, waiting for transfers between devices, hop(): return lax.ppermute(values, both, [(i, i ^ by) for i in range(8)])  59.6 us
    pallas_call x2, Pallas kernels, update(): pl.pallas_call(kernel, grid=(chunks, 256 // n), in_specs=[mem(pltpu.SMEM)...  31.6 us
    ppermute x33, starting transfers between devices, hop(): return lax.ppermute(values, both, [(i, i ^ by) for i in range(8)])  26.8 us
    ppermute x7, waiting for transfers between devices, hop_tp(): return lax.ppermute(values, 'tp', [(i, i ^ by) for i in range(4)])  16.9 us
    ppermute x7, starting transfers between devices, hop_tp(): return lax.ppermute(values, 'tp', [(i, i ^ by) for i in range(4)])  11 us
    unnamed x51, local copies, waits for them, and re-layouts  10.3 us
    all_to_all x1, waiting for transfers between devices, whole_device(): lax.all_to_all(send, both, split_axis=0, concat_axis=0, tiled=True)  8.92 us
    pallas_call x1, Pallas kernels, whole_device(): pl.pallas_call(feed_forward_kernel, grid=(1,), in_specs=[mem(pltpu.SMEM)]...  8.15 us
  transfers between devices with their start and end apart: 42, of which 15 were waited for; matrix products, arithmetic and copies ran while one was open for 5% of the time, Pallas kernels for 27%

profile of v1, /device:TPU:0, one launch (start us, length us, event | category | flops | bytes accessed | tf_op | source)
XLA Modules:
  0.0 228.1 jit_solution(11113225130994125767)
XLA Ops:
  0.7 2.8 %copy-done.3 = f32[48,32768]{1,0:T(8,128)S(1)} copy-done((f32[48,32768]{1,0:T(8,128)S(1)}, f32[48,32768]{1,0:T(8,128)}, u32[]{:S(2)}) %copy-start.3) | copy-done | bytes 6291480
  3.5 3.4 %relayout.2.own.own_in.own_down = bf16[12,512,256]{2,1,0:T(8,128)(2,1)S(1)} custom-call(f32[6,2048,128]{2,1,0:T(8,128)S(1)} %bitcast.83), custom_call_target="tpu_custom_call" | custom-call | tf_op jit(solution)/shard_map/relayout/pallas_call | solution.py:454
  6.9 3.0 %collective-permute-start.4 = (bf16[2,512,256]{2,1,0:T(8,128)(2,1)S(1)}, bf16[2,512,256]{2,1,0:T(8,128)(2,1)}, u32[]{:S(2)}, u32[]{:S(2)}) collective-permute-start(bf16[2,512,256]{2,1,0:T(8,128)(2,1)S(1)} %dynamic-slice_bitcast_fusion), channel_id=1, source_target_pairs={{0,16},{4,20},{8,24},{12,28},{16,0},{20,4},{24,8},{28,12},{1,17},{... | collective-permute-start | bytes 1572872 | tf_op jit(solution)/shard_map/ppermute | solution.py:818
  10.0 17.5 %collective-permute-done.r0 = bf16[512,256]{1,0:T(8,128)(2,1)} collective-permute-done((bf16[512,256]{1,0:T(8,128)(2,1)S(1)}, bf16[512,256]{1,0:T(8,128)(2,1)}, u32[]{:S(2)}, u32[]{:S(2)}) %collective-permute-start) | collective-permute-done | bytes 262176 | tf_op jit(solution)/shard_map/ppermute | solution.py:818
  30.0 7.2 %collective-permute-done.2.r2 = bf16[512,256]{1,0:T(8,128)(2,1)} collective-permute-done((bf16[512,256]{1,0:T(8,128)(2,1)}, bf16[512,256]{1,0:T(8,128)(2,1)}, u32[]{:S(2)}, u32[]{:S(2)}) %collective-permute-start.2) | collective-permute-done | bytes 262176 | tf_op jit(solution)/shard_map/ppermute | solution.py:818
  44.6 2.8 %project.1 = (bf16[8,128,256]{2,1,0:T(8,128)(2,1)S(1)}, bf16[256,1024]{1,0:T(8,128)(2,1)S(1)}) custom-call(s32[3]{0:T(128)S(1)} %pad_add_fusion.scal.place.refs_0_, bf16[256,1024]{1,0:T(8,128)(2,1)S(1)} %bitcast.91, bf16[256,1024]{1,0:T(8,128)(2,1)S(1)} %bitcast.95, f32[4,1024]{1,0:T(4,128)S(1)} %slice.65.norms, f32[4,256]{1,0:T(4,128)S(1)} %pad.4.bias, ...), custom_call_target="tpu_custom_call" | custom-call | tf_op jit(solution)/shard_map/project/pallas_call | solution.py:852
  49.0 4.2 %all-to-all-start = ((bf16[8,128,256]{2,1,0:T(8,128)(2,1)}), bf16[8,128,256]{2,1,0:T(8,128)(2,1)S(1)}, u32[]{:S(2)}, u32[]{:S(2)}) async-start(bf16[8,128,256]{2,1,0:T(8,128)(2,1)} %copy-done.14), calls=%async_computation | async-start | bytes 1048576 | tf_op jit(solution)/shard_map/all_to_all | solution.py:862
  54.0 8.9 %all-to-all-done = bf16[8,128,256]{2,1,0:T(8,128)(2,1)S(1)} async-done(((bf16[8,128,256]{2,1,0:T(8,128)(2,1)}), bf16[8,128,256]{2,1,0:T(8,128)(2,1)S(1)}, u32[]{:S(2)}, u32[]{:S(2)}) %all-to-all-start) | async-done | bytes 524320 | tf_op jit(solution)/shard_map/all_to_all | solution.py:862
  63.0 5.9 %attention.1 = bf16[1024,256]{1,0:T(8,128)(2,1)} custom-call(bf16[1024,256]{1,0:T(8,128)(2,1)S(1)} %bitcast.99, s32[1024,1]{1,0:T(8,128)S(1)} %copy.23.seg), custom_call_target="tpu_custom_call" | custom-call | tf_op jit(solution)/shard_map/attention/pallas_call | solution.py:865
  68.9 3.7 %all-to-all-start.1 = ((bf16[8,128,256]{2,1,0:T(8,128)(2,1)}), bf16[8,128,256]{2,1,0:T(8,128)(2,1)S(1)}, u32[]{:S(2)}, u32[]{:S(2)}) async-start(bf16[8,128,256]{2,1,0:T(8,128)(2,1)} %bitcast.16), calls=%async_computation.1 | async-start | bytes 1048576 | tf_op jit(solution)/shard_map/all_to_all | solution.py:874
  74.5 8.1 %feed_forward.1 = (f32[256,1024]{1,0:T(8,128)S(1)}, f32[256,1024]{1,0:T(8,128)S(1)}, bf16[2,2,2,512,256]{4,3,2,1,0:T(8,128)(2,1)}, bf16[2,2,2,512,256]{4,3,2,1,0...) custom-call(s32[3]{0:T(128)S(1)} %pad_add_fusion.scal.place.refs_0_, ...), custom_call_target="tpu_custom_call" | custom-call | tf_op jit(solution)/shard_map/feed_forward/pallas_call | solution.py:878
  84.8 6.3 %gather.1 = (bf16[2,2,64,1024]{3,2,1,0:T(8,128)(2,1)S(1)}, bf16[2,2,64,1024]{3,2,1,0:T(8,128)(2,1)S(1)}, bf16[2,2,1,512,256]{4,3,2,1,0:T(8,128)(2,1)S(1)}, bf16[...) custom-call(s32[3]{0:T(128)S(1)} %pad_add_fusion.scal.place.refs_0_, ...), custom_call_target="tpu_custom_call" | custom-call | tf_op jit(solution)/shard_map/gather/pallas_call | solution.py:916
  92.7 12.5 %collective-permute-done.8 = bf16[2,2,64,1024]{3,2,1,0:T(8,128)(2,1)S(1)} collective-permute-done((bf16[2,2,64,1024]{3,2,1,0:T(8,128)(2,1)S(1)}, bf16[2,2,64,1024]{3,2,1,0:T(8,128)(2,1)S(1)}, u32[]{:S(2)}, u32[]{:S(2)}) %collective-permute-start.8) | collective-permute-done | bytes 524320 | tf_op jit(solution)/shard_map/ppermute | solution.py:821
  105.5 2.7 %collective-permute-start.9 = (bf16[2,64,1024]{2,1,0:T(8,128)(2,1)S(1)}, bf16[2,64,1024]{2,1,0:T(8,128)(2,1)S(1)}, u32[]{:S(2)}, u32[]{:S(2)}) collective-permute-start(bf16[2,64,1024]{2,1,0:T(8,128)(2,1)S(1)} %slice_bitcast_fusion.8), channel_id=1, source_target_pairs={{0,2},{1,3},{2,0},{3,1},{4,6},{5,7},{6,4},{7,5},{8,10},{9,11},{10,... | collective-permute-start | bytes 786440 | tf_op jit(solution)/shard_map/ppermute | solution.py:821
  125.8 2.9 %add_convert_fusion = bf16[2,2,2,512,256]{4,3,2,1,0:T(8,128)(2,1)S(1)} fusion(bf16[2,2,2,512,256]{4,3,2,1,0:T(8,128)(2,1)} %collective-permute-done.24, bf16[2,2,2,512,256]{4,3,2,1,0:T(8,128)(2,1)} %get-tuple-element.48), kind=kLoop, calls=%fused_computation | loop fusion | flops 4194304 | bytes 6291456 | tf_op jit(solution)/shard_map/convert_element_type | solution.py:898
  136.3 14.8 %collective-permute-done.25.a = bf16[2,512,256]{2,1,0:T(8,128)(2,1)S(1)} collective-permute-done((bf16[2,512,256]{2,1,0:T(8,128)(2,1)S(1)}, bf16[2,512,256]{2,1,0:T(8,128)(2,1)S(1)}, u32[]{:S(2)}, u32[]{:S(2)}) %collective-permute-start.25) | collective-permute-done | bytes 524320 | tf_op jit(solution)/shard_map/ppermute | solution.py:818
  158.1 3.5 %relayout.3.momenta.refs_9_ = f32[12,512,256]{2,1,0:T(8,128)S(1)} custom-call(f32[6,2048,128]{2,1,0:T(8,128)S(1)} %bitcast.87), custom_call_target="tpu_custom_call" | custom-call | tf_op jit(solution)/shard_map/relayout/pallas_call | solution.py:454
  161.6 2.7 %gram.3 = (bf16[2,512,256]{2,1,0:T(8,128)(2,1)S(1)}, f32[2,4,64,64]{3,2,1,0:T(8,128)S(1)}) custom-call(s32[3]{0:T(128)S(1)} %pad_add_fusion.scal.place.refs_0_, bf16[2,512,256]{2,1,0:T(8,128)(2,1)S(1)} %get-tuple-element.70.own, bf16[2,512,256]{2,1,0:T(8,128)(2,1)S(1)} %collective-permute-done.25.a, bf16[2,512,256]{2,1,0:T(8,128)(2,1)S(1)} %collective-permute-done.26.b, ...), custom_call_target="tpu_custom_call" | custom-call | tf_op jit(solution)/shard_map/gram/pallas_call | solution.py:654
  170.8 5.6 %collective-permute-done.31.theirs = f32[2,4,64,64]{3,2,1,0:T(8,128)S(1)} collective-permute-done((f32[2,4,64,64]{3,2,1,0:T(8,128)S(1)}, f32[2,4,64,64]{3,2,1,0:T(8,128)S(1)}, u32[]{:S(2)}, u32[]{:S(2)}) %collective-permute-start.31) | collective-permute-done | bytes 131104 | tf_op jit(solution)/shard_map/ppermute | solution.py:818
  176.7 3.9 %newton.3.refs_5_ = f32[2,4,64,64]{3,2,1,0:T(8,128)S(1)} custom-call(f32[2,4,64,64]{3,2,1,0:T(8,128)S(1)} %get-tuple-element.51.mine, f32[2,4,64,64]{3,2,1,0:T(8,128)S(1)} %collective-permute-done.31.theirs), custom_call_target="tpu_custom_call" | custom-call | tf_op jit(solution)/shard_map/newton/pallas_call | solution.py:714
  182.4 3.0 %newton.2.q0 = f32[1,4,64,64]{3,2,1,0:T(8,128)S(1)} custom-call(f32[1,4,64,64]{3,2,1,0:T(8,128)S(1)} %get-tuple-element.47.mine, f32[1,4,64,64]{3,2,1,0:T(8,128)S(1)} %collective-permute-done.20.theirs), custom_call_target="tpu_custom_call" | custom-call | tf_op jit(solution)/shard_map/newton/pallas_call | solution.py:714
  185.8 5.4 %collective-permute-done.22.q2 = f32[1,4,64,64]{3,2,1,0:T(8,128)S(1)} collective-permute-done((f32[1,4,64,64]{3,2,1,0:T(8,128)S(1)}, f32[1,4,64,64]{3,2,1,0:T(8,128)S(1)}, u32[]{:S(2)}, u32[]{:S(2)}) %collective-permute-start.22) | collective-permute-done | bytes 65568 | tf_op jit(solution)/shard_map/ppermute | solution.py:818
  196.4 20.7 %update.2 = (f32[6,2048,128]{2,1,0:T(8,128)}, f32[6,2048,128]{2,1,0:T(8,128)}, f32[6,2048,128]{2,1,0:T(8,128)}) custom-call(s32[3]{0:T(128)S(1)} %pad_add_fusion.scal.place.refs_0_, bf16[2,512,256]{2,1,0:T(8,128)(2,1)S(1)} %get-tuple-element.50.refs_1_, bf16[2,512,256]{2,1,0:T(8,128)(2,1)S(1)} %collective-permute-done.28.refs_2_, ...), custom_call_target="tpu_custom_call" | custom-call | tf_op jit(solution)/shard_map/update/pallas_call | solution.py:783
  217.2 10.9 %update.3 = (f32[6,2048,128]{2,1,0:T(8,128)}, f32[6,2048,128]{2,1,0:T(8,128)}, f32[6,2048,128]{2,1,0:T(8,128)}) custom-call(s32[3]{0:T(128)S(1)} %pad_add_fusion.scal.place.refs_0_, bf16[1,512,256]{2,1,0:T(8,128)(2,1)S(1)} %get-tuple-element.46.g0, ...), custom_call_target="tpu_custom_call", output_to_operand_aliasing={{0}: (12, {}), {1}: (13, {}), {2}: (14, {})} | custom-call | tf_op jit(solution)/shard_map/update/pallas_call | solution.py:783
  (163 shorter events, 64.6 us)
Async XLA Ops:
  6.9 22.4 %collective-permute-start.4 = (bf16[2,512,256]{2,1,0:T(8,128)(2,1)S(1)}, bf16[2,512,256]{2,1,0:T(8,128)(2,1)}, u32[]{:S(2)}, u32[]{:S(2)}) collective-permute-start(bf16[2,512,256]{2,1,0:T(8,128)(2,1)S(1)} %dynamic-slice_bitcast_fusion), channel_id=1, source_target_pairs={{0,16},{4,20},{8,24},{12,28},{16,0},{20,4},{24,8},{28,12},{1,17},{... | collective-permute-start | bytes 1572872 | tf_op jit(solution)/shard_map/ppermute | solution.py:818
  10.0 17.6 %collective-permute-start = (bf16[512,256]{1,0:T(8,128)(2,1)S(1)}, bf16[512,256]{1,0:T(8,128)(2,1)}, u32[]{:S(2)}, u32[]{:S(2)}) collective-permute-start(bf16[512,256]{1,0:T(8,128)(2,1)S(1)} %dynamic-slice_bitcast_fusion.1), channel_id=1, source_target_pairs={{0,16},{4,20},{8,24},{12,28},{16,0},{20,4},{24,8},{28,12},{1,17},{... | collective-permute-start | bytes 786440 | tf_op jit(solution)/shard_map/ppermute | solution.py:818
  29.3 24.4 %collective-permute-start.6 = (bf16[2,512,256]{2,1,0:T(8,128)(2,1)}, bf16[2,512,256]{2,1,0:T(8,128)(2,1)}, u32[]{:S(2)}, u32[]{:S(2)}) collective-permute-start(bf16[2,512,256]{2,1,0:T(8,128)(2,1)} %collective-permute-done.4.r0), channel_id=1, source_target_pairs={{0,8},{4,12},{8,0},{12,4},{16,24},{20,28},{24,16},{28,20},{1,9},{5... | collective-permute-start | bytes 1572872 | tf_op jit(solution)/shard_map/ppermute | solution.py:818
  53.2 19.4 %collective-permute-start.5 = (bf16[2,512,256]{2,1,0:T(8,128)(2,1)}, bf16[2,512,256]{2,1,0:T(8,128)(2,1)S(1)}, u32[]{:S(2)}, u32[]{:S(2)}) collective-permute-start(bf16[2,512,256]{2,1,0:T(8,128)(2,1)} %collective-permute-done.4.r0), channel_id=1, source_target_pairs={{0,4},{4,0},{8,12},{12,8},{16,20},{20,16},{24,28},{28,24},{1,5},{5... | collective-permute-start | bytes 1572872 | tf_op jit(solution)/shard_map/ppermute | solution.py:818
  53.7 19.7 %collective-permute-start.7 = (bf16[2,512,256]{2,1,0:T(8,128)(2,1)}, bf16[2,512,256]{2,1,0:T(8,128)(2,1)}, u32[]{:S(2)}, u32[]{:S(2)}) collective-permute-start(bf16[2,512,256]{2,1,0:T(8,128)(2,1)} %collective-permute-done.6.r2), channel_id=1, source_target_pairs={{0,4},{4,0},{8,12},{12,8},{16,20},{20,16},{24,28},{28,24},{1,5},{5... | collective-permute-start | bytes 1572872 | tf_op jit(solution)/shard_map/ppermute | solution.py:818
  68.9 15.9 %all-to-all-start.1 = ((bf16[8,128,256]{2,1,0:T(8,128)(2,1)}), bf16[8,128,256]{2,1,0:T(8,128)(2,1)S(1)}, u32[]{:S(2)}, u32[]{:S(2)}) async-start(bf16[8,128,256]{2,1,0:T(8,128)(2,1)} %bitcast.16), calls=%async_computation.1 | async-start | bytes 1048576 | tf_op jit(solution)/shard_map/all_to_all | solution.py:874
  84.6 41.2 %collective-permute-start.24 = (bf16[2,2,2,512,256]{4,3,2,1,0:T(8,128)(2,1)}, bf16[2,2,2,512,256]{4,3,2,1,0:T(8,128)(2,1)}, u32[]{:S(2)}, u32[]{:S(2)}) collective-permute-start(bf16[2,2,2,512,256]{4,3,2,1,0:T(8,128)(2,1)} %get-tuple-element.49), channel_id=1, source_target_pairs={{0,4},{4,0},{8,12},{12,8},{16,20},{20,16},{24,28},{28,24},{1,5},{5... | collective-permute-start | bytes 6291464 | tf_op jit(solution)/shard_map/ppermute | solution.py:818
  105.5 17.6 %collective-permute-start.9 = (bf16[2,64,1024]{2,1,0:T(8,128)(2,1)S(1)}, bf16[2,64,1024]{2,1,0:T(8,128)(2,1)S(1)}, u32[]{:S(2)}, u32[]{:S(2)}) collective-permute-start(bf16[2,64,1024]{2,1,0:T(8,128)(2,1)S(1)} %slice_bitcast_fusion.8), channel_id=1, source_target_pairs={{0,2},{1,3},{2,0},{3,1},{4,6},{5,7},{6,4},{7,5},{8,10},{9,11},{10,... | collective-permute-start | bytes 786440 | tf_op jit(solution)/shard_map/ppermute | solution.py:821
  111.8 20.3 %collective-permute-start.13 = (bf16[2,2,1,512,256]{4,3,2,1,0:T(8,128)(2,1)}, bf16[2,2,1,512,256]{4,3,2,1,0:T(8,128)(2,1)S(1)}, u32[]{:S(2)}, u32[]{:S(2)}) collective-permute-start(bf16[2,2,1,512,256]{4,3,2,1,0:T(8,128)(2,1)} %get-tuple-element.45), channel_id=1, source_target_pairs={{0,4},{4,0},{8,12},{12,8},{16,20},{20,16},{24,28},{28,24},{1,5},{5... | collective-permute-start | bytes 3145736 | tf_op jit(solution)/shard_map/ppermute | solution.py:818
  123.1 41.2 %collective-permute-start.11 = (bf16[2,64,1024]{2,1,0:T(8,128)(2,1)S(1)}, bf16[2,64,1024]{2,1,0:T(8,128)(2,1)S(1)}, u32[]{:S(2)}, u32[]{:S(2)}) collective-permute-start(bf16[2,64,1024]{2,1,0:T(8,128)(2,1)S(1)} %fusion.r0), channel_id=1, source_target_pairs={{0,2},{1,3},{2,0},{3,1},{4,6},{5,7},{6,4},{7,5},{8,10},{9,11},{10,... | collective-permute-start | bytes 786440 | tf_op jit(solution)/shard_map/ppermute | solution.py:821
  128.8 22.2 %collective-permute-start.25 = (bf16[2,512,256]{2,1,0:T(8,128)(2,1)S(1)}, bf16[2,512,256]{2,1,0:T(8,128)(2,1)S(1)}, u32[]{:S(2)}, u32[]{:S(2)}) collective-permute-start(bf16[2,512,256]{2,1,0:T(8,128)(2,1)S(1)} %get-tuple-element.69), channel_id=1, source_target_pairs={{0,16},{4,20},{8,24},{12,28},{16,0},{20,4},{24,8},{28,12},{1,17},{... | collective-permute-start | bytes 1572872 | tf_op jit(solution)/shard_map/ppermute | solution.py:818
  130.6 22.1 %collective-permute-start.26 = (bf16[2,512,256]{2,1,0:T(8,128)(2,1)S(1)}, bf16[2,512,256]{2,1,0:T(8,128)(2,1)S(1)}, u32[]{:S(2)}, u32[]{:S(2)}) collective-permute-start(bf16[2,512,256]{2,1,0:T(8,128)(2,1)S(1)} %get-tuple-element.68), channel_id=1, source_target_pairs={{0,8},{4,12},{8,0},{12,4},{16,24},{20,28},{24,16},{28,20},{1,9},{5... | collective-permute-start | bytes 1572872 | tf_op jit(solution)/shard_map/ppermute | solution.py:818
  132.1 24.4 %collective-permute-start.27 = (bf16[2,512,256]{2,1,0:T(8,128)(2,1)S(1)}, bf16[2,512,256]{2,1,0:T(8,128)(2,1)S(1)}, u32[]{:S(2)}, u32[]{:S(2)}) collective-permute-start(bf16[2,512,256]{2,1,0:T(8,128)(2,1)S(1)} %get-tuple-element.67), channel_id=1, source_target_pairs={{0,24},{4,28},{8,16},{12,20},{16,8},{20,12},{24,0},{28,4},{1,25},{... | collective-permute-start | bytes 1572872 | tf_op jit(solution)/shard_map/ppermute | solution.py:818
  134.6 31.6 %collective-permute-start.14 = (bf16[1,512,256]{2,1,0:T(8,128)(2,1)S(1)}, bf16[1,512,256]{2,1,0:T(8,128)(2,1)S(1)}, u32[]{:S(2)}, u32[]{:S(2)}) collective-permute-start(bf16[1,512,256]{2,1,0:T(8,128)(2,1)S(1)} %get-tuple-element.73), channel_id=1, source_target_pairs={{0,16},{4,20},{8,24},{12,28},{16,0},{20,4},{24,8},{28,12},{1,17},{... | collective-permute-start | bytes 786440 | tf_op jit(solution)/shard_map/ppermute | solution.py:818
  151.1 15.1 %collective-permute-start.15 = (bf16[1,512,256]{2,1,0:T(8,128)(2,1)S(1)}, bf16[1,512,256]{2,1,0:T(8,128)(2,1)S(1)}, u32[]{:S(2)}, u32[]{:S(2)}) collective-permute-start(bf16[1,512,256]{2,1,0:T(8,128)(2,1)S(1)} %get-tuple-element.72), channel_id=1, source_target_pairs={{0,8},{4,12},{8,0},{12,4},{16,24},{20,28},{24,16},{28,20},{1,9},{5... | collective-permute-start | bytes 786440 | tf_op jit(solution)/shard_map/ppermute | solution.py:818
  156.5 14.2 %collective-permute-start.10 = (bf16[2,64,1024]{2,1,0:T(8,128)(2,1)S(1)}, bf16[2,64,1024]{2,1,0:T(8,128)(2,1)S(1)}, u32[]{:S(2)}, u32[]{:S(2)}) collective-permute-start(bf16[2,64,1024]{2,1,0:T(8,128)(2,1)S(1)} %fusion.r0), channel_id=1, source_target_pairs={{0,1},{1,0},{2,3},{3,2},{4,5},{5,4},{6,7},{7,6},{8,9},{9,8},{10,11... | collective-permute-start | bytes 786440 | tf_op jit(solution)/shard_map/ppermute | solution.py:821
  164.3 27.4 %collective-permute-start.29 = (bf16[2,512,256]{2,1,0:T(8,128)(2,1)S(1)}, bf16[2,512,256]{2,1,0:T(8,128)(2,1)S(1)}, u32[]{:S(2)}, u32[]{:S(2)}) collective-permute-start(bf16[2,512,256]{2,1,0:T(8,128)(2,1)S(1)} %get-tuple-element.50.refs_1_), channel_id=1, source_target_pairs={{0,8},{4,12},{8,0},{12,4},{16,24},{20,28},{24,16},{28,20},{1,9},{5... | collective-permute-start | bytes 1572872 | tf_op jit(solution)/shard_map/ppermute | solution.py:818
  166.1 27.2 %collective-permute-start.28 = (bf16[2,512,256]{2,1,0:T(8,128)(2,1)S(1)}, bf16[2,512,256]{2,1,0:T(8,128)(2,1)S(1)}, u32[]{:S(2)}, u32[]{:S(2)}) collective-permute-start(bf16[2,512,256]{2,1,0:T(8,128)(2,1)S(1)} %get-tuple-element.50.refs_1_), channel_id=1, source_target_pairs={{0,4},{4,0},{8,12},{12,8},{16,20},{20,16},{24,28},{28,24},{1,5},{5... | collective-permute-start | bytes 1572872 | tf_op jit(solution)/shard_map/ppermute | solution.py:818
  166.1 19.3 %collective-permute-start.12 = (bf16[2,64,1024]{2,1,0:T(8,128)(2,1)S(1)}, bf16[2,64,1024]{2,1,0:T(8,128)(2,1)S(1)}, u32[]{:S(2)}, u32[]{:S(2)}) collective-permute-start(bf16[2,64,1024]{2,1,0:T(8,128)(2,1)S(1)} %collective-permute-done.11.r2), channel_id=1, source_target_pairs={{0,1},{1,0},{2,3},{3,2},{4,5},{5,4},{6,7},{7,6},{8,9},{9,8},{10,11... | collective-permute-start | bytes 786440 | tf_op jit(solution)/shard_map/ppermute | solution.py:821
  176.4 15.4 %collective-permute-start.18 = (bf16[1,512,256]{2,1,0:T(8,128)(2,1)S(1)}, bf16[1,512,256]{2,1,0:T(8,128)(2,1)S(1)}, u32[]{:S(2)}, u32[]{:S(2)}) collective-permute-start(bf16[1,512,256]{2,1,0:T(8,128)(2,1)S(1)} %get-tuple-element.46.g0), channel_id=1, source_target_pairs={{0,8},{4,12},{8,0},{12,4},{16,24},{20,28},{24,16},{28,20},{1,9},{5... | collective-permute-start | bytes 786440 | tf_op jit(solution)/shard_map/ppermute | solution.py:818
  191.8 25.4 %collective-permute-start.17 = (bf16[1,512,256]{2,1,0:T(8,128)(2,1)S(1)}, bf16[1,512,256]{2,1,0:T(8,128)(2,1)S(1)}, u32[]{:S(2)}, u32[]{:S(2)}) collective-permute-start(bf16[1,512,256]{2,1,0:T(8,128)(2,1)S(1)} %get-tuple-element.46.g0), channel_id=1, source_target_pairs={{0,4},{4,0},{8,12},{12,8},{16,20},{20,16},{24,28},{28,24},{1,5},{5... | collective-permute-start | bytes 786440 | tf_op jit(solution)/shard_map/ppermute | solution.py:818
  192.8 24.4 %collective-permute-start.21 = (f32[1,4,64,64]{3,2,1,0:T(8,128)S(1)}, f32[1,4,64,64]{3,2,1,0:T(8,128)S(1)}, u32[]{:S(2)}, u32[]{:S(2)}) collective-permute-start(f32[1,4,64,64]{3,2,1,0:T(8,128)S(1)} %newton.2.q0), channel_id=1, source_target_pairs={{0,4},{4,0},{8,12},{12,8},{16,20},{20,16},{24,28},{28,24},{1,5},{5... | collective-permute-start | bytes 196616 | tf_op jit(solution)/shard_map/ppermute | solution.py:818
  193.1 24.0 %collective-permute-start.23 = (f32[1,4,64,64]{3,2,1,0:T(8,128)S(1)}, f32[1,4,64,64]{3,2,1,0:T(8,128)S(1)}, u32[]{:S(2)}, u32[]{:S(2)}) collective-permute-start(f32[1,4,64,64]{3,2,1,0:T(8,128)S(1)} %collective-permute-done.22.q2), channel_id=1, source_target_pairs={{0,4},{4,0},{8,12},{12,8},{16,20},{20,16},{24,28},{28,24},{1,5},{5... | collective-permute-start | bytes 196616 | tf_op jit(solution)/shard_map/ppermute | solution.py:818
  193.3 23.9 %collective-permute-start.19 = (bf16[1,512,256]{2,1,0:T(8,128)(2,1)S(1)}, bf16[1,512,256]{2,1,0:T(8,128)(2,1)S(1)}, u32[]{:S(2)}, u32[]{:S(2)}) collective-permute-start(bf16[1,512,256]{2,1,0:T(8,128)(2,1)S(1)} %collective-permute-done.18.g2), channel_id=1, source_target_pairs={{0,4},{4,0},{8,12},{12,8},{16,20},{20,16},{24,28},{28,24},{1,5},{5... | collective-permute-start | bytes 786440 | tf_op jit(solution)/shard_map/ppermute | solution.py:818
  (42 other events, 548.1 us)

commit v2 on v1

--- a/solution.py
+++ b/solution.py
@@ -407,11 +407,10 @@
     return array.reshape(groups, rows // 8, 8, 128).transpose(0, 2, 1, 3).reshape(groups * 8, rows * 16)
 
 
-def piece_members(piece):
-    chunk, place = divmod(piece, 4)
-    if chunk == 0:
-        return [place, 4 + place, 8 + place, 12 + place]
-    return [16 * chunk + 4 * place + j for j in range(4)]
+def members_of(head):
+    if head:
+        return lambda piece, j: (j // 2, 4 * (j % 2) + piece)
+    return lambda piece, j: (piece // 2, 4 * (piece % 2) + j)
 
 
 def mem(kind=pltpu.VMEM):
@@ -436,31 +435,77 @@
 TN = ((0,), (0,))
 
 
-def relayout_kernel(n, src, out, scratch):
+def corner(array):
+    block = (1,) * (array.ndim - 2) + (min(16, array.shape[-2]), 128)
+    return pl.BlockSpec(block, lambda *_: (0,) * array.ndim)
+
+
+def launch(kernel, operands, out_shapes, name, specs=None, after=(), vmem=20, **more):
+    taken = len(operands)
+    body = kernel
+    if after:
+        body = lambda *refs: kernel(*refs[:taken], *refs[taken + len(after) :])
+    if specs is None:
+        specs = [mem(pltpu.SMEM)] + [mem()] * (taken - 1)
+    more.setdefault("grid", (1,))
+    return pl.pallas_call(
+        body,
+        in_specs=list(specs) + [corner(a) for a in after],
+        out_shape=out_shapes,
+        compiler_params=limits(vmem),
+        name=name,
+        **more,
+    )(*operands, *after)
+
+
+def relayout_kernel(n, head, src, out, scratch):
     low = low_lanes(n)
-    for piece in range(12):
-        members = piece_members(piece)
+    place_of = members_of(head)
+    for piece in range(4):
         for half in range(2):
             k = 2 * piece + half
-            first, second = members[2 * half : 2 * half + 2]
-            a = src[first // 8, pl.ds(first % 8, n, stride=8), :]
-            b = src[second // 8, pl.ds(second % 8, n, stride=8), :]
+            pair = []
+            for j in (2 * half, 2 * half + 1):
+                group, line = place_of(piece, j)
+                pair.append(src[group, pl.ds(line, n, stride=8), :])
+            a, b = pair
             scratch[k, pl.ds(0, n, stride=2), :] = jnp.where(low, a, pltpu.roll(b, 64, 1))
             scratch[k, pl.ds(1, n, stride=2), :] = jnp.where(low, pltpu.roll(a, 64, 1), b)
             out[piece, :, half * 128 : (half + 1) * 128] = scratch[k].astype(out.dtype)
 
 
-def relayout(array, dtype, n=32):
+def relayout(array, dtype, first, count, n=64, after=()):
+    return launch(
+        functools.partial(relayout_kernel, n, first == 0),
+        [native_view(array)],
+        jax.ShapeDtypeStruct((4 * count, 512, 256), dtype),
+        "relayout",
+        specs=[pl.BlockSpec((2, 8 * n, 128), lambda k, i: (first + k, i, 0))],
+        after=after,
+        grid=(count, 256 // n),
+        out_specs=pl.BlockSpec((4, 2 * n, 256), lambda k, i: (k, i, 0)),
+        scratch_shapes=[pltpu.VMEM((8, 2 * n, 128), jnp.float32)],
+    )
+
+
+def pick_kernel(place, piece, *refs):
+    refs[-1][...] = piece[...]
+
+
+def picked(weights, place, after=()):
+    count = weights.shape[0] // 4
     return pl.pallas_call(
-        functools.partial(relayout_kernel, n),
-        grid=(256 // n,),
-        in_specs=[pl.BlockSpec((6, 8 * n, 128), lambda i: (0, i, 0))],
-        out_specs=pl.BlockSpec((12, 2 * n, 256), lambda i: (0, i, 0)),
-        out_shape=jax.ShapeDtypeStruct((12, 512, 256), dtype),
-        scratch_shapes=[pltpu.VMEM((24, 2 * n, 128), jnp.float32)],
-        compiler_params=limits(40),
-        name="relayout",
-    )(native_view(array))
+        pick_kernel,
+        grid_spec=pltpu.PrefetchScalarGridSpec(
+            num_scalar_prefetch=1,
+            grid=(count,),
+            in_specs=[pl.BlockSpec((1, 512, 256), lambda i, s: (4 * i + s[1], 0, 0))]
+            + [corner(a) for a in after],
+            out_specs=pl.BlockSpec((1, 512, 256), lambda i, s: (i, 0, 0)),
+        ),
+        out_shape=jax.ShapeDtypeStruct((count, 512, 256), weights.dtype),
+        name="pick",
+    )(place, weights, *after)
 
 
 def normalized(x):
@@ -491,11 +536,10 @@
     return values * cosine + other * sine
 
 
-def project_kernel(scal, x, cot, norms, bias, cosine, sine, own, r0, r1, r2, r3, send, h1):
+def project_kernel(scal, x, cot, norms, bias, cosine, sine, own, r0, r1, r2, r3, send):
     first = scal[0] == 0
     hat, _ = normalized(x[...].astype(jnp.float32))
     h = (hat * norms[0:1] + norms[1:2]).astype(jnp.bfloat16)
-    h1[...] = h
     h_own, h_other = halves(h, first)
     c_own, c_other = halves(cot[...], first)
     tokens = h.shape[0]
@@ -548,7 +592,7 @@
 
 
 def feed_forward_kernel(
-    scal, x, cot, norms, bias, own_in, own_down, r0, r1, r2, r3,
+    scal, x, cot, norms, bias, weights, r0, r1, r2, r3,
     branch, input_part, keep, send, hidden_sums, norm_grads, cot_sums,
 ):
     first = scal[0] == 0
@@ -560,8 +604,8 @@
     outs = [0.0] * 4
     for r, other in enumerate((r0, r1, r2, r3)):
         piece = scal[1] ^ r
-        in_own, in_other = own_in[piece], other[0]
-        down_own, down_other = own_down[piece], other[1]
+        in_own, in_other = weights[piece], other[0]
+        down_own, down_other = weights[4 + piece], other[1]
         pre = dot(h_own, in_own) + dot(h_other, in_other) + bias[pl.ds(piece, 1), :]
         cumulative = 0.5 * (1.0 + lax.erf(pre * 0.7071067811865476))
         slope = cumulative + pre * (0.3989422804014327 * jnp.exp(-0.5 * pre * pre))
@@ -576,9 +620,8 @@
         outs[2] += dot(grad, in_own, NT)
         outs[3] += dot(grad, in_other, NT)
         target = send if r % 2 else keep
-        for side, (h_side, c_side) in enumerate(((h_own, c_own), (h_other, c_other))):
-            target[side, r // 2, 0] = dot(h_side, grad, TN).astype(jnp.bfloat16)
-            target[side, r // 2, 1] = dot(c_side, act, TN).astype(jnp.bfloat16)
+        target[r // 2, 0] = grad
+        target[r // 2, 1] = act
     branch[...] = whole(outs[0], outs[1], first)
     second = whole(outs[2], outs[3], first)
     norm_grads[0:1] = jnp.sum(second * hat, axis=0, keepdims=True)
@@ -586,37 +629,73 @@
     input_part[...] = norm_back(second, hat, root, norms[2:3])
 
 
+def both_cores(scal, x, x_beside, cot, cot_beside, norms, at):
+    first = scal[0] == 0
+    tokens = jnp.concatenate([x[...], x_beside[...]], axis=0).astype(jnp.float32)
+    hat, _ = normalized(tokens)
+    h = (hat * norms[at : at + 1] + norms[at + 1 : at + 2]).astype(jnp.bfloat16)
+    c = jnp.concatenate([cot[...], cot_beside[...]], axis=0)
+    return list(zip(halves(h, first), halves(c, first)))
+
+
+def unit_grads_kernel(scal, x, x_beside, cot, cot_beside, norms, keep, came, *outs):
+    for side, (h, c) in enumerate(both_cores(scal, x, x_beside, cot, cot_beside, norms, 2)):
+        for far in range(2):
+            grad = jnp.concatenate([keep[far, 0], came[far, 0]], axis=0)
+            act = jnp.concatenate([keep[far, 1], came[far, 1]], axis=0)
+            outs[2 * far + side][0] = dot(h, grad, TN).astype(jnp.bfloat16)
+            outs[2 * far + side][1] = dot(c, act, TN).astype(jnp.bfloat16)
+
+
+def turn_kernel(scal, cosine, sine, back, keep, send, sums):
+    low = low_lanes(keep.shape[1])
+    for r in range(4):
+        head = scal[1] ^ r
+        grads = jnp.concatenate([back[head], back[4 + head]], axis=0)
+        left = turned(grads[:, :128].astype(jnp.float32), cosine[...], -sine[...])
+        left = left.astype(jnp.bfloat16)
+        right = grads[:, 128:]
+        target = send if r % 2 else keep
+        target[r // 2, :, :128] = left
+        target[r // 2, :, 128:] = right
+        right = jnp.where(low, right.astype(jnp.float32), 0.0)
+        wide = jnp.concatenate([left.astype(jnp.float32), right], axis=1)
+        sums[pl.ds(head, 1), :] = jnp.sum(wide, axis=0, keepdims=True)
+
+
+def split_last(piece):
+    wide = piece.astype(jnp.float32)
+    lane = lax.broadcasted_iota(jnp.int32, (1, wide.shape[1]), 1)
+    share = (lane < 3 * HD).astype(jnp.float32)
+    pre_grad = (wide * share).astype(jnp.bfloat16)
+    attended = (wide * (1.0 - share)).astype(jnp.bfloat16)
+    return pre_grad, attended
+
+
+def head_grads_kernel(scal, x, x_beside, cot, cot_beside, norms, keep, came, *outs):
+    sides = both_cores(scal, x, x_beside, cot, cot_beside, norms, 0)
+    for far in range(2):
+        piece = jnp.concatenate([keep[far], came[far]], axis=0)
+        pre_grad, attended = split_last(piece)
+        for side, (h, c) in enumerate(sides):
+            grad = dot(h, pre_grad, TN) + dot(c, attended, TN)
+            outs[2 * far + side][0] = grad.astype(jnp.bfloat16)
+
+
 def gather_kernel(
-    scal, x, cot, norms, cosine, sine, back, h1, own, r0, r1, r2, r3, ff_branch, ff_part,
-    near, far, keep, send, sums, norm_grads, parts,
+    scal, x, norms, keep, send, weights, r0, r1, r2, r3, ff_branch, ff_part,
+    near, far, norm_grads, parts,
 ):
     first = scal[0] == 0
     hat, root = normalized(x[...].astype(jnp.float32))
-    h_own, h_other = halves(h1[...], first)
-    c_own, c_other = halves(cot[...], first)
-    tokens = h_own.shape[0]
-    low = low_lanes(tokens)
     outs = [0.0] * 4
     for r, other in enumerate((r0, r1, r2, r3)):
-        head = scal[1] ^ r
-        mine, theirs = own[head], other[...]
-        grads = jnp.concatenate([back[head], back[4 + head]], axis=0)
-        left = turned(grads[:, :128].astype(jnp.float32), cosine[...], -sine[...])
-        right = grads[:, 128:].astype(jnp.float32)
-        value_grad = jnp.where(low, right, 0.0).astype(jnp.bfloat16)
-        attended = jnp.where(low, 0.0, right).astype(jnp.bfloat16)
-        pre_grad = jnp.concatenate([left.astype(jnp.bfloat16), value_grad], axis=1)
-        sums[pl.ds(head, 1), :] = jnp.sum(pre_grad.astype(jnp.float32), axis=0, keepdims=True)
-        outs[0] += dot(attended, mine[:, 128:], NT)
-        outs[1] += dot(attended, theirs[:, 128:], NT)
+        mine, theirs = weights[scal[1] ^ r], other[0]
+        pre_grad, attended = split_last((send if r % 2 else keep)[r // 2])
+        outs[0] += dot(attended, mine, NT)
+        outs[1] += dot(attended, theirs, NT)
         outs[2] += dot(pre_grad, mine, NT)
         outs[3] += dot(pre_grad, theirs, NT)
-        target = send if r % 2 else keep
-        for side, (h_side, c_side) in enumerate(((h_own, c_own), (h_other, c_other))):
-            grad = dot(h_side, pre_grad, TN)
-            out_grad = dot(c_side, attended, TN)
-            target[side, r // 2, 0, :, :128] = grad[:, :128].astype(jnp.bfloat16)
-            target[side, r // 2, 0, :, 128:] = (grad[:, 128:] + out_grad).astype(jnp.bfloat16)
     branch = ff_branch[...] + whole(outs[0], outs[1], first)
     grad = whole(outs[2], outs[3], first)
     norm_grads[0:1] = jnp.sum(grad * hat, axis=0, keepdims=True)
@@ -636,7 +715,8 @@
         input_grad[q] = cot[q].astype(jnp.float32) + piece[1].astype(jnp.float32)
 
 
-def gram_kernel(place, own, a, b, c, momenta, grads, grams):
+def gram_kernel(place, own, a, b, c, momenta, *refs):
+    grads, grams = refs[-2:]
     total = own[...].astype(jnp.float32) + a[...].astype(jnp.float32)
     total = total + b[...].astype(jnp.float32) + c[...].astype(jnp.float32)
     short = total.astype(jnp.bfloat16)
@@ -648,7 +728,7 @@
         grams[0, j] = gram[cut, cut]
 
 
-def gram_of(own, a, b, c, momenta, first_chunk, place):
+def gram_of(own, a, b, c, momenta, place, after=()):
     chunks = own.shape[0]
     piece = pl.BlockSpec((1, 512, 256), lambda i, s: (i, 0, 0))
     return pl.pallas_call(
@@ -657,23 +737,24 @@
             num_scalar_prefetch=1,
             grid=(chunks,),
             in_specs=[piece] * 4
-            + [pl.BlockSpec((1, 512, 256), lambda i, s: (4 * (first_chunk + i) + s[1], 0, 0))],
+            + [pl.BlockSpec((1, 512, 256), lambda i, s: (4 * i + s[1], 0, 0))]
+            + [corner(a) for a in after],
             out_specs=[piece, pl.BlockSpec((1, 4, HD, HD), lambda i, s: (i, 0, 0, 0))],
         ),
         out_shape=[
             jax.ShapeDtypeStruct((chunks, 512, 256), jnp.bfloat16),
             jax.ShapeDtypeStruct((chunks, 4, HD, HD), jnp.float32),
         ],
-        compiler_params=limits(32),
+        compiler_params=limits(20),
         name="gram",
-    )(place, own, a, b, c, momenta)
+    )(place, own, a, b, c, momenta, *after)
 
 
 def newton_kernel(mine, theirs, out):
     linear, square, cubic = quintic
     shape = (HD, HD)
     eye = lax.broadcasted_iota(jnp.int32, shape, 0) == lax.broadcasted_iota(jnp.int32, shape, 1)
-    high = lax.Precision.HIGHEST
+    full = lax.Precision.HIGHEST
     chunks = mine.shape[0]
     places = [(i, j) for i in range(chunks) for j in range(4)]
     states = []
@@ -683,18 +764,18 @@
         scale = 1.0 / (jnp.sqrt(trace) + muon_epsilon)
         states.append([gram * scale * scale, None, scale])
     for iteration in range(NEWTON):
-        squares = [dot(s[0], s[0], precision=high) for s in states]
+        squares = [dot(s[0], s[0], precision=full) for s in states]
         steps = [
             jnp.where(eye, linear, 0.0) + square * s[0] + cubic * sq
             for s, sq in zip(states, squares)
         ]
         if iteration == 0:
-            halfway = [dot(s[0], m, precision=high) for s, m in zip(states, steps)]
+            halfway = [dot(s[0], m, precision=full) for s, m in zip(states, steps)]
             for s, m in zip(states, steps):
                 s[1] = m
         elif iteration < NEWTON - 1:
             both = [
-                dot(jnp.concatenate([s[0], s[1]], axis=0), m, precision=high)
+                dot(jnp.concatenate([s[0], s[1]], axis=0), m, precision=full)
                 for s, m in zip(states, steps)
             ]
             halfway = [x[:HD] for x in both]
@@ -702,33 +783,34 @@
                 s[1] = x[HD:]
         else:
             for s, m in zip(states, steps):
-                s[1] = dot(s[1], m, precision=high)
+                s[1] = dot(s[1], m, precision=full)
         if iteration < NEWTON - 1:
             for s, x, m in zip(states, halfway, steps):
-                s[0] = dot(x, m, precision=high)
+                s[0] = dot(x, m, precision=full)
     for (i, j), s in zip(places, states):
-        out[i, j] = s[1] * s[2]
-
-
-def newton(mine, theirs):
-    return pl.pallas_call(
+        mix = s[1] * s[2]
+        coarse = mix.astype(jnp.bfloat16)
+        fine = (mix - coarse.astype(jnp.float32)).astype(jnp.bfloat16)
+        out[i, j] = jnp.concatenate([coarse, fine], axis=1)
+
+
+def newton(mine, theirs, after=()):
+    return launch(
         newton_kernel,
-        in_specs=[mem()] * 2,
+        [mine, theirs],
+        jax.ShapeDtypeStruct((*mine.shape[:-1], 2 * HD), jnp.bfloat16),
+        "newton",
+        specs=[mem()] * 2,
+        after=after,
         out_specs=mem(),
-        out_shape=jax.ShapeDtypeStruct(mine.shape, jnp.float32),
-        compiler_params=limits(32),
-        name="newton",
-    )(mine, theirs)
+    )
 
 
 def update_kernel(
-    n, chunk_start, scal, g0, g1, g2, g3, q0, q1, q2, q3, momenta, native_momenta, native,
-    grads_in, weights_in, momenta_in, grads, weights, moved, mixing, first, second,
+    n, head, scal, g0, g1, g2, g3, q0, q1, q2, q3, momenta, native_momenta, native, *refs
 ):
-    if chunk_start == 0:
-        place_of = lambda p, j: (j // 2, 4 * (j % 2) + p)
-    else:
-        place_of = lambda p, j: (p // 2, 4 * (p % 2) + j)
+    grads, weights, moved, mixing, first, second, steps = refs[-7:]
+    place_of = members_of(head)
 
     @pl.when((pl.program_id(0) == 0) & (pl.program_id(1) == 0))
     def _():
@@ -738,67 +820,70 @@
     def _():
         for r, q in enumerate((q0, q1, q2, q3)):
             for j in range(4):
-                mixing[r, j * HD : (j + 1) * HD, j * HD : (j + 1) * HD] = q[0, j]
+                wide = q[0, j].astype(jnp.float32)
+                other = pltpu.roll(wide, HD, 1)
+                below = low_lanes(HD) == (j % 2 == 0)
+                rows = slice(j * HD, (j + 1) * HD)
+                lanes = slice(128 * (j // 2), 128 * (j // 2) + 128)
+                pair = (wide, other) if j % 2 == 0 else (other, wide)
+                for level in range(2):
+                    part = jnp.where(below, pair[level], 0.0)
+                    mixing[r, level, rows, lanes] = part.astype(jnp.bfloat16)
 
     low = low_lanes(n)
     for r, piece in enumerate((g0, g1, g2, g3)):
         place = scal[1] ^ r
         grad = piece[0].astype(jnp.float32)
         update = 1.95 * grad + 0.9025 * momenta[place]
-        settled = dot(update, mixing[r], precision=lax.Precision.HIGHEST)
+        coarse = update.astype(jnp.bfloat16)
+        fine = (update - coarse.astype(jnp.float32)).astype(jnp.bfloat16)
+        settled = dot(coarse, mixing[r, 0]) + dot(coarse, mixing[r, 1]) + dot(fine, mixing[r, 0])
         for half in range(2):
             k = 2 * r + half
             first[k] = grad[:, half * 128 : (half + 1) * 128]
             second[k] = settled[:, half * 128 : (half + 1) * 128]
-            pairs = []
-            for s in (first, second):
-                even = s[k, pl.ds(0, n, stride=2), :]
-                odd = s[k, pl.ds(1, n, stride=2), :]
-                pairs.append(
-                    (
-                        jnp.where(low, even, pltpu.roll(odd, 64, 1)),
-                        jnp.where(low, pltpu.roll(even, 64, 1), odd),
-                    )
+            for source, target in ((first, grads), (second, steps)):
+                even = source[k, pl.ds(0, n, stride=2), :]
+                odd = source[k, pl.ds(1, n, stride=2), :]
+                lines = (
+                    jnp.where(low, even, pltpu.roll(odd, 64, 1)),
+                    jnp.where(low, pltpu.roll(even, 64, 1), odd),
                 )
-            for w in range(2):
-                group, line = place_of(place, 2 * half + w)
-                rows = pl.ds(line, n, stride=8)
-                value, step = pairs[0][w], pairs[1][w]
-                grads[group, rows, :] = value
-                moved[group, rows, :] = momentum_decay * native_momenta[group, rows, :] + value
-                weight = native[group, rows, :]
-                weights[group, rows, :] = weight - muon_rate * (4.0 * step + weight_decay * weight)
-
-
-def update(chunk_start, chunks, scal, grads, mixes, momenta, native_momenta, native, before, n=32):
-    block = pl.BlockSpec((2, 8 * n, 128), lambda k, i: (chunk_start + k, i, 0))
+                for w in range(2):
+                    group, line = place_of(place, 2 * half + w)
+                    target[group, pl.ds(line, n, stride=8), :] = lines[w]
+    moved[...] = momentum_decay * native_momenta[...] + grads[...]
+    weight = native[...]
+    weights[...] = weight - muon_rate * (4.0 * steps[...] + weight_decay * weight)
+
+
+def update(first, scal, grads, mixes, momenta, native_momenta, native, before=(), after=(), n=64):
+    chunks = grads[0].shape[0]
+    block = pl.BlockSpec((2, 8 * n, 128), lambda k, i: (first + k, i, 0))
     piece = pl.BlockSpec((1, 2 * n, 256), lambda k, i: (k, i, 0))
-    mix = pl.BlockSpec((1, 4, HD, HD), lambda k, i: (k, 0, 0, 0))
-    full = jax.ShapeDtypeStruct((6, 2048, 128), jnp.float32)
-    kernel = functools.partial(update_kernel, n, chunk_start)
-    if before is None:
-        body = kernel
-        kernel = lambda *refs: body(*refs[:12], None, None, None, *refs[12:])
-        before = ()
-    return pl.pallas_call(
-        kernel,
-        grid=(chunks, 256 // n),
-        in_specs=[mem(pltpu.SMEM)]
+    mix = pl.BlockSpec((1, 4, HD, 2 * HD), lambda k, i: (k, 0, 0, 0))
+    return launch(
+        functools.partial(update_kernel, n, first == 0),
+        [scal, *grads, *mixes, momenta, native_view(native_momenta), native_view(native), *before],
+        [jax.ShapeDtypeStruct((6, 2048, 128), jnp.float32)] * 3,
+        "update",
+        specs=[mem(pltpu.SMEM)]
         + [piece] * 4
         + [mix] * 4
-        + [pl.BlockSpec((4, 2 * n, 256), lambda k, i: (chunk_start + k, i, 0)), block, block]
+        + [pl.BlockSpec((4, 2 * n, 256), lambda k, i: (k, i, 0)), block, block]
         + [mem(pl.ANY)] * len(before),
+        after=after,
+        vmem=32,
+        grid=(chunks, 256 // n),
         out_specs=[block] * 3,
-        out_shape=[full] * 3,
         scratch_shapes=[
-            pltpu.VMEM((4, 256, 256), jnp.float32),
+            pltpu.VMEM((4, 2, 256, 256), jnp.bfloat16),
             pltpu.VMEM((8, 2 * n, 128), jnp.float32),
             pltpu.VMEM((8, 2 * n, 128), jnp.float32),
+            pltpu.VMEM((2, 8 * n, 128), jnp.float32),
         ],
         input_output_aliases={12 + i: i for i in range(len(before))},
-        compiler_params=limits(40),
-        name="update",
-    )(scal, *grads, *mixes, momenta, native_momenta, native, *before)
+    )
 
 
 def whole_device(
@@ -820,6 +905,10 @@
     def hop_tp(values, by):
         return lax.ppermute(values, "tp", [(i, i ^ by) for i in range(4)])
 
+    def spread(piece):
+        c = hop(piece, 2)
+        return [piece, hop(piece, 1), c, hop(c, 1)]
+
     x = inputs.reshape(tokens, width)
     cot = cotangent.reshape(tokens, width)
     norms = small[: 4 * width].reshape(4, width)
@@ -828,157 +917,159 @@
     qkv_bias = jnp.pad(qkv_bias, ((0, 0), (0, HD)))
     unit_start = 6 * width + H * 3 * HD + tp_at * 1024
     unit_bias = lax.dynamic_slice_in_dim(small, unit_start, 1024).reshape(4, 256)
-    frequency = rope_base ** (-2.0 * jnp.arange(ROTARY // 2, dtype=f32) / ROTARY)
+    lane = jnp.arange(128) % HD
+    frequency = rope_base ** (-2.0 * (lane % 8).astype(f32) / ROTARY)
     angles = positions.astype(f32).reshape(tokens, 1) * frequency
-    cos, sin = jnp.cos(angles), jnp.sin(angles)
-    rest = jnp.ones((tokens, HD - ROTARY), f32)
-    cosine = jnp.concatenate([cos, cos, rest, cos, cos, rest], axis=1)
-    sine = jnp.concatenate([-sin, sin, 0.0 * rest, -sin, sin, 0.0 * rest], axis=1)
-
-    weights = relayout(matrices, bf16)
-
-    def gathered(piece):
-        a = hop(piece, 4)
-        c = hop(a, 2)
-        return [a, hop(a, 1), c, hop(c, 1)]
-
-    by_chunk = weights.reshape(3, 4, 512, 256)
-    mine = lax.dynamic_index_in_dim(by_chunk, ctx_at, 1, keepdims=False)
-    others_head = gathered(mine[0])
-    others_unit = gathered(mine[1:])
-    piled = relayout(momenta, f32)
-
-    own_chunk = lambda k: pl.BlockSpec((4, 512, 256), lambda *_: (k, 0, 0))
-    send, h1 = pl.pallas_call(
+    cosine = jnp.where(lane < ROTARY, jnp.cos(angles), 1.0)
+    sign = jnp.where(lane < 8, -1.0, jnp.where(lane < ROTARY, 1.0, 0.0))
+    sine = jnp.sin(angles) * sign
+
+    head_weights = relayout(matrices, bf16, 0, 1)
+    first_hop = hop(picked(head_weights, scal), 4)
+    other_heads = spread(first_hop)
+    unit_weights = relayout(matrices, bf16, 1, 2)
+    other_units = spread(hop(picked(unit_weights, scal, after=(first_hop, cosine, sine)), 4))
+    x_beside = hop(x, 1)
+    cot_beside = hop(cot, 1)
+
+    send = launch(
         project_kernel,
-        grid=(1,),
-        in_specs=[mem(pltpu.SMEM)] + [mem()] * 6 + [own_chunk(0)] + [mem()] * 4,
-        out_specs=[mem()] * 2,
-        out_shape=[shaped((8, local_rows, 256), bf16), shaped((tokens, width), bf16)],
-        compiler_params=limits(40),
-        name="project",
-    )(scal, x, cot, norms, qkv_bias, cosine, sine, weights, *others_head)
-
+        [scal, x, cot, norms, qkv_bias, cosine, sine, head_weights]
+        + [piece[0] for piece in other_heads],
+        shaped((8, local_rows, 256), bf16),
+        "project",
+        out_specs=mem(),
+    )
     arrived = lax.all_to_all(send, both, split_axis=0, concat_axis=0, tiled=True)
+    piled_heads = relayout(momenta, f32, 0, 1, after=(send,))
+    piled_units = relayout(momenta, f32, 1, 2, after=(send,))
     documents = lax.dynamic_index_in_dim(segments, blk_at, 0, keepdims=False)
     length = documents.shape[0]
-    attended = pl.pallas_call(
+    attended = launch(
         attention_kernel,
-        in_specs=[mem()] * 2,
+        [arrived.reshape(length, 256), documents.reshape(length, 1)],
+        shaped((length, 256), bf16),
+        "attention",
+        specs=[mem()] * 2,
+        after=(piled_units,),
+        vmem=32,
         out_specs=mem(),
-        out_shape=shaped((length, 256), bf16),
         scratch_shapes=[pltpu.VMEM((length, HD), f32)] * 2,
-        compiler_params=limits(48),
-        name="attention",
-    )(arrived.reshape(length, 256), documents.reshape(length, 1))
+    )
     back = lax.all_to_all(
         attended.reshape(8, local_rows, 256), both, split_axis=0, concat_axis=0, tiled=True
     )
 
-    ff_branch, ff_part, ff_keep, ff_send, unit_sums, norm_two, cot_sums = pl.pallas_call(
+    ff_branch, ff_part, unit_keep, unit_send, unit_sums, norm_two, cot_sums = launch(
         feed_forward_kernel,
-        grid=(1,),
-        in_specs=[mem(pltpu.SMEM)] + [mem()] * 4 + [own_chunk(1), own_chunk(2)] + [mem()] * 4,
-        out_specs=[mem()] * 7,
-        out_shape=[
+        [scal, x, cot, norms, unit_bias, unit_weights, *other_units],
+        [
             shaped((tokens, width), f32),
             shaped((tokens, width), f32),
-            shaped((2, 2, 2, 512, 256), bf16),
-            shaped((2, 2, 2, 512, 256), bf16),
+            shaped((2, 2, tokens, 256), bf16),
+            shaped((2, 2, tokens, 256), bf16),
             shaped((4, 256), f32),
             shaped((2, width), f32),
             shaped((1, width), f32),
         ],
-        compiler_params=limits(48),
-        name="feed_forward",
-    )(scal, x, cot, norms, unit_bias, weights, weights, *others_unit)
-
-    def reduced(keep, send):
-        came = hop(send, 1)
-        summed = (keep.astype(f32) + came.astype(f32)).astype(bf16)
-        return summed[0, 0], hop(summed[1, 0], 4), hop(summed[0, 1], 2), hop(summed[1, 1], 6)
-
-    def spread(piece):
-        c = hop(piece, 2)
-        return [piece, hop(piece, 1), c, hop(c, 1)]
-
-    def muon(keep, send, first_chunk, before):
-        grads, grams = gram_of(*reduced(keep, send), piled, first_chunk, scal)
-        pieces = spread(grads)
-        mixes = spread(newton(grams, hop(grams, 4)))
-        return update(
-            first_chunk, grads.shape[0], scal, pieces, mixes, piled, native_view(momenta),
-            native_view(matrices), before,
-        )
-
-    before = muon(ff_keep, ff_send, 1, None)
-
-    near, far, keep, send_back, qkv_sums, norm_one = pl.pallas_call(
+        "feed_forward",
+        after=(attended,),
+        out_specs=[mem()] * 7,
+    )
+    unit_grads = launch(
+        unit_grads_kernel,
+        [scal, x, x_beside, cot, cot_beside, norms, unit_keep, hop(unit_send, 1)],
+        [shaped((2, 512, 256), bf16)] * 4,
+        "unit_grads",
+        out_specs=[mem()] * 4,
+    )
+    head_keep, head_send, qkv_sums = launch(
+        turn_kernel,
+        [scal, cosine, sine, back],
+        [shaped((2, tokens, 256), bf16)] * 2 + [shaped((4, 256), f32)],
+        "turn",
+        after=(unit_grads[0],),
+        out_specs=[mem()] * 3,
+    )
+    near, far, norm_one = launch(
         gather_kernel,
-        grid=(1,),
-        in_specs=[mem(pltpu.SMEM)] + [mem()] * 7 + [own_chunk(0)] + [mem()] * 6,
-        out_specs=[mem()] * 6,
-        out_shape=[
+        [scal, x, norms, head_keep, head_send, head_weights, *other_heads, ff_branch, ff_part],
+        [
             shaped((2, 2, 64, width), bf16),
             shaped((2, 2, 64, width), bf16),
-            shaped((2, 2, 1, 512, 256), bf16),
-            shaped((2, 2, 1, 512, 256), bf16),
-            shaped((4, 256), f32),
             shaped((2, width), f32),
         ],
+        "gather",
+        out_specs=[mem()] * 3,
         scratch_shapes=[pltpu.VMEM((4, 2, 64, width), bf16)],
-        compiler_params=limits(48),
-        name="gather",
-    )(scal, x, cot, norms, cosine, sine, back, h1, weights, *others_head, ff_branch, ff_part)
-
-    outs = muon(keep, send_back, 0, before)
+    )
+    head_grads = launch(
+        head_grads_kernel,
+        [scal, x, x_beside, cot, cot_beside, norms, head_keep, hop(head_send, 1)],
+        [shaped((1, 512, 256), bf16)] * 4,
+        "head_grads",
+        after=(norm_one,),
+        out_specs=[mem()] * 4,
+    )
+
+    def reduced(grads):
+        return grads[0], hop(grads[1], 4), hop(grads[2], 2), hop(grads[3], 6)
+
+    unit_sum, unit_grams = gram_of(*reduced(unit_grads), piled_units, scal, after=(head_grads[0],))
+    unit_pieces = spread(unit_sum)
+    unit_mixes = spread(newton(unit_grams, hop(unit_grams, 4)))
+    before = update(1, scal, unit_pieces, unit_mixes, piled_units, momenta, matrices)
+    head_sum, head_grams = gram_of(*reduced(head_grads), piled_heads, scal)
+    head_pieces = spread(head_sum)
+    head_mixes = spread(newton(head_grams, hop(head_grams, 4), after=(before[0],)))
+    outs = update(0, scal, head_pieces, head_mixes, piled_heads, momenta, matrices, before)
 
     summed = (near.astype(f32) + hop_tp(far, 1).astype(f32)).astype(bf16)
     total = (summed[0].astype(f32) + hop_tp(summed[1], 2).astype(f32)).astype(bf16)
     beside = hop_tp(total, 2)
-    block_output, input_grad = pl.pallas_call(
+    block_output, input_grad = launch(
         finish_rows_kernel,
-        in_specs=[mem(pltpu.SMEM)] + [mem()] * 7,
+        [
+            scal,
+            x.reshape(4, 64, width),
+            cot.reshape(4, 64, width),
+            (small[4 * width : 5 * width] + small[5 * width : 6 * width]).reshape(1, width),
+            total,
+            hop_tp(total, 1),
+            beside,
+            hop_tp(beside, 1),
+        ],
+        [shaped((4, 64, width), f32)] * 2,
+        "finish_rows",
         out_specs=[mem()] * 2,
-        out_shape=[shaped((4, 64, width), f32)] * 2,
-        compiler_params=limits(32),
-        name="finish_rows",
-    )(
-        scal,
-        x.reshape(4, 64, width),
-        cot.reshape(4, 64, width),
-        (small[4 * width : 5 * width] + small[5 * width : 6 * width]).reshape(1, width),
-        total,
-        hop_tp(total, 1),
-        beside,
-        hop_tp(beside, 1),
-    )
-
-    share = jnp.where(tp_at == 0, 1.0, 0.0).astype(f32)
-    cot_total = cot_sums[0] * share
+    )
+
     local = jnp.concatenate(
         [
             norm_one.reshape(-1),
             norm_two.reshape(-1),
+            cot_sums[0],
+            qkv_sums[:, : 3 * HD].reshape(-1),
+            unit_sums.reshape(-1),
+        ]
+    )
+    parts = lax.all_gather(local, ("tp", "blk", "ctx")).reshape(4, 8, -1).sum(axis=1)
+    shared = parts[:, : 4 * width].sum(axis=0)
+    cot_total = parts[0, 4 * width : 5 * width]
+    small_grads = jnp.concatenate(
+        [
+            shared,
             cot_total,
             cot_total,
-            jnp.zeros((small.shape[0] - 6 * width,), f32),
+            parts[:, 5 * width : 5 * width + 12 * HD].reshape(-1),
+            parts[:, 5 * width + 12 * HD :].reshape(-1),
         ]
     )
-    local = lax.dynamic_update_slice_in_dim(
-        local, qkv_sums[:, : 3 * HD].reshape(-1), qkv_start, 0
-    )
-    small_grads = lax.dynamic_update_slice_in_dim(local, unit_sums.reshape(-1), unit_start, 0)
-    for by in (1, 2, 4):
-        small_grads = small_grads + hop(small_grads, by)
-    for by in (1, 2):
-        small_grads = small_grads + hop_tp(small_grads, by)
-    new_matrices_at = native_back(outs[1])
     return (
         block_output.reshape(inputs.shape),
         input_grad.reshape(inputs.shape),
         native_back(outs[0]),
-        new_matrices_at,
+        native_back(outs[1]),
         native_back(outs[2]),
         small_grads,
         *small_step(small, small_first, small_second, small_grads),

time: 229 us -> 286 us (1.25)
  blocking collectives: 0 us -> 58.1 us
  local copies, waits for them, and re-layouts: 15.6 us -> 66 us
  waiting for transfers between devices: 85.4 us -> 47.3 us
  starting transfers between devices: 45.6 us -> 33.9 us
    all_gather x0 -> x1, blocking collectives: none -> 58.1 us  [whole_device(): lax.all_gather(local, ('tp', 'blk', 'ctx')).reshape(4, 8, -1).sum(axis=1)]
    unnamed x51 -> x157, local copies, waits for them, and re-layouts: 10.3 us -> 60.5 us
    ppermute x33 -> x32, waiting for transfers between devices: 59.6 us -> 42.9 us  [hop(): return lax.ppermute(values, both, [(i, i ^ by) for i in range(8)])]
    ppermute x7 -> x5, waiting for transfers between devices: 16.9 us -> 4.44 us  [hop_tp(): return lax.ppermute(values, 'tp', [(i, i ^ by) for i in range(4)])]
    all_to_all x1, waiting for transfers between devices: 8.92 us -> 0.01 us  [whole_device(): lax.all_to_all(send, both, split_axis=0, concat_axis=0, tiled=True)]
    ppermute x33 -> x32, starting transfers between devices: 26.8 us -> 18.7 us  [hop(): return lax.ppermute(values, both, [(i, i ^ by) for i in range(8)])]
    ppermute x7 -> x5, starting transfers between devices: 11 us -> 6.51 us  [hop_tp(): return lax.ppermute(values, 'tp', [(i, i ^ by) for i in range(4)])]
    convert_element_type x2 -> x0, other arithmetic: 3.16 us -> none  [reduced(): summed = (keep.astype(f32) + came.astype(f32)).astype(bf16)]
  transfers between devices with their start and end apart: 42 -> 39, of which waited for: 15 -> 6; matrix products, arithmetic and copies ran while one was open for 5% -> 5% of each run, Pallas kernels for 27% -> 21%
where the time goes in v2:
time: 286 us; the launch traced here: 284 us
  Pallas kernels  72.8 us (25%)
  local copies, waits for them, and re-layouts  66 us (23%)
  blocking collectives  58.1 us (20%)
  waiting for transfers between devices  47.3 us (17%)
  starting transfers between devices  33.9 us (12%)
  other arithmetic  4.93 us (2%)
    pallas_call x16, Pallas kernels, launch(): pl.pallas_call(body, in_specs=list(specs) + [corner(a) for a in after], o...  62.6 us
    unnamed x157, local copies, waits for them, and re-layouts  60.5 us
    all_gather x1, blocking collectives, whole_device(): lax.all_gather(local, ('tp', 'blk', 'ctx')).reshape(4, 8, -1).sum(axis=1)  58.1 us
    ppermute x32, waiting for transfers between devices, hop(): return lax.ppermute(values, both, [(i, i ^ by) for i in range(8)])  42.9 us
    ppermute x32, starting transfers between devices, hop(): return lax.ppermute(values, both, [(i, i ^ by) for i in range(8)])  18.7 us
    ppermute x5, starting transfers between devices, hop_tp(): return lax.ppermute(values, 'tp', [(i, i ^ by) for i in range(4)])  6.51 us
  transfers between devices with their start and end apart: 39, of which 6 were waited for; matrix products, arithmetic and copies ran while one was open for 5% of the time, Pallas kernels for 21%

profile of v2, /device:TPU:0, one launch (start us, length us, event | category | flops | bytes accessed | tf_op | source)
XLA Modules:
  0.0 284.2 jit_solution(17727232352512913871)
XLA Ops:
  8.7 3.0 %collective-permute-start = (bf16[1,512,256]{2,1,0:T(8,128)(2,1)}, bf16[1,512,256]{2,1,0:T(8,128)(2,1)S(1)}, u32[]{:S(2)}, u32[]{:S(2)}) collective-permute-start(bf16[1,512,256]{2,1,0:T(8,128)(2,1)} %pick.2), channel_id=1, source_target_pairs={{0,16},{4,20},{8,24},{12,28},{16,0},{20,4},{24,8},{28,12},{1,17},{... | collective-permute-start | bytes 786440 | tf_op jit(solution)/shard_map/ppermute | solution.py:903
  23.1 13.3 %collective-permute-done.6.refs_6_ = bf16[2,512,256]{2,1,0:T(8,128)(2,1)} collective-permute-done((bf16[2,512,256]{2,1,0:T(8,128)(2,1)}, bf16[2,512,256]{2,1,0:T(8,128)(2,1)}, u32[]{:S(2)}, u32[]{:S(2)}) %collective-permute-start.6) | collective-permute-done | bytes 524320 | tf_op jit(solution)/shard_map/ppermute | solution.py:903
  38.5 16.3 %collective-permute-done.2.r2 = bf16[1,512,256]{2,1,0:T(8,128)(2,1)S(1)} collective-permute-done((bf16[1,512,256]{2,1,0:T(8,128)(2,1)}, bf16[1,512,256]{2,1,0:T(8,128)(2,1)S(1)}, u32[]{:S(2)}, u32[]{:S(2)}) %collective-permute-start.2) | collective-permute-done | bytes 262176 | tf_op jit(solution)/shard_map/ppermute | solution.py:903
  59.5 3.0 %project.1.refs_1_ = bf16[8,128,256]{2,1,0:T(8,128)(2,1)} custom-call(s32[3]{0:T(128)S(1)} %copy-done.56, bf16[256,1024]{1,0:T(8,128)(2,1)S(1)} %bitcast.78, bf16[256,1024]{1,0:T(8,128)(2,1)S(1)} %bitcast.85, f32[4,1024]{1,0:T(4,128)S(1)} %slice.43.norms.refs_3_.refs_5_, f32[4,256]{1,0:T(4,128)S(1)} %pad.4.bias, f32[256,128]{1,0:T(8,128)S(1)} %copy-done.29, ...), custom_call_target="tpu_custom_call" | custom-call | tf_op jit(solution)/shard_map/project/pallas_call | solution.py:451
  62.5 4.3 %all-to-all-start = ((bf16[8,128,256]{2,1,0:T(8,128)(2,1)}), bf16[8,128,256]{2,1,0:T(8,128)(2,1)}, u32[]{:S(2)}, u32[]{:S(2)}) async-start(bf16[8,128,256]{2,1,0:T(8,128)(2,1)} %project.1.refs_1_), calls=%async_computation | async-start | bytes 1048576 | tf_op jit(solution)/shard_map/all_to_all | solution.py:943
  71.3 3.4 %relayout.5.refs_2_.momenta = f32[8,512,256]{2,1,0:T(8,128)S(1)} custom-call(f32[6,2048,128]{2,1,0:T(8,128)S(1)} %bitcast.73, bf16[8,128,256]{2,1,0:T(8,128)(2,1)} %project.1.refs_1_), custom_call_target="tpu_custom_call" | custom-call | tf_op jit(solution)/shard_map/relayout/pallas_call | solution.py:451
  80.0 6.2 %attention.1.refs_10_ = bf16[1024,256]{1,0:T(8,128)(2,1)S(1)} custom-call(bf16[1024,256]{1,0:T(8,128)(2,1)} %bitcast.16.refs_0_, s32[1024,1]{1,0:T(8,128)S(1)} %copy-done.31, f32[8,512,256]{2,1,0:T(8,128)S(1)} %copy-done.9), custom_call_target="tpu_custom_call" | custom-call | tf_op jit(solution)/shard_map/attention/pallas_call | solution.py:451
  86.2 5.4 %feed_forward.1 = (f32[256,1024]{1,0:T(8,128)S(1)}, f32[256,1024]{1,0:T(8,128)S(1)}, bf16[2,2,256,256]{3,2,1,0:T(8,128)(2,1)S(1)}, bf16[2,2,256,256]{3,2,1,0:T(8...) custom-call(s32[3]{0:T(128)S(1)} %copy-done.56, bf16[256,1024]{1,0:T(8,128)(2,1)S(1)} %bitcast.80, ...), custom_call_target="tpu_custom_call" | custom-call | tf_op jit(solution)/shard_map/feed_forward/pallas_call | solution.py:451
  94.9 4.4 %all-to-all-start.1 = ((bf16[8,128,256]{2,1,0:T(8,128)(2,1)}), bf16[8,128,256]{2,1,0:T(8,128)(2,1)}, u32[]{:S(2)}, u32[]{:S(2)}) async-start(bf16[8,128,256]{2,1,0:T(8,128)(2,1)} %bitcast.91), calls=%async_computation.1 | async-start | bytes 1048576 | tf_op jit(solution)/shard_map/all_to_all | solution.py:959
  104.8 3.3 %unit_grads.1 = (bf16[2,512,256]{2,1,0:T(8,128)(2,1)S(1)}, bf16[2,512,256]{2,1,0:T(8,128)(2,1)S(1)}, bf16[2,512,256]{2,1,0:T(8,128)(2,1)S(1)}, bf16[2,512,256]{2,1,0:T(8,128)(2,1)S(1)}) custom-call(s32[3]{0:T(128)S(1)} %copy-done.56, bf16[256,1024]{1,0:T(8,128)(2,1)S(1)} %bitcast.81, bf16[256,1024]{1,0:T(8,128)(2,1)} %collective-permute-done.4.x_beside.refs_2_, ...), custom_call_target="tpu_custom_call" | custom-call | tf_op jit(solution)/shard_map/unit_grads/pallas_call | solution.py:451
  122.8 3.0 %gather.1 = (bf16[2,2,64,1024]{3,2,1,0:T(8,128)(2,1)S(1)}, bf16[2,2,64,1024]{3,2,1,0:T(8,128)(2,1)S(1)}, f32[2,1024]{1,0:T(2,128)S(1)}) custom-call(s32[3]{0:T(128)S(1)} %copy-done.56, bf16[256,1024]{1,0:T(8,128)(2,1)S(1)} %bitcast.82, f32[4,1024]{1,0:T(4,128)S(1)} %copy-done.46, bf16[2,256,256]{2,1,0:T(8,128)(2,1)S(1)} %get-tuple-element.45.keep.refs_6_, ...), custom_call_target="tpu_custom_call" | custom-call | tf_op jit(solution)/shard_map/gather/pallas_call | solution.py:451
  134.4 58.1 %all-gather.1 = f32[32,1,6912]{2,1,0:T(1,128)S(1)} all-gather(f32[1,1,6912]{2,1,0:T(1,128)S(1)} %reshape.184), channel_id=2, replica_groups=mesh['blk'=2,'ctx'=4,'tp'=4] {'tp','blk','ctx'}, dimensions={0}, use_global_device_ids=true | all-gather | bytes 912384 | tf_op jit(solution)/shard_map/all_gather | solution.py:1056
  195.1 4.2 %head_grads.1 = (bf16[1,512,256]{2,1,0:T(8,128)(2,1)S(1)}, bf16[1,512,256]{2,1,0:T(8,128)(2,1)S(1)}, bf16[1,512,256]{2,1,0:T(8,128)(2,1)S(1)}, bf16[1,512,256]{2,1,0:T(8,128)(2,1)}) custom-call(s32[3]{0:T(128)S(1)} %copy-done.56, bf16[256,1024]{1,0:T(8,128)(2,1)S(1)} %bitcast.83, bf16[256,1024]{1,0:T(8,128)(2,1)} %collective-permute-done.4.x_beside.refs_2_, ...), custom_call_target="tpu_custom_call" | custom-call | tf_op jit(solution)/shard_map/head_grads/pallas_call | solution.py:451
  199.4 3.4 %collective-permute-start.19 = (bf16[1,512,256]{2,1,0:T(8,128)(2,1)}, bf16[1,512,256]{2,1,0:T(8,128)(2,1)}, u32[]{:S(2)}, u32[]{:S(2)}) collective-permute-start(bf16[1,512,256]{2,1,0:T(8,128)(2,1)} %get-tuple-element.57), channel_id=1, source_target_pairs={{0,24},{4,28},{8,16},{12,20},{16,8},{20,12},{24,0},{28,4},{1,25},{... | collective-permute-start | bytes 786440 | tf_op jit(solution)/shard_map/ppermute | solution.py:903
  208.2 11.5 %collective-permute-done.30.theirs = f32[2,4,64,64]{3,2,1,0:T(8,128)S(1)} collective-permute-done((f32[2,4,64,64]{3,2,1,0:T(8,128)S(1)}, f32[2,4,64,64]{3,2,1,0:T(8,128)S(1)}, u32[]{:S(2)}, u32[]{:S(2)}) %collective-permute-start.30) | collective-permute-done | bytes 131104 | tf_op jit(solution)/shard_map/ppermute | solution.py:903
  220.3 4.0 %newton.2.q0 = bf16[2,4,64,128]{3,2,1,0:T(8,128)(2,1)S(1)} custom-call(f32[2,4,64,64]{3,2,1,0:T(8,128)S(1)} %get-tuple-element.64.mine, f32[2,4,64,64]{3,2,1,0:T(8,128)S(1)} %collective-permute-done.30.theirs), custom_call_target="tpu_custom_call" | custom-call | tf_op jit(solution)/shard_map/newton/pallas_call | solution.py:451
  236.8 2.9 %collective-permute-start.14 = (bf16[2,64,1024]{2,1,0:T(8,128)(2,1)S(1)}, bf16[2,64,1024]{2,1,0:T(8,128)(2,1)S(1)}, u32[]{:S(2)}, u32[]{:S(2)}) collective-permute-start(bf16[2,64,1024]{2,1,0:T(8,128)(2,1)S(1)} %fusion.r0), channel_id=1, source_target_pairs={{0,2},{1,3},{2,0},{3,1},{4,6},{5,7},{6,4},{7,5},{8,10},{9,11},{10,... | collective-permute-start | bytes 786440 | tf_op jit(solution)/shard_map/ppermute | solution.py:906
  241.0 2.8 copy-done.4
  243.8 2.8 copy-done.7
  248.8 11.2 %update.2 = (f32[6,2048,128]{2,1,0:T(8,128)}, f32[6,2048,128]{2,1,0:T(8,128)}, f32[6,2048,128]{2,1,0:T(8,128)}) custom-call(s32[3]{0:T(128)S(1)} %copy-done.56, bf16[2,512,256]{2,1,0:T(8,128)(2,1)} %get-tuple-element.63.g0, bf16[2,512,256]{2,1,0:T(8,128)(2,1)} %collective-permute-done.27.g1, bf16[2,512,256]{2,1,0:T(8,128)(2,1)} %collective-permute-done.28.g2, ...), custom_call_target="tpu_custom_call" | custom-call | tf_op jit(solution)/shard_map/update/pallas_call | solution.py:451
  260.0 2.8 copy-done.12
  262.8 3.1 %newton.3.q0 = bf16[1,4,64,128]{3,2,1,0:T(8,128)(2,1)S(1)} custom-call(f32[1,4,64,64]{3,2,1,0:T(8,128)S(1)} %get-tuple-element.59.refs_0_, f32[1,4,64,64]{3,2,1,0:T(8,128)S(1)} %collective-permute-done.23.refs_1_, f32[6,2048,128]{2,1,0:T(8,128)S(1)} %copy-done.12), custom_call_target="tpu_custom_call" | custom-call | tf_op jit(solution)/shard_map/newton/pallas_call | solution.py:451
  271.7 4.4 %collective-permute-done.15.r3 = bf16[2,64,1024]{2,1,0:T(8,128)(2,1)S(1)} collective-permute-done((bf16[2,64,1024]{2,1,0:T(8,128)(2,1)S(1)}, bf16[2,64,1024]{2,1,0:T(8,128)(2,1)S(1)}, u32[]{:S(2)}, u32[]{:S(2)}) %collective-permute-start.15) | collective-permute-done | bytes 262176 | tf_op jit(solution)/shard_map/ppermute | solution.py:906
  278.3 6.0 %update.3 = (f32[6,2048,128]{2,1,0:T(8,128)}, f32[6,2048,128]{2,1,0:T(8,128)}, f32[6,2048,128]{2,1,0:T(8,128)}) custom-call(s32[3]{0:T(128)S(1)} %copy-done.56, bf16[1,512,256]{2,1,0:T(8,128)(2,1)S(1)} %get-tuple-element.58.g0, bf16[1,512,256]{2,1,0:T(8,128)(2,1)S(1)} %collective-permute-done.20.g1, ...), custom_call_target="tpu_custom_call", output_to_operand_aliasing={{0}: (12, {}), {1}: (13, {}), {2}: (14, {})} | custom-call | tf_op jit(solution)/shard_map/update/pallas_call | solution.py:451
  (259 shorter events, 100.3 us)
Async XLA Ops:
  36.5 18.8 %collective-permute-start.8 = (bf16[2,512,256]{2,1,0:T(8,128)(2,1)}, bf16[2,512,256]{2,1,0:T(8,128)(2,1)}, u32[]{:S(2)}, u32[]{:S(2)}) collective-permute-start(bf16[2,512,256]{2,1,0:T(8,128)(2,1)} %collective-permute-done.6.refs_6_), channel_id=1, source_target_pairs={{0,8},{4,12},{8,0},{12,4},{16,24},{20,28},{24,16},{28,20},{1,9},{5... | collective-permute-start | bytes 1572872 | tf_op jit(solution)/shard_map/ppermute | solution.py:903
  38.0 16.8 %collective-permute-start.2 = (bf16[1,512,256]{2,1,0:T(8,128)(2,1)}, bf16[1,512,256]{2,1,0:T(8,128)(2,1)S(1)}, u32[]{:S(2)}, u32[]{:S(2)}) collective-permute-start(bf16[1,512,256]{2,1,0:T(8,128)(2,1)} %copy-done.21), channel_id=1, source_target_pairs={{0,8},{4,12},{8,0},{12,4},{16,24},{20,28},{24,16},{28,20},{1,9},{5... | collective-permute-start | bytes 786440 | tf_op jit(solution)/shard_map/ppermute | solution.py:903
  38.5 17.0 %collective-permute-start.1 = (bf16[1,512,256]{2,1,0:T(8,128)(2,1)}, bf16[1,512,256]{2,1,0:T(8,128)(2,1)S(1)}, u32[]{:S(2)}, u32[]{:S(2)}) collective-permute-start(bf16[1,512,256]{2,1,0:T(8,128)(2,1)} %copy-done.21), channel_id=1, source_target_pairs={{0,4},{4,0},{8,12},{12,8},{16,20},{20,16},{24,28},{28,24},{1,5},{5... | collective-permute-start | bytes 786440 | tf_op jit(solution)/shard_map/ppermute | solution.py:903
  54.8 31.4 %collective-permute-start.7 = (bf16[2,512,256]{2,1,0:T(8,128)(2,1)}, bf16[2,512,256]{2,1,0:T(8,128)(2,1)}, u32[]{:S(2)}, u32[]{:S(2)}) collective-permute-start(bf16[2,512,256]{2,1,0:T(8,128)(2,1)} %collective-permute-done.6.refs_6_), channel_id=1, source_target_pairs={{0,4},{4,0},{8,12},{12,8},{16,20},{20,16},{24,28},{28,24},{1,5},{5... | collective-permute-start | bytes 1572872 | tf_op jit(solution)/shard_map/ppermute | solution.py:903
  55.3 30.9 %collective-permute-start.9 = (bf16[2,512,256]{2,1,0:T(8,128)(2,1)}, bf16[2,512,256]{2,1,0:T(8,128)(2,1)}, u32[]{:S(2)}, u32[]{:S(2)}) collective-permute-start(bf16[2,512,256]{2,1,0:T(8,128)(2,1)} %collective-permute-done.8.refs_8_), channel_id=1, source_target_pairs={{0,4},{4,0},{8,12},{12,8},{16,20},{20,16},{24,28},{28,24},{1,5},{5... | collective-permute-start | bytes 1572872 | tf_op jit(solution)/shard_map/ppermute | solution.py:903
  62.5 14.3 %all-to-all-start = ((bf16[8,128,256]{2,1,0:T(8,128)(2,1)}), bf16[8,128,256]{2,1,0:T(8,128)(2,1)}, u32[]{:S(2)}, u32[]{:S(2)}) async-start(bf16[8,128,256]{2,1,0:T(8,128)(2,1)} %project.1.refs_1_), calls=%async_computation | async-start | bytes 1048576 | tf_op jit(solution)/shard_map/all_to_all | solution.py:943
  66.9 37.9 %collective-permute-start.4 = (bf16[256,1024]{1,0:T(8,128)(2,1)S(1)}, bf16[256,1024]{1,0:T(8,128)(2,1)}, u32[]{:S(2)}, u32[]{:S(2)}) collective-permute-start(bf16[256,1024]{1,0:T(8,128)(2,1)S(1)} %bitcast.79), channel_id=1, source_target_pairs={{0,4},{4,0},{8,12},{12,8},{16,20},{20,16},{24,28},{28,24},{1,5},{5... | collective-permute-start | bytes 1572872 | tf_op jit(solution)/shard_map/ppermute | solution.py:903
  67.0 37.7 %collective-permute-start.5 = (bf16[256,1024]{1,0:T(8,128)(2,1)S(1)}, bf16[256,1024]{1,0:T(8,128)(2,1)}, u32[]{:S(2)}, u32[]{:S(2)}) collective-permute-start(bf16[256,1024]{1,0:T(8,128)(2,1)S(1)} %bitcast.86), channel_id=1, source_target_pairs={{0,4},{4,0},{8,12},{12,8},{16,20},{20,16},{24,28},{28,24},{1,5},{5... | collective-permute-start | bytes 1572872 | tf_op jit(solution)/shard_map/ppermute | solution.py:903
  94.9 16.4 %all-to-all-start.1 = ((bf16[8,128,256]{2,1,0:T(8,128)(2,1)}), bf16[8,128,256]{2,1,0:T(8,128)(2,1)}, u32[]{:S(2)}, u32[]{:S(2)}) async-start(bf16[8,128,256]{2,1,0:T(8,128)(2,1)} %bitcast.91), calls=%async_computation.1 | async-start | bytes 1048576 | tf_op jit(solution)/shard_map/all_to_all | solution.py:959
  115.4 78.0 %collective-permute-start.16 = (bf16[2,256,256]{2,1,0:T(8,128)(2,1)}, bf16[2,256,256]{2,1,0:T(8,128)(2,1)}, u32[]{:S(2)}, u32[]{:S(2)}) collective-permute-start(bf16[2,256,256]{2,1,0:T(8,128)(2,1)} %get-tuple-element.46.send), channel_id=1, source_target_pairs={{0,4},{4,0},{8,12},{12,8},{16,20},{20,16},{24,28},{28,24},{1,5},{5... | collective-permute-start | bytes 786440 | tf_op jit(solution)/shard_map/ppermute | solution.py:903
  129.3 70.1 %collective-permute-start.24 = (bf16[2,512,256]{2,1,0:T(8,128)(2,1)}, bf16[2,512,256]{2,1,0:T(8,128)(2,1)S(1)}, u32[]{:S(2)}, u32[]{:S(2)}) collective-permute-start(bf16[2,512,256]{2,1,0:T(8,128)(2,1)} %copy-done.65), channel_id=1, source_target_pairs={{0,16},{4,20},{8,24},{12,28},{16,0},{20,4},{24,8},{28,12},{1,17},{... | collective-permute-start | bytes 1572872 | tf_op jit(solution)/shard_map/ppermute | solution.py:903
  131.0 68.4 %collective-permute-start.25 = (bf16[2,512,256]{2,1,0:T(8,128)(2,1)}, bf16[2,512,256]{2,1,0:T(8,128)(2,1)S(1)}, u32[]{:S(2)}, u32[]{:S(2)}) collective-permute-start(bf16[2,512,256]{2,1,0:T(8,128)(2,1)} %copy-done.64), channel_id=1, source_target_pairs={{0,8},{4,12},{8,0},{12,4},{16,24},{20,28},{24,16},{28,20},{1,9},{5... | collective-permute-start | bytes 1572872 | tf_op jit(solution)/shard_map/ppermute | solution.py:903
  132.5 70.3 %collective-permute-start.26 = (bf16[2,512,256]{2,1,0:T(8,128)(2,1)}, bf16[2,512,256]{2,1,0:T(8,128)(2,1)S(1)}, u32[]{:S(2)}, u32[]{:S(2)}) collective-permute-start(bf16[2,512,256]{2,1,0:T(8,128)(2,1)} %copy-done.62), channel_id=1, source_target_pairs={{0,24},{4,28},{8,16},{12,20},{16,8},{20,12},{24,0},{28,4},{1,25},{... | collective-permute-start | bytes 1572872 | tf_op jit(solution)/shard_map/ppermute | solution.py:903
  132.8 73.9 %collective-permute-start.11 = (bf16[2,2,64,1024]{3,2,1,0:T(8,128)(2,1)}, bf16[2,2,64,1024]{3,2,1,0:T(8,128)(2,1)S(1)}, u32[]{:S(2)}, u32[]{:S(2)}) collective-permute-start(bf16[2,2,64,1024]{3,2,1,0:T(8,128)(2,1)} %copy-done.63), channel_id=1, source_target_pairs={{0,1},{1,0},{2,3},{3,2},{4,5},{5,4},{6,7},{7,6},{8,9},{9,8},{10,11... | collective-permute-start | bytes 1572872 | tf_op jit(solution)/shard_map/ppermute | solution.py:906
  199.3 25.0 %collective-permute-start.18 = (bf16[1,512,256]{2,1,0:T(8,128)(2,1)S(1)}, bf16[1,512,256]{2,1,0:T(8,128)(2,1)S(1)}, u32[]{:S(2)}, u32[]{:S(2)}) collective-permute-start(bf16[1,512,256]{2,1,0:T(8,128)(2,1)S(1)} %get-tuple-element.56), channel_id=1, source_target_pairs={{0,8},{4,12},{8,0},{12,4},{16,24},{20,28},{24,16},{28,20},{1,9},{5... | collective-permute-start | bytes 786440 | tf_op jit(solution)/shard_map/ppermute | solution.py:903
  199.4 29.2 %collective-permute-start.19 = (bf16[1,512,256]{2,1,0:T(8,128)(2,1)}, bf16[1,512,256]{2,1,0:T(8,128)(2,1)}, u32[]{:S(2)}, u32[]{:S(2)}) collective-permute-start(bf16[1,512,256]{2,1,0:T(8,128)(2,1)} %get-tuple-element.57), channel_id=1, source_target_pairs={{0,24},{4,28},{8,16},{12,20},{16,8},{20,12},{24,0},{28,4},{1,25},{... | collective-permute-start | bytes 786440 | tf_op jit(solution)/shard_map/ppermute | solution.py:903
  206.7 18.8 %collective-permute-start.28 = (bf16[2,512,256]{2,1,0:T(8,128)(2,1)}, bf16[2,512,256]{2,1,0:T(8,128)(2,1)}, u32[]{:S(2)}, u32[]{:S(2)}) collective-permute-start(bf16[2,512,256]{2,1,0:T(8,128)(2,1)} %get-tuple-element.63.g0), channel_id=1, source_target_pairs={{0,8},{4,12},{8,0},{12,4},{16,24},{20,28},{24,16},{28,20},{1,9},{5... | collective-permute-start | bytes 1572872 | tf_op jit(solution)/shard_map/ppermute | solution.py:903
  208.2 31.5 %collective-permute-start.27 = (bf16[2,512,256]{2,1,0:T(8,128)(2,1)}, bf16[2,512,256]{2,1,0:T(8,128)(2,1)}, u32[]{:S(2)}, u32[]{:S(2)}) collective-permute-start(bf16[2,512,256]{2,1,0:T(8,128)(2,1)} %get-tuple-element.63.g0), channel_id=1, source_target_pairs={{0,4},{4,0},{8,12},{12,8},{16,20},{20,16},{24,28},{28,24},{1,5},{5... | collective-permute-start | bytes 1572872 | tf_op jit(solution)/shard_map/ppermute | solution.py:903
  219.7 14.4 %collective-permute-start.12 = (bf16[2,64,1024]{2,1,0:T(8,128)(2,1)}, bf16[2,64,1024]{2,1,0:T(8,128)(2,1)}, u32[]{:S(2)}, u32[]{:S(2)}) collective-permute-start(bf16[2,64,1024]{2,1,0:T(8,128)(2,1)} %slice_bitcast_fusion), channel_id=1, source_target_pairs={{0,2},{1,3},{2,0},{3,1},{4,6},{5,7},{6,4},{7,5},{8,10},{9,11},{10,... | collective-permute-start | bytes 786440 | tf_op jit(solution)/shard_map/ppermute | solution.py:906
  225.5 15.5 %collective-permute-start.29 = (bf16[2,512,256]{2,1,0:T(8,128)(2,1)}, bf16[2,512,256]{2,1,0:T(8,128)(2,1)}, u32[]{:S(2)}, u32[]{:S(2)}) collective-permute-start(bf16[2,512,256]{2,1,0:T(8,128)(2,1)} %collective-permute-done.28.g2), channel_id=1, source_target_pairs={{0,4},{4,0},{8,12},{12,8},{16,20},{20,16},{24,28},{28,24},{1,5},{5... | collective-permute-start | bytes 1572872 | tf_op jit(solution)/shard_map/ppermute | solution.py:903
  233.0 27.0 %collective-permute-start.23 = (f32[1,4,64,64]{3,2,1,0:T(8,128)S(1)}, f32[1,4,64,64]{3,2,1,0:T(8,128)S(1)}, u32[]{:S(2)}, u32[]{:S(2)}) collective-permute-start(f32[1,4,64,64]{3,2,1,0:T(8,128)S(1)} %get-tuple-element.59.refs_0_), channel_id=1, source_target_pairs={{0,16},{4,20},{8,24},{12,28},{16,0},{20,4},{24,8},{28,12},{1,17},{... | collective-permute-start | bytes 196616 | tf_op jit(solution)/shard_map/ppermute | solution.py:903
  235.8 31.3 %collective-permute-start.21 = (bf16[1,512,256]{2,1,0:T(8,128)(2,1)S(1)}, bf16[1,512,256]{2,1,0:T(8,128)(2,1)S(1)}, u32[]{:S(2)}, u32[]{:S(2)}) collective-permute-start(bf16[1,512,256]{2,1,0:T(8,128)(2,1)S(1)} %get-tuple-element.58.g0), channel_id=1, source_target_pairs={{0,8},{4,12},{8,0},{12,4},{16,24},{20,28},{24,16},{28,20},{1,9},{5... | collective-permute-start | bytes 786440 | tf_op jit(solution)/shard_map/ppermute | solution.py:903
  236.8 30.8 %collective-permute-start.14 = (bf16[2,64,1024]{2,1,0:T(8,128)(2,1)S(1)}, bf16[2,64,1024]{2,1,0:T(8,128)(2,1)S(1)}, u32[]{:S(2)}, u32[]{:S(2)}) collective-permute-start(bf16[2,64,1024]{2,1,0:T(8,128)(2,1)S(1)} %fusion.r0), channel_id=1, source_target_pairs={{0,2},{1,3},{2,0},{3,1},{4,6},{5,7},{6,4},{7,5},{8,10},{9,11},{10,... | collective-permute-start | bytes 786440 | tf_op jit(solution)/shard_map/ppermute | solution.py:906
  239.7 29.9 %collective-permute-start.13 = (bf16[2,64,1024]{2,1,0:T(8,128)(2,1)S(1)}, bf16[2,64,1024]{2,1,0:T(8,128)(2,1)S(1)}, u32[]{:S(2)}, u32[]{:S(2)}) collective-permute-start(bf16[2,64,1024]{2,1,0:T(8,128)(2,1)S(1)} %fusion.r0), channel_id=1, source_target_pairs={{0,1},{1,0},{2,3},{3,2},{4,5},{5,4},{6,7},{7,6},{8,9},{9,8},{10,11... | collective-permute-start | bytes 786440 | tf_op jit(solution)/shard_map/ppermute | solution.py:906
  (89 other events, 923.1 us)

commit v3 on v2

--- a/solution.py
+++ b/solution.py
@@ -440,25 +440,39 @@
     return pl.BlockSpec(block, lambda *_: (0,) * array.ndim)
 
 
-def launch(kernel, operands, out_shapes, name, specs=None, after=(), vmem=20, **more):
+def takes(microseconds):
+    return pl.CostEstimate(
+        flops=int(microseconds * 1.15e9), transcendentals=0, bytes_accessed=int(1e6)
+    )
+
+
+def full(array):
+    return pl.BlockSpec(array.shape, lambda *_: (0,) * array.ndim)
+
+
+def launch(kernel, operands, out_shapes, name, specs=None, after=(), vmem=20, cost=3, **more):
     taken = len(operands)
     body = kernel
     if after:
         body = lambda *refs: kernel(*refs[:taken], *refs[taken + len(after) :])
     if specs is None:
-        specs = [mem(pltpu.SMEM)] + [mem()] * (taken - 1)
+        specs = [mem(pltpu.SMEM)] + [full(a) for a in operands[1:]]
+    if "out_specs" not in more:
+        more["out_specs"] = jax.tree.map(full, out_shapes)
     more.setdefault("grid", (1,))
     return pl.pallas_call(
         body,
         in_specs=list(specs) + [corner(a) for a in after],
         out_shape=out_shapes,
         compiler_params=limits(vmem),
+        cost_estimate=takes(cost),
         name=name,
         **more,
     )(*operands, *after)
 
 
-def relayout_kernel(n, head, src, out, scratch):
+def relayout_kernel(n, head, scal, src, out, *refs):
+    scratch = refs[-1]
     low = low_lanes(n)
     place_of = members_of(head)
     for piece in range(4):
@@ -472,40 +486,44 @@
             scratch[k, pl.ds(0, n, stride=2), :] = jnp.where(low, a, pltpu.roll(b, 64, 1))
             scratch[k, pl.ds(1, n, stride=2), :] = jnp.where(low, pltpu.roll(a, 64, 1), b)
             out[piece, :, half * 128 : (half + 1) * 128] = scratch[k].astype(out.dtype)
-
-
-def relayout(array, dtype, first, count, n=64, after=()):
+    if len(refs) == 2:
+        refs[0][0] = out[scal[1]]
+
+
+def relayout(scal, array, dtype, first, count, mine=False, n=64, after=()):
+    shapes = [jax.ShapeDtypeStruct((4 * count, 512, 256), dtype)]
+    specs = [pl.BlockSpec((4, 2 * n, 256), lambda k, i: (k, i, 0))]
+    if mine:
+        shapes.append(jax.ShapeDtypeStruct((count, 512, 256), dtype))
+        specs.append(pl.BlockSpec((1, 2 * n, 256), lambda k, i: (k, i, 0)))
     return launch(
         functools.partial(relayout_kernel, n, first == 0),
-        [native_view(array)],
-        jax.ShapeDtypeStruct((4 * count, 512, 256), dtype),
+        [scal, native_view(array)],
+        shapes,
         "relayout",
-        specs=[pl.BlockSpec((2, 8 * n, 128), lambda k, i: (first + k, i, 0))],
+        specs=[
+            mem(pltpu.SMEM),
+            pl.BlockSpec((2, 8 * n, 128), lambda k, i: (first + k, i, 0)),
+        ],
         after=after,
+        cost=1.3 * count,
         grid=(count, 256 // n),
-        out_specs=pl.BlockSpec((4, 2 * n, 256), lambda k, i: (k, i, 0)),
+        out_specs=specs,
         scratch_shapes=[pltpu.VMEM((8, 2 * n, 128), jnp.float32)],
     )
 
 
-def pick_kernel(place, piece, *refs):
-    refs[-1][...] = piece[...]
-
-
-def picked(weights, place, after=()):
-    count = weights.shape[0] // 4
-    return pl.pallas_call(
-        pick_kernel,
-        grid_spec=pltpu.PrefetchScalarGridSpec(
-            num_scalar_prefetch=1,
-            grid=(count,),
-            in_specs=[pl.BlockSpec((1, 512, 256), lambda i, s: (4 * i + s[1], 0, 0))]
-            + [corner(a) for a in after],
-            out_specs=pl.BlockSpec((1, 512, 256), lambda i, s: (i, 0, 0)),
-        ),
-        out_shape=jax.ShapeDtypeStruct((count, 512, 256), weights.dtype),
-        name="pick",
-    )(place, weights, *after)
+def add_up(groups):
+    for parts, target in groups:
+        values = [part[...].astype(jnp.float32) for part in parts]
+        while len(values) > 1:
+            values = [sum(values[i : i + 2]) for i in range(0, len(values), 2)]
+        target[...] = values[0].astype(target.dtype)
+
+
+def grouped(refs, counts, targets):
+    refs = iter(refs)
+    return [([next(refs) for _ in range(n)], target) for n, target in zip(counts, targets)]
 
 
 def normalized(x):
@@ -672,7 +690,10 @@
     return pre_grad, attended
 
 
-def head_grads_kernel(scal, x, x_beside, cot, cot_beside, norms, keep, came, *outs):
+def head_grads_kernel(
+    scal, x, x_beside, cot, cot_beside, norms, keep, came, totals, totals_came, *outs
+):
+    add_up([((totals, totals_came), outs[4])])
     sides = both_cores(scal, x, x_beside, cot, cot_beside, norms, 0)
     for far in range(2):
         piece = jnp.concatenate([keep[far], came[far]], axis=0)
@@ -684,7 +705,7 @@
 
 def gather_kernel(
     scal, x, norms, keep, send, weights, r0, r1, r2, r3, ff_branch, ff_part,
-    near, far, norm_grads, parts,
+    norm_two, cot_sums, unit_sums, qkv_sums, z0, z1, z2, z3, totals, parts,
 ):
     first = scal[0] == 0
     hat, root = normalized(x[...].astype(jnp.float32))
@@ -698,14 +719,21 @@
         outs[3] += dot(pre_grad, theirs, NT)
     branch = ff_branch[...] + whole(outs[0], outs[1], first)
     grad = whole(outs[2], outs[3], first)
-    norm_grads[0:1] = jnp.sum(grad * hat, axis=0, keepdims=True)
-    norm_grads[1:2] = jnp.sum(grad, axis=0, keepdims=True)
+    totals[...] = jnp.zeros_like(totals)
+    rows = [jnp.sum(grad * hat, axis=0, keepdims=True), jnp.sum(grad, axis=0, keepdims=True)]
+    rows += [norm_two[0:1], norm_two[1:2], cot_sums[...]]
+    for i, row in enumerate(rows):
+        for q in range(4):
+            at = 4 * (i % 2) + q
+            totals[i // 2, at : at + 1, :] = row[:, 256 * q : 256 * q + 256]
+    totals[3 + scal[2], 0:4, :] = qkv_sums[...]
+    totals[3 + scal[2], 4:8, :] = unit_sums[...]
     input_part = ff_part[...] + norm_back(grad, hat, root, norms[0:1])
     for q in range(4):
         parts[q, 0] = branch[64 * q : 64 * q + 64].astype(jnp.bfloat16)
         parts[q, 1] = input_part[64 * q : 64 * q + 64].astype(jnp.bfloat16)
     for r in range(4):
-        (far if r % 2 else near)[r // 2] = parts[scal[2] ^ r]
+        (z0, z1, z2, z3)[r][...] = parts[scal[2] ^ r]
 
 
 def finish_rows_kernel(scal, x, cot, bias, r0, r1, r2, r3, block_output, input_grad):
@@ -715,8 +743,14 @@
         input_grad[q] = cot[q].astype(jnp.float32) + piece[1].astype(jnp.float32)
 
 
-def gram_kernel(place, own, a, b, c, momenta, *refs):
-    grads, grams = refs[-2:]
+def gram_kernel(counts, place, own, a, b, c, momenta, *refs):
+    sums = len(counts)
+    grads, grams = refs[-2 - sums], refs[-1 - sums]
+
+    @pl.when(pl.program_id(0) == 0)
+    def _():
+        add_up(grouped(refs, counts, refs[len(refs) - sums :]))
+
     total = own[...].astype(jnp.float32) + a[...].astype(jnp.float32)
     total = total + b[...].astype(jnp.float32) + c[...].astype(jnp.float32)
     short = total.astype(jnp.bfloat16)
@@ -728,29 +762,38 @@
         grams[0, j] = gram[cut, cut]
 
 
-def gram_of(own, a, b, c, momenta, place, after=()):
+def gram_of(own, a, b, c, momenta, place, sums, after=()):
     chunks = own.shape[0]
     piece = pl.BlockSpec((1, 512, 256), lambda i, s: (i, 0, 0))
+    flat = [part for group in sums for part in group]
+    targets = [jax.ShapeDtypeStruct(group[0].shape, group[0].dtype) for group in sums]
     return pl.pallas_call(
-        gram_kernel,
+        functools.partial(gram_kernel, [len(group) for group in sums]),
         grid_spec=pltpu.PrefetchScalarGridSpec(
             num_scalar_prefetch=1,
             grid=(chunks,),
             in_specs=[piece] * 4
             + [pl.BlockSpec((1, 512, 256), lambda i, s: (4 * i + s[1], 0, 0))]
+            + [full(part) for part in flat]
             + [corner(a) for a in after],
-            out_specs=[piece, pl.BlockSpec((1, 4, HD, HD), lambda i, s: (i, 0, 0, 0))],
+            out_specs=[piece, pl.BlockSpec((1, 4, HD, HD), lambda i, s: (i, 0, 0, 0))]
+            + [full(target) for target in targets],
         ),
         out_shape=[
             jax.ShapeDtypeStruct((chunks, 512, 256), jnp.bfloat16),
             jax.ShapeDtypeStruct((chunks, 4, HD, HD), jnp.float32),
+            *targets,
         ],
         compiler_params=limits(20),
+        cost_estimate=takes(2.5),
         name="gram",
-    )(place, own, a, b, c, momenta, *after)
-
-
-def newton_kernel(mine, theirs, out):
+    )(place, own, a, b, c, momenta, *flat, *after)
+
+
+def newton_kernel(counts, mine, theirs, *refs):
+    taken = sum(counts)
+    out = refs[taken]
+    add_up(grouped(refs, counts, refs[taken + 1 :]))
     linear, square, cubic = quintic
     shape = (HD, HD)
     eye = lax.broadcasted_iota(jnp.int32, shape, 0) == lax.broadcasted_iota(jnp.int32, shape, 1)
@@ -794,15 +837,18 @@
         out[i, j] = jnp.concatenate([coarse, fine], axis=1)
 
 
-def newton(mine, theirs, after=()):
+def newton(mine, theirs, sums, after=()):
+    flat = [part for group in sums for part in group]
+    operands = [mine, theirs, *flat]
     return launch(
-        newton_kernel,
-        [mine, theirs],
-        jax.ShapeDtypeStruct((*mine.shape[:-1], 2 * HD), jnp.bfloat16),
+        functools.partial(newton_kernel, [len(group) for group in sums]),
+        operands,
+        [jax.ShapeDtypeStruct((*mine.shape[:-1], 2 * HD), jnp.bfloat16)]
+        + [jax.ShapeDtypeStruct(group[0].shape, group[0].dtype) for group in sums],
         "newton",
-        specs=[mem()] * 2,
+        cost=3.5,
+        specs=[full(a) for a in operands],
         after=after,
-        out_specs=mem(),
     )
 
 
@@ -873,7 +919,7 @@
         + [pl.BlockSpec((4, 2 * n, 256), lambda k, i: (k, i, 0)), block, block]
         + [mem(pl.ANY)] * len(before),
         after=after,
-        vmem=32,
+        cost=5.5 * chunks,
         grid=(chunks, 256 // n),
         out_specs=[block] * 3,
         scratch_shapes=[
@@ -924,11 +970,15 @@
     sign = jnp.where(lane < 8, -1.0, jnp.where(lane < ROTARY, 1.0, 0.0))
     sine = jnp.sin(angles) * sign
 
-    head_weights = relayout(matrices, bf16, 0, 1)
-    first_hop = hop(picked(head_weights, scal), 4)
+    head_weights, mine = relayout(scal, matrices, bf16, 0, 1, mine=True)
+    first_hop = hop(mine, 4)
     other_heads = spread(first_hop)
-    unit_weights = relayout(matrices, bf16, 1, 2)
-    other_units = spread(hop(picked(unit_weights, scal, after=(first_hop, cosine, sine)), 4))
+    (piled_heads,) = relayout(scal, momenta, f32, 0, 1, after=(mine,))
+    (piled_units,) = relayout(scal, momenta, f32, 1, 2, after=(mine,))
+    unit_weights, mine = relayout(
+        scal, matrices, bf16, 1, 2, mine=True, after=(first_hop, piled_heads, piled_units, cosine, sine)
+    )
+    other_units = spread(hop(mine, 4))
     x_beside = hop(x, 1)
     cot_beside = hop(cot, 1)
 
@@ -938,11 +988,8 @@
         + [piece[0] for piece in other_heads],
         shaped((8, local_rows, 256), bf16),
         "project",
-        out_specs=mem(),
     )
     arrived = lax.all_to_all(send, both, split_axis=0, concat_axis=0, tiled=True)
-    piled_heads = relayout(momenta, f32, 0, 1, after=(send,))
-    piled_units = relayout(momenta, f32, 1, 2, after=(send,))
     documents = lax.dynamic_index_in_dim(segments, blk_at, 0, keepdims=False)
     length = documents.shape[0]
     attended = launch(
@@ -950,10 +997,8 @@
         [arrived.reshape(length, 256), documents.reshape(length, 1)],
         shaped((length, 256), bf16),
         "attention",
-        specs=[mem()] * 2,
-        after=(piled_units,),
-        vmem=32,
-        out_specs=mem(),
+        cost=6,
+        specs=[full(arrived.reshape(length, 256)), pl.BlockSpec((length, 1), lambda *_: (0, 0))],
         scratch_shapes=[pltpu.VMEM((length, HD), f32)] * 2,
     )
     back = lax.all_to_all(
@@ -973,59 +1018,69 @@
             shaped((1, width), f32),
         ],
         "feed_forward",
+        cost=5.5,
         after=(attended,),
-        out_specs=[mem()] * 7,
+    )
+    head_keep, head_send, qkv_sums = launch(
+        turn_kernel,
+        [scal, cosine, sine, back],
+        [shaped((2, tokens, 256), bf16)] * 2 + [shaped((4, 256), f32)],
+        "turn",
+        cost=2,
+        after=(unit_sums,),
     )
     unit_grads = launch(
         unit_grads_kernel,
         [scal, x, x_beside, cot, cot_beside, norms, unit_keep, hop(unit_send, 1)],
         [shaped((2, 512, 256), bf16)] * 4,
         "unit_grads",
-        out_specs=[mem()] * 4,
-    )
-    head_keep, head_send, qkv_sums = launch(
-        turn_kernel,
-        [scal, cosine, sine, back],
-        [shaped((2, tokens, 256), bf16)] * 2 + [shaped((4, 256), f32)],
-        "turn",
+        cost=3.5,
+        after=(qkv_sums,),
+    )
+    sums = [norm_two, cot_sums, unit_sums, qkv_sums]
+    *quarters, totals = launch(
+        gather_kernel,
+        [scal, x, norms, head_keep, head_send, head_weights, *other_heads, ff_branch, ff_part, *sums],
+        [shaped((2, 64, width), bf16)] * 4 + [shaped((7, 8, 256), f32)],
+        "gather",
         after=(unit_grads[0],),
-        out_specs=[mem()] * 3,
-    )
-    near, far, norm_one = launch(
-        gather_kernel,
-        [scal, x, norms, head_keep, head_send, head_weights, *other_heads, ff_branch, ff_part],
-        [
-            shaped((2, 2, 64, width), bf16),
-            shaped((2, 2, 64, width), bf16),
-            shaped((2, width), f32),
-        ],
-        "gather",
-        out_specs=[mem()] * 3,
         scratch_shapes=[pltpu.VMEM((4, 2, 64, width), bf16)],
     )
-    head_grads = launch(
+    *head_grads, totals = launch(
         head_grads_kernel,
-        [scal, x, x_beside, cot, cot_beside, norms, head_keep, hop(head_send, 1)],
-        [shaped((1, 512, 256), bf16)] * 4,
+        [scal, x, x_beside, cot, cot_beside, norms, head_keep, hop(head_send, 1), totals, hop(totals, 1)],
+        [shaped((1, 512, 256), bf16)] * 4 + [shaped((7, 8, 256), f32)],
         "head_grads",
-        after=(norm_one,),
-        out_specs=[mem()] * 4,
+        cost=4,
     )
 
     def reduced(grads):
         return grads[0], hop(grads[1], 4), hop(grads[2], 2), hop(grads[3], 6)
 
-    unit_sum, unit_grams = gram_of(*reduced(unit_grads), piled_units, scal, after=(head_grads[0],))
+    unit_reduced = reduced(unit_grads)
+    head_reduced = reduced(head_grads)
+    spread_totals = [totals, hop(totals, 4), hop(totals, 2), hop(totals, 6)]
+    unit_sum, unit_grams, near, far = gram_of(
+        *unit_reduced,
+        piled_units,
+        scal,
+        [(quarters[0], hop_tp(quarters[1], 1)), (quarters[2], hop_tp(quarters[3], 1))],
+        after=(head_grads[0],),
+    )
     unit_pieces = spread(unit_sum)
-    unit_mixes = spread(newton(unit_grams, hop(unit_grams, 4)))
-    before = update(1, scal, unit_pieces, unit_mixes, piled_units, momenta, matrices)
-    head_sum, head_grams = gram_of(*reduced(head_grads), piled_heads, scal)
+    unit_mix, total, totals = newton(
+        unit_grams, hop(unit_grams, 4), [(near, hop_tp(far, 2)), spread_totals]
+    )
+    head_sum, head_grams, totals = gram_of(
+        *head_reduced, piled_heads, scal, [(totals, hop_tp(totals, 1))], after=(unit_mix,)
+    )
     head_pieces = spread(head_sum)
-    head_mixes = spread(newton(head_grams, hop(head_grams, 4), after=(before[0],)))
-    outs = update(0, scal, head_pieces, head_mixes, piled_heads, momenta, matrices, before)
-
-    summed = (near.astype(f32) + hop_tp(far, 1).astype(f32)).astype(bf16)
-    total = (summed[0].astype(f32) + hop_tp(summed[1], 2).astype(f32)).astype(bf16)
+    before = update(1, scal, unit_pieces, spread(unit_mix), piled_units, momenta, matrices)
+    head_mix, totals = newton(
+        head_grams, hop(head_grams, 4), [(totals, hop_tp(totals, 2))], after=(before[0],)
+    )
+    outs = update(0, scal, head_pieces, spread(head_mix), piled_heads, momenta, matrices, before)
+
     beside = hop_tp(total, 2)
     block_output, input_grad = launch(
         finish_rows_kernel,
@@ -1041,28 +1096,17 @@
         ],
         [shaped((4, 64, width), f32)] * 2,
         "finish_rows",
-        out_specs=[mem()] * 2,
-    )
-
-    local = jnp.concatenate(
-        [
-            norm_one.reshape(-1),
-            norm_two.reshape(-1),
-            cot_sums[0],
-            qkv_sums[:, : 3 * HD].reshape(-1),
-            unit_sums.reshape(-1),
-        ]
-    )
-    parts = lax.all_gather(local, ("tp", "blk", "ctx")).reshape(4, 8, -1).sum(axis=1)
-    shared = parts[:, : 4 * width].sum(axis=0)
-    cot_total = parts[0, 4 * width : 5 * width]
+        cost=2,
+    )
+
+    cot_total = totals[2, :4].reshape(-1) * 0.25
     small_grads = jnp.concatenate(
         [
-            shared,
+            totals[:2].reshape(-1),
             cot_total,
             cot_total,
-            parts[:, 5 * width : 5 * width + 12 * HD].reshape(-1),
-            parts[:, 5 * width + 12 * HD :].reshape(-1),
+            totals[3:, :4, : 3 * HD].reshape(-1),
+            totals[3:, 4:].reshape(-1),
         ]
     )
     return (

time: 286 us -> 194 us (0.68)
  blocking collectives: 58.1 us -> 0 us
  local copies, waits for them, and re-layouts: 66 us -> 21.5 us
  starting transfers between devices: 33.9 us -> 47.3 us
  waiting for transfers between devices: 47.3 us -> 54.3 us
  Pallas kernels: 72.8 us -> 66.2 us
    all_gather x1 -> x0, blocking collectives: 58.1 us -> none  [whole_device(): lax.all_gather(local, ('tp', 'blk', 'ctx')).reshape(4, 8, -1).sum(axis=1)]
    unnamed x157 -> x79, local copies, waits for them, and re-layouts: 60.5 us -> 21 us
    ppermute x32 -> x36, starting transfers between devices: 18.7 us -> 29.2 us  [hop(): return lax.ppermute(values, both, [(i, i ^ by) for i in range(8)])]
    ppermute x32 -> x36, waiting for transfers between devices: 42.9 us -> 35.1 us  [hop(): return lax.ppermute(values, both, [(i, i ^ by) for i in range(8)])]
    ppermute x5 -> x8, waiting for transfers between devices: 4.44 us -> 12.1 us  [hop_tp(): return lax.ppermute(values, 'tp', [(i, i ^ by) for i in range(4)])]
    all_to_all x1, waiting for transfers between devices: 0.01 us -> 7.1 us  [whole_device(): lax.all_to_all(send, both, split_axis=0, concat_axis=0, tiled=True)]
    pallas_call x4 -> x2, Pallas kernels: 10.1 us -> 4.28 us  [gram_of(): pl.pallas_call(functools.partial(gram_kernel, [len(group) for group in su...]
    ppermute x5 -> x8, starting transfers between devices: 6.51 us -> 11 us  [hop_tp(): return lax.ppermute(values, 'tp', [(i, i ^ by) for i in range(4)])]
  transfers between devices with their start and end apart: 39 -> 46, of which waited for: 6 -> 14; matrix products, arithmetic and copies ran while one was open for 5% -> 1% of each run, Pallas kernels for 21% -> 27%
where the time goes in v3:
time: 194 us; the launch traced here: 193 us
  Pallas kernels  66.2 us (34%)
  waiting for transfers between devices  54.3 us (28%)
  starting transfers between devices  47.3 us (24%)
  local copies, waits for them, and re-layouts  21.5 us (11%)
  other arithmetic  2.16 us (1%)
    pallas_call x16, Pallas kernels, launch(): pl.pallas_call(body, in_specs=list(specs) + [corner(a) for a in after], o...  61.9 us
    ppermute x36, waiting for transfers between devices, hop(): return lax.ppermute(values, both, [(i, i ^ by) for i in range(8)])  35.1 us
    ppermute x36, starting transfers between devices, hop(): return lax.ppermute(values, both, [(i, i ^ by) for i in range(8)])  29.2 us
    unnamed x79, local copies, waits for them, and re-layouts  21 us
    ppermute x8, waiting for transfers between devices, hop_tp(): return lax.ppermute(values, 'tp', [(i, i ^ by) for i in range(4)])  12.1 us
    ppermute x8, starting transfers between devices, hop_tp(): return lax.ppermute(values, 'tp', [(i, i ^ by) for i in range(4)])  11 us
    all_to_all x1, waiting for transfers between devices, whole_device(): lax.all_to_all(send, both, split_axis=0, concat_axis=0, tiled=True)  7.1 us
    pallas_call x2, Pallas kernels, gram_of(): pl.pallas_call(functools.partial(gram_kernel, [len(group) for group in su...  4.28 us
  transfers between devices with their start and end apart: 46, of which 14 were waited for; matrix products, arithmetic and copies ran while one was open for 1% of the time, Pallas kernels for 27%

profile of v3, /device:TPU:0, one launch (start us, length us, event | category | flops | bytes accessed | tf_op | source)
XLA Modules:
  0.0 192.8 jit_solution(2127273726941637209)
XLA Ops:
  6.3 3.0 %collective-permute-start.2 = (bf16[1,512,256]{2,1,0:T(8,128)(2,1)S(1)}, bf16[1,512,256]{2,1,0:T(8,128)(2,1)S(1)}, u32[]{:S(2)}, u32[]{:S(2)}) collective-permute-start(bf16[1,512,256]{2,1,0:T(8,128)(2,1)S(1)} %get-tuple-element.57.refs_2_), channel_id=1, source_target_pairs={{0,16},{4,20},{8,24},{12,28},{16,0},{20,4},{24,8},{28,12},{1,17},{... | collective-permute-start | bytes 786440 | tf_op jit(solution)/shard_map/ppermute | solution.py:949
  11.7 3.2 %relayout.6.refs_4_.momenta = f32[8,512,256]{2,1,0:T(8,128)S(1)} custom-call(s32[3]{0:T(128)S(1)} %pad_add_fusion.scal.refs_0_.place, f32[6,2048,128]{2,1,0:T(8,128)S(1)} %bitcast.63, bf16[1,512,256]{2,1,0:T(8,128)(2,1)S(1)} %get-tuple-element.57.refs_2_), custom_call_target="tpu_custom_call" | custom-call | flops 2990000128 | bytes 1000000 | tf_op jit(solution)/shard_map/relayout/pallas_call | solution.py:463
  15.6 3.1 %relayout.7 = (bf16[8,512,256]{2,1,0:T(8,128)(2,1)S(1)}, bf16[2,512,256]{2,1,0:T(8,128)(2,1)S(1)}) custom-call(s32[3]{0:T(128)S(1)} %pad_add_fusion.scal.refs_0_.place, f32[6,2048,128]{2,1,0:T(8,128)S(1)} %bitcast.57, bf16[1,512,256]{2,1,0:T(8,128)(2,1)S(1)} %collective-permute-done.2.refs_2_.refs_6_, f32[4,512,256]{2,1,0:T(8,128)S(1)} %relayout.5.refs_3_.momenta, ...), custom_call_target="tpu_custom_call" | custom-call | flops 2990000128 | bytes 1000000 | tf_op jit(solution)/shard_map/relayout/pallas_call | solution.py:463
  23.3 5.4 %collective-permute-done.8.refs_8_ = bf16[1,512,256]{2,1,0:T(8,128)(2,1)S(1)} collective-permute-done((bf16[1,512,256]{2,1,0:T(8,128)(2,1)S(1)}, bf16[1,512,256]{2,1,0:T(8,128)(2,1)S(1)}, u32[]{:S(2)}, u32[]{:S(2)}) %collective-permute-start.8) | collective-permute-done | bytes 262176 | tf_op jit(solution)/shard_map/ppermute | solution.py:949
  28.9 4.4 %collective-permute-done.3.refs_6_ = bf16[2,512,256]{2,1,0:T(8,128)(2,1)} collective-permute-done((bf16[2,512,256]{2,1,0:T(8,128)(2,1)S(1)}, bf16[2,512,256]{2,1,0:T(8,128)(2,1)}, u32[]{:S(2)}, u32[]{:S(2)}) %collective-permute-start.3) | collective-permute-done | bytes 524320 | tf_op jit(solution)/shard_map/ppermute | solution.py:949
  35.9 3.8 %project.1 = bf16[8,128,256]{2,1,0:T(8,128)(2,1)} custom-call(s32[3]{0:T(128)S(1)} %pad_add_fusion.scal.refs_0_.place, bf16[256,1024]{1,0:T(8,128)(2,1)} %bitcast.6.x.refs_1_, bf16[256,1024]{1,0:T(8,128)(2,1)} %bitcast.7.cot.refs_2_.refs_3_, f32[4,1024]{1,0:T(4,128)S(1)} %slice.34.norms.refs_3_.refs_5_.refs_2_, f32[4,256]{1,0:T(4,128)S(1)} %pad.4.bias, ...), custom_call_target="tpu_custom_call" | custom-call | flops 3449999872 | bytes 1000000 | tf_op jit(solution)/shard_map/project/pallas_call | solution.py:463
  39.7 3.5 %all-to-all-start = ((bf16[8,128,256]{2,1,0:T(8,128)(2,1)}), bf16[8,128,256]{2,1,0:T(8,128)(2,1)S(1)}, u32[]{:S(2)}, u32[]{:S(2)}) async-start(bf16[8,128,256]{2,1,0:T(8,128)(2,1)} %project.1), calls=%async_computation | async-start | bytes 1048576 | tf_op jit(solution)/shard_map/all_to_all | solution.py:992
  45.8 7.1 %all-to-all-done = bf16[8,128,256]{2,1,0:T(8,128)(2,1)S(1)} async-done(((bf16[8,128,256]{2,1,0:T(8,128)(2,1)}), bf16[8,128,256]{2,1,0:T(8,128)(2,1)S(1)}, u32[]{:S(2)}, u32[]{:S(2)}) %all-to-all-start) | async-done | bytes 524320 | tf_op jit(solution)/shard_map/all_to_all | solution.py:992
  52.9 5.1 %attention.1.refs_10_ = bf16[1024,256]{1,0:T(8,128)(2,1)S(1)} custom-call(bf16[1024,256]{1,0:T(8,128)(2,1)S(1)} %bitcast.69, s32[1024,1]{1,0:T(8,128)S(1)} %copy.21.seg), custom_call_target="tpu_custom_call" | custom-call | flops 6899999744 | bytes 1000000 | tf_op jit(solution)/shard_map/attention/pallas_call | solution.py:463
  58.8 3.7 %all-to-all-start.1 = ((bf16[8,128,256]{2,1,0:T(8,128)(2,1)}), bf16[8,128,256]{2,1,0:T(8,128)(2,1)S(1)}, u32[]{:S(2)}, u32[]{:S(2)}) async-start(bf16[8,128,256]{2,1,0:T(8,128)(2,1)} %bitcast.70), calls=%async_computation.1 | async-start | bytes 1048576 | tf_op jit(solution)/shard_map/all_to_all | solution.py:1004
  65.2 5.5 %feed_forward.1 = (f32[256,1024]{1,0:T(8,128)S(1)}, f32[256,1024]{1,0:T(8,128)S(1)}, bf16[2,2,256,256]{3,2,1,0:T(8,128)(2,1)S(1)}, bf16[2,2,256,256]{3,2,1,0:T(8...) custom-call(s32[3]{0:T(128)S(1)} %pad_add_fusion.scal.refs_0_.place, ...), custom_call_target="tpu_custom_call" | custom-call | flops 6325000192 | bytes 1000000 | tf_op jit(solution)/shard_map/feed_forward/pallas_call | solution.py:463
  75.5 3.8 %unit_grads.1 = (bf16[2,512,256]{2,1,0:T(8,128)(2,1)S(1)}, bf16[2,512,256]{2,1,0:T(8,128)(2,1)S(1)}, bf16[2,512,256]{2,1,0:T(8,128)(2,1)S(1)}, bf16[2,512,256]{2,1,0:T(8,128)(2,1)S(1)}) custom-call(s32[3]{0:T(128)S(1)} %pad_add_fusion.scal.refs_0_.place, bf16[256,1024]{1,0:T(8,128)(2,1)} %bitcast.6.x.refs_1_, ...), custom_call_target="tpu_custom_call" | custom-call | flops 4024999936 | bytes 1000000 | tf_op jit(solution)/shard_map/unit_grads/pallas_call | solution.py:463
  82.8 3.2 %gather.1 = (bf16[2,64,1024]{2,1,0:T(8,128)(2,1)S(1)}, bf16[2,64,1024]{2,1,0:T(8,128)(2,1)S(1)}, bf16[2,64,1024]{2,1,0:T(8,128)(2,1)S(1)}, bf16[2,64,1024]{2,1,0:T(8,128)(2,1)S(1)}, f32[7,8,256]{2,1,0:T(8,128)S(1)}) custom-call(s32[3]{0:T(128)S(1)} %pad_add_fusion.scal.refs_0_.place, bf16[256,1024]{1,0:T(8,128)(2,1)} %bitcast.6.x.refs_1_, ...), custom_call_target="tpu_custom_call" | custom-call | flops 3449999872 | bytes 1000000 | tf_op jit(solution)/shard_map/gather/pallas_call | solution.py:463
  89.0 3.5 %head_grads.1 = (bf16[1,512,256]{2,1,0:T(8,128)(2,1)S(1)}, bf16[1,512,256]{2,1,0:T(8,128)(2,1)S(1)}, bf16[1,512,256]{2,1,0:T(8,128)(2,1)S(1)}, bf16[1,512,256]{2,1,0:T(8,128)(2,1)S(1)}, f32[7,8,256]{2,1,0:T(8,128)S(1)}) custom-call(s32[3]{0:T(128)S(1)} %pad_add_fusion.scal.refs_0_.place, bf16[256,1024]{1,0:T(8,128)(2,1)} %bitcast.6.x.refs_1_, ...), custom_call_target="tpu_custom_call" | custom-call | flops 4600000000 | bytes 1000000 | tf_op jit(solution)/shard_map/head_grads/pallas_call | solution.py:463
  95.3 5.2 %collective-permute-done.15.refs_3_ = bf16[2,64,1024]{2,1,0:T(8,128)(2,1)S(1)} collective-permute-done((bf16[2,64,1024]{2,1,0:T(8,128)(2,1)S(1)}, bf16[2,64,1024]{2,1,0:T(8,128)(2,1)S(1)}, u32[]{:S(2)}, u32[]{:S(2)}) %collective-permute-start.15) | collective-permute-done | bytes 262176 | tf_op jit(solution)/shard_map/ppermute | solution.py:952
  100.5 5.3 %collective-permute-done.13.c = bf16[2,512,256]{2,1,0:T(8,128)(2,1)S(1)} collective-permute-done((bf16[2,512,256]{2,1,0:T(8,128)(2,1)S(1)}, bf16[2,512,256]{2,1,0:T(8,128)(2,1)S(1)}, u32[]{:S(2)}, u32[]{:S(2)}) %collective-permute-start.13) | collective-permute-done | bytes 524320 | tf_op jit(solution)/shard_map/ppermute | solution.py:949
  116.4 4.4 %collective-permute-done.20.refs_3_ = f32[7,8,256]{2,1,0:T(8,128)S(1)} collective-permute-done((f32[7,8,256]{2,1,0:T(8,128)S(1)}, f32[7,8,256]{2,1,0:T(8,128)S(1)}, u32[]{:S(2)}, u32[]{:S(2)}) %collective-permute-start.20) | collective-permute-done | bytes 57376 | tf_op jit(solution)/shard_map/ppermute | solution.py:949
  126.0 4.0 %newton.2 = (bf16[2,4,64,128]{3,2,1,0:T(8,128)(2,1)S(1)}, bf16[2,64,1024]{2,1,0:T(8,128)(2,1)S(1)}, f32[7,8,256]{2,1,0:T(8,128)S(1)}) custom-call(f32[2,4,64,64]{3,2,1,0:T(8,128)S(1)} %get-tuple-element.81.mine, f32[2,4,64,64]{3,2,1,0:T(8,128)S(1)} %collective-permute-done.18.theirs, bf16[2,64,1024]{2,1,0:T(8,128)(2,1)S(1)} %get-tuple-element.82.refs_0_, ...), custom_call_target="tpu_custom_call" | custom-call | flops 4024999936 | bytes 1000000 | tf_op jit(solution)/shard_map/newton/pallas_call | solution.py:463
  132.0 5.2 %collective-permute-done.28.c = bf16[1,512,256]{2,1,0:T(8,128)(2,1)S(1)} collective-permute-done((bf16[1,512,256]{2,1,0:T(8,128)(2,1)S(1)}, bf16[1,512,256]{2,1,0:T(8,128)(2,1)S(1)}, u32[]{:S(2)}, u32[]{:S(2)}) %collective-permute-start.28) | collective-permute-done | bytes 262176 | tf_op jit(solution)/shard_map/ppermute | solution.py:949
  140.5 5.3 %collective-permute-done.36.g2 = bf16[2,512,256]{2,1,0:T(8,128)(2,1)S(1)} collective-permute-done((bf16[2,512,256]{2,1,0:T(8,128)(2,1)S(1)}, bf16[2,512,256]{2,1,0:T(8,128)(2,1)S(1)}, u32[]{:S(2)}, u32[]{:S(2)}) %collective-permute-start.36) | collective-permute-done | bytes 524320 | tf_op jit(solution)/shard_map/ppermute | solution.py:949
  150.4 4.1 %collective-permute-done.25.r3 = bf16[2,64,1024]{2,1,0:T(8,128)(2,1)S(1)} collective-permute-done((bf16[2,64,1024]{2,1,0:T(8,128)(2,1)S(1)}, bf16[2,64,1024]{2,1,0:T(8,128)(2,1)S(1)}, u32[]{:S(2)}, u32[]{:S(2)}) %collective-permute-start.25) | collective-permute-done | bytes 262176 | tf_op jit(solution)/shard_map/ppermute | solution.py:952
  158.7 10.4 %update.2 = (f32[6,2048,128]{2,1,0:T(8,128)}, f32[6,2048,128]{2,1,0:T(8,128)}, f32[6,2048,128]{2,1,0:T(8,128)}) custom-call(s32[3]{0:T(128)S(1)} %pad_add_fusion.scal.refs_0_.place, bf16[2,512,256]{2,1,0:T(8,128)(2,1)S(1)} %get-tuple-element.96.g0, bf16[2,512,256]{2,1,0:T(8,128)(2,1)S(1)} %collective-permute-done.35.g1, ...), custom_call_target="tpu_custom_call" | custom-call | flops 12650000384 | bytes 1000000 | tf_op jit(solution)/shard_map/update/pallas_call | solution.py:463
  171.9 3.1 %newton.3 = (bf16[1,4,64,128]{3,2,1,0:T(8,128)(2,1)S(1)}, f32[7,8,256]{2,1,0:T(8,128)S(1)}) custom-call(f32[1,4,64,64]{3,2,1,0:T(8,128)S(1)} %get-tuple-element.94.refs_0_, f32[1,4,64,64]{3,2,1,0:T(8,128)S(1)} %collective-permute-done.33.refs_1_, f32[7,8,256]{2,1,0:T(8,128)S(1)} %get-tuple-element.95.refs_2_, ...), custom_call_target="tpu_custom_call" | custom-call | flops 4024999936 | bytes 1000000 | tf_op jit(solution)/shard_map/newton/pallas_call | solution.py:463
  186.8 5.9 %update.3 = (f32[6,2048,128]{2,1,0:T(8,128)}, f32[6,2048,128]{2,1,0:T(8,128)}, f32[6,2048,128]{2,1,0:T(8,128)}) custom-call(s32[3]{0:T(128)S(1)} %pad_add_fusion.scal.refs_0_.place, bf16[1,512,256]{2,1,0:T(8,128)(2,1)S(1)} %get-tuple-element.93.g0, ...), custom_call_target="tpu_custom_call", output_to_operand_aliasing={{0}: (12, {}), {1}: (13, {}), {2}: (14, {})} | custom-call | flops 6325000192 | bytes 1000000 | tf_op jit(solution)/shard_map/update/pallas_call | solution.py:463
  (188 shorter events, 80.4 us)
Async XLA Ops:
  20.1 13.2 %collective-permute-start.3 = (bf16[2,512,256]{2,1,0:T(8,128)(2,1)S(1)}, bf16[2,512,256]{2,1,0:T(8,128)(2,1)}, u32[]{:S(2)}, u32[]{:S(2)}) collective-permute-start(bf16[2,512,256]{2,1,0:T(8,128)(2,1)S(1)} %get-tuple-element.59), channel_id=1, source_target_pairs={{0,16},{4,20},{8,24},{12,28},{16,0},{20,4},{24,8},{28,12},{1,17},{... | collective-permute-start | bytes 1572872 | tf_op jit(solution)/shard_map/ppermute | solution.py:949
  33.3 12.5 %collective-permute-start.5 = (bf16[2,512,256]{2,1,0:T(8,128)(2,1)}, bf16[2,512,256]{2,1,0:T(8,128)(2,1)}, u32[]{:S(2)}, u32[]{:S(2)}) collective-permute-start(bf16[2,512,256]{2,1,0:T(8,128)(2,1)} %collective-permute-done.3.refs_6_), channel_id=1, source_target_pairs={{0,8},{4,12},{8,0},{12,4},{16,24},{20,28},{24,16},{28,20},{1,9},{5... | collective-permute-start | bytes 1572872 | tf_op jit(solution)/shard_map/ppermute | solution.py:949
  39.7 13.2 %all-to-all-start = ((bf16[8,128,256]{2,1,0:T(8,128)(2,1)}), bf16[8,128,256]{2,1,0:T(8,128)(2,1)S(1)}, u32[]{:S(2)}, u32[]{:S(2)}) async-start(bf16[8,128,256]{2,1,0:T(8,128)(2,1)} %project.1), calls=%async_computation | async-start | bytes 1048576 | tf_op jit(solution)/shard_map/all_to_all | solution.py:992
  43.2 31.6 %collective-permute-start = (bf16[256,1024]{1,0:T(8,128)(2,1)}, bf16[256,1024]{1,0:T(8,128)(2,1)}, u32[]{:S(2)}, u32[]{:S(2)}) collective-permute-start(bf16[256,1024]{1,0:T(8,128)(2,1)} %bitcast.6.x.refs_1_), channel_id=1, source_target_pairs={{0,4},{4,0},{8,12},{12,8},{16,20},{20,16},{24,28},{28,24},{1,5},{5... | collective-permute-start | bytes 1572872 | tf_op jit(solution)/shard_map/ppermute | solution.py:949
  43.6 31.2 %collective-permute-start.1 = (bf16[256,1024]{1,0:T(8,128)(2,1)}, bf16[256,1024]{1,0:T(8,128)(2,1)}, u32[]{:S(2)}, u32[]{:S(2)}) collective-permute-start(bf16[256,1024]{1,0:T(8,128)(2,1)} %bitcast.7.cot.refs_2_.refs_3_), channel_id=1, source_target_pairs={{0,4},{4,0},{8,12},{12,8},{16,20},{20,16},{24,28},{28,24},{1,5},{5... | collective-permute-start | bytes 1572872 | tf_op jit(solution)/shard_map/ppermute | solution.py:949
  44.1 18.4 %collective-permute-start.4 = (bf16[2,512,256]{2,1,0:T(8,128)(2,1)}, bf16[2,512,256]{2,1,0:T(8,128)(2,1)}, u32[]{:S(2)}, u32[]{:S(2)}) collective-permute-start(bf16[2,512,256]{2,1,0:T(8,128)(2,1)} %collective-permute-done.3.refs_6_), channel_id=1, source_target_pairs={{0,4},{4,0},{8,12},{12,8},{16,20},{20,16},{24,28},{28,24},{1,5},{5... | collective-permute-start | bytes 1572872 | tf_op jit(solution)/shard_map/ppermute | solution.py:949
  45.8 16.7 %collective-permute-start.6 = (bf16[2,512,256]{2,1,0:T(8,128)(2,1)}, bf16[2,512,256]{2,1,0:T(8,128)(2,1)}, u32[]{:S(2)}, u32[]{:S(2)}) collective-permute-start(bf16[2,512,256]{2,1,0:T(8,128)(2,1)} %collective-permute-done.5.refs_8_), channel_id=1, source_target_pairs={{0,4},{4,0},{8,12},{12,8},{16,20},{20,16},{24,28},{28,24},{1,5},{5... | collective-permute-start | bytes 1572872 | tf_op jit(solution)/shard_map/ppermute | solution.py:949
  58.8 14.8 %all-to-all-start.1 = ((bf16[8,128,256]{2,1,0:T(8,128)(2,1)}), bf16[8,128,256]{2,1,0:T(8,128)(2,1)S(1)}, u32[]{:S(2)}, u32[]{:S(2)}) async-start(bf16[8,128,256]{2,1,0:T(8,128)(2,1)} %bitcast.70), calls=%async_computation.1 | async-start | bytes 1048576 | tf_op jit(solution)/shard_map/all_to_all | solution.py:1004
  74.5 11.7 %collective-permute-start.16 = (bf16[2,256,256]{2,1,0:T(8,128)(2,1)S(1)}, bf16[2,256,256]{2,1,0:T(8,128)(2,1)S(1)}, u32[]{:S(2)}, u32[]{:S(2)}) collective-permute-start(bf16[2,256,256]{2,1,0:T(8,128)(2,1)S(1)} %get-tuple-element.70.refs_4_), channel_id=1, source_target_pairs={{0,4},{4,0},{8,12},{12,8},{16,20},{20,16},{24,28},{28,24},{1,5},{5... | collective-permute-start | bytes 786440 | tf_op jit(solution)/shard_map/ppermute | solution.py:949
  79.3 21.2 %collective-permute-start.11 = (bf16[2,512,256]{2,1,0:T(8,128)(2,1)S(1)}, bf16[2,512,256]{2,1,0:T(8,128)(2,1)S(1)}, u32[]{:S(2)}, u32[]{:S(2)}) collective-permute-start(bf16[2,512,256]{2,1,0:T(8,128)(2,1)S(1)} %get-tuple-element.66), channel_id=1, source_target_pairs={{0,16},{4,20},{8,24},{12,28},{16,0},{20,4},{24,8},{28,12},{1,17},{... | collective-permute-start | bytes 1572872 | tf_op jit(solution)/shard_map/ppermute | solution.py:949
  81.1 19.4 %collective-permute-start.12 = (bf16[2,512,256]{2,1,0:T(8,128)(2,1)S(1)}, bf16[2,512,256]{2,1,0:T(8,128)(2,1)S(1)}, u32[]{:S(2)}, u32[]{:S(2)}) collective-permute-start(bf16[2,512,256]{2,1,0:T(8,128)(2,1)S(1)} %get-tuple-element.67), channel_id=1, source_target_pairs={{0,8},{4,12},{8,0},{12,4},{16,24},{20,28},{24,16},{28,20},{1,9},{5... | collective-permute-start | bytes 1572872 | tf_op jit(solution)/shard_map/ppermute | solution.py:949
  82.5 23.2 %collective-permute-start.13 = (bf16[2,512,256]{2,1,0:T(8,128)(2,1)S(1)}, bf16[2,512,256]{2,1,0:T(8,128)(2,1)S(1)}, u32[]{:S(2)}, u32[]{:S(2)}) collective-permute-start(bf16[2,512,256]{2,1,0:T(8,128)(2,1)S(1)} %get-tuple-element.68), channel_id=1, source_target_pairs={{0,24},{4,28},{8,16},{12,20},{16,8},{20,12},{24,0},{28,4},{1,25},{... | collective-permute-start | bytes 1572872 | tf_op jit(solution)/shard_map/ppermute | solution.py:949
  87.8 12.7 %collective-permute-start.15 = (bf16[2,64,1024]{2,1,0:T(8,128)(2,1)S(1)}, bf16[2,64,1024]{2,1,0:T(8,128)(2,1)S(1)}, u32[]{:S(2)}, u32[]{:S(2)}) collective-permute-start(bf16[2,64,1024]{2,1,0:T(8,128)(2,1)S(1)} %get-tuple-element.78), channel_id=1, source_target_pairs={{0,1},{1,0},{2,3},{3,2},{4,5},{5,4},{6,7},{7,6},{8,9},{9,8},{10,11... | collective-permute-start | bytes 786440 | tf_op jit(solution)/shard_map/ppermute | solution.py:952
  108.6 17.4 %collective-permute-start.19 = (bf16[2,64,1024]{2,1,0:T(8,128)(2,1)S(1)}, bf16[2,64,1024]{2,1,0:T(8,128)(2,1)S(1)}, u32[]{:S(2)}, u32[]{:S(2)}) collective-permute-start(bf16[2,64,1024]{2,1,0:T(8,128)(2,1)S(1)} %get-tuple-element.83), channel_id=1, source_target_pairs={{0,2},{1,3},{2,0},{3,1},{4,6},{5,7},{6,4},{7,5},{8,10},{9,11},{10,... | collective-permute-start | bytes 786440 | tf_op jit(solution)/shard_map/ppermute | solution.py:952
  111.3 13.0 %collective-permute-start.18 = (f32[2,4,64,64]{3,2,1,0:T(8,128)S(1)}, f32[2,4,64,64]{3,2,1,0:T(8,128)S(1)}, u32[]{:S(2)}, u32[]{:S(2)}) collective-permute-start(f32[2,4,64,64]{3,2,1,0:T(8,128)S(1)} %get-tuple-element.81.mine), channel_id=1, source_target_pairs={{0,16},{4,20},{8,24},{12,28},{16,0},{20,4},{24,8},{28,12},{1,17},{... | collective-permute-start | bytes 393224 | tf_op jit(solution)/shard_map/ppermute | solution.py:949
  124.0 13.2 %collective-permute-start.28 = (bf16[1,512,256]{2,1,0:T(8,128)(2,1)S(1)}, bf16[1,512,256]{2,1,0:T(8,128)(2,1)S(1)}, u32[]{:S(2)}, u32[]{:S(2)}) collective-permute-start(bf16[1,512,256]{2,1,0:T(8,128)(2,1)S(1)} %get-tuple-element.90), channel_id=1, source_target_pairs={{0,24},{4,28},{8,16},{12,20},{16,8},{20,12},{24,0},{28,4},{1,25},{... | collective-permute-start | bytes 786440 | tf_op jit(solution)/shard_map/ppermute | solution.py:949
  124.3 21.4 %collective-permute-start.36 = (bf16[2,512,256]{2,1,0:T(8,128)(2,1)S(1)}, bf16[2,512,256]{2,1,0:T(8,128)(2,1)S(1)}, u32[]{:S(2)}, u32[]{:S(2)}) collective-permute-start(bf16[2,512,256]{2,1,0:T(8,128)(2,1)S(1)} %get-tuple-element.96.g0), channel_id=1, source_target_pairs={{0,8},{4,12},{8,0},{12,4},{16,24},{20,28},{24,16},{28,20},{1,9},{5... | collective-permute-start | bytes 1572872 | tf_op jit(solution)/shard_map/ppermute | solution.py:949
  130.0 15.8 %collective-permute-start.24 = (bf16[2,64,1024]{2,1,0:T(8,128)(2,1)S(1)}, bf16[2,64,1024]{2,1,0:T(8,128)(2,1)S(1)}, u32[]{:S(2)}, u32[]{:S(2)}) collective-permute-start(bf16[2,64,1024]{2,1,0:T(8,128)(2,1)S(1)} %get-tuple-element.85.r0), channel_id=1, source_target_pairs={{0,2},{1,3},{2,0},{3,1},{4,6},{5,7},{6,4},{7,5},{8,10},{9,11},{10,... | collective-permute-start | bytes 786440 | tf_op jit(solution)/shard_map/ppermute | solution.py:952
  132.0 26.3 %collective-permute-start.35 = (bf16[2,512,256]{2,1,0:T(8,128)(2,1)S(1)}, bf16[2,512,256]{2,1,0:T(8,128)(2,1)S(1)}, u32[]{:S(2)}, u32[]{:S(2)}) collective-permute-start(bf16[2,512,256]{2,1,0:T(8,128)(2,1)S(1)} %get-tuple-element.96.g0), channel_id=1, source_target_pairs={{0,4},{4,0},{8,12},{12,8},{16,20},{20,16},{24,28},{28,24},{1,5},{5... | collective-permute-start | bytes 1572872 | tf_op jit(solution)/shard_map/ppermute | solution.py:949
  137.1 13.2 %collective-permute-start.23 = (bf16[2,64,1024]{2,1,0:T(8,128)(2,1)S(1)}, bf16[2,64,1024]{2,1,0:T(8,128)(2,1)S(1)}, u32[]{:S(2)}, u32[]{:S(2)}) collective-permute-start(bf16[2,64,1024]{2,1,0:T(8,128)(2,1)S(1)} %get-tuple-element.85.r0), channel_id=1, source_target_pairs={{0,1},{1,0},{2,3},{3,2},{4,5},{5,4},{6,7},{7,6},{8,9},{9,8},{10,11... | collective-permute-start | bytes 786440 | tf_op jit(solution)/shard_map/ppermute | solution.py:952
  145.7 12.9 %collective-permute-start.37 = (bf16[2,512,256]{2,1,0:T(8,128)(2,1)S(1)}, bf16[2,512,256]{2,1,0:T(8,128)(2,1)S(1)}, u32[]{:S(2)}, u32[]{:S(2)}) collective-permute-start(bf16[2,512,256]{2,1,0:T(8,128)(2,1)S(1)} %collective-permute-done.36.g2), channel_id=1, source_target_pairs={{0,4},{4,0},{8,12},{12,8},{16,20},{20,16},{24,28},{28,24},{1,5},{5... | collective-permute-start | bytes 1572872 | tf_op jit(solution)/shard_map/ppermute | solution.py:949
  157.2 24.0 %collective-permute-start.30 = (bf16[1,512,256]{2,1,0:T(8,128)(2,1)S(1)}, bf16[1,512,256]{2,1,0:T(8,128)(2,1)S(1)}, u32[]{:S(2)}, u32[]{:S(2)}) collective-permute-start(bf16[1,512,256]{2,1,0:T(8,128)(2,1)S(1)} %get-tuple-element.93.g0), channel_id=1, source_target_pairs={{0,4},{4,0},{8,12},{12,8},{16,20},{20,16},{24,28},{28,24},{1,5},{5... | collective-permute-start | bytes 786440 | tf_op jit(solution)/shard_map/ppermute | solution.py:949
  157.7 11.4 %collective-permute-start.33 = (f32[1,4,64,64]{3,2,1,0:T(8,128)S(1)}, f32[1,4,64,64]{3,2,1,0:T(8,128)S(1)}, u32[]{:S(2)}, u32[]{:S(2)}) collective-permute-start(f32[1,4,64,64]{3,2,1,0:T(8,128)S(1)} %get-tuple-element.94.refs_0_), channel_id=1, source_target_pairs={{0,16},{4,20},{8,24},{12,28},{16,0},{20,4},{24,8},{28,12},{1,17},{... | collective-permute-start | bytes 196616 | tf_op jit(solution)/shard_map/ppermute | solution.py:949
  158.7 22.5 %collective-permute-start.32 = (bf16[1,512,256]{2,1,0:T(8,128)(2,1)S(1)}, bf16[1,512,256]{2,1,0:T(8,128)(2,1)S(1)}, u32[]{:S(2)}, u32[]{:S(2)}) collective-permute-start(bf16[1,512,256]{2,1,0:T(8,128)(2,1)S(1)} %collective-permute-done.31.g2), channel_id=1, source_target_pairs={{0,4},{4,0},{8,12},{12,8},{16,20},{20,16},{24,28},{28,24},{1,5},{5... | collective-permute-start | bytes 786440 | tf_op jit(solution)/shard_map/ppermute | solution.py:949
  (58 other events, 465.4 us)

commit v4 on v3

--- a/solution.py
+++ b/solution.py
@@ -446,6 +446,18 @@
     )
 
 
+def in_hbm(array):
+    if array.size * array.dtype.itemsize < 1 << 20:
+        return array
+    return pltpu.with_memory_space_constraint(array, pltpu.HBM)
+
+
+def out_hbm(shape):
+    if shape.size * shape.dtype.itemsize < 1 << 20:
+        return shape
+    return pltpu.HBM(shape.shape, shape.dtype)
+
+
 def full(array):
     return pl.BlockSpec(array.shape, lambda *_: (0,) * array.ndim)
 
@@ -463,12 +475,12 @@
     return pl.pallas_call(
         body,
         in_specs=list(specs) + [corner(a) for a in after],
-        out_shape=out_shapes,
+        out_shape=jax.tree.map(out_hbm, out_shapes),
         compiler_params=limits(vmem),
         cost_estimate=takes(cost),
         name=name,
         **more,
-    )(*operands, *after)
+    )(*map(in_hbm, operands), *map(in_hbm, after))
 
 
 def relayout_kernel(n, head, scal, src, out, *refs):
@@ -518,7 +530,11 @@
         values = [part[...].astype(jnp.float32) for part in parts]
         while len(values) > 1:
             values = [sum(values[i : i + 2]) for i in range(0, len(values), 2)]
-        target[...] = values[0].astype(target.dtype)
+        if isinstance(target, list):
+            for i, part in enumerate(target):
+                part[...] = values[0][i].astype(part.dtype)
+        else:
+            target[...] = values[0].astype(target.dtype)
 
 
 def grouped(refs, counts, targets):
@@ -656,13 +672,23 @@
     return list(zip(halves(h, first), halves(c, first)))
 
 
-def unit_grads_kernel(scal, x, x_beside, cot, cot_beside, norms, keep, came, *outs):
+def unit_grads_kernel(
+    scal, x, x_beside, cot, cot_beside, norms, keep, came, in_keep, in_send, down_keep, down_send
+):
     for side, (h, c) in enumerate(both_cores(scal, x, x_beside, cot, cot_beside, norms, 2)):
         for far in range(2):
             grad = jnp.concatenate([keep[far, 0], came[far, 0]], axis=0)
             act = jnp.concatenate([keep[far, 1], came[far, 1]], axis=0)
-            outs[2 * far + side][0] = dot(h, grad, TN).astype(jnp.bfloat16)
-            outs[2 * far + side][1] = dot(c, act, TN).astype(jnp.bfloat16)
+            (in_send if side else in_keep)[far] = dot(h, grad, TN).astype(jnp.bfloat16)
+            (down_send if far else down_keep)[side] = dot(c, act, TN).astype(jnp.bfloat16)
+
+
+def combine_kernel(in_keep, in_came, down_keep, down_came, own, in_send, down_send):
+    pairs = ((in_keep, in_came, in_send), (down_keep, down_came, down_send))
+    for k, (keep, came, send) in enumerate(pairs):
+        total = keep[...].astype(jnp.float32) + came[...].astype(jnp.float32)
+        own[k] = total[0].astype(jnp.bfloat16)
+        send[0] = total[1].astype(jnp.bfloat16)
 
 
 def turn_kernel(scal, cosine, sine, back, keep, send, sums):
@@ -693,19 +719,24 @@
 def head_grads_kernel(
     scal, x, x_beside, cot, cot_beside, norms, keep, came, totals, totals_came, *outs
 ):
-    add_up([((totals, totals_came), outs[4])])
+    both = (totals[...] + totals_came[...]).reshape(64, 256)
+    coarse = both.astype(jnp.bfloat16)
+    fine = (both - coarse.astype(jnp.float32)).astype(jnp.bfloat16)
     sides = both_cores(scal, x, x_beside, cot, cot_beside, norms, 0)
     for far in range(2):
         piece = jnp.concatenate([keep[far], came[far]], axis=0)
         pre_grad, attended = split_last(piece)
         for side, (h, c) in enumerate(sides):
             grad = dot(h, pre_grad, TN) + dot(c, attended, TN)
-            outs[2 * far + side][0] = grad.astype(jnp.bfloat16)
+            target = outs[2 * far + side]
+            target[0:512] = grad.astype(jnp.bfloat16)
+            target[512:576] = coarse
+            target[576:640] = fine
 
 
 def gather_kernel(
     scal, x, norms, keep, send, weights, r0, r1, r2, r3, ff_branch, ff_part,
-    norm_two, cot_sums, unit_sums, qkv_sums, z0, z1, z2, z3, totals, parts,
+    norm_two, cot_sums, unit_sums, qkv_sums, near, far, totals, parts,
 ):
     first = scal[0] == 0
     hat, root = normalized(x[...].astype(jnp.float32))
@@ -733,7 +764,7 @@
         parts[q, 0] = branch[64 * q : 64 * q + 64].astype(jnp.bfloat16)
         parts[q, 1] = input_part[64 * q : 64 * q + 64].astype(jnp.bfloat16)
     for r in range(4):
-        (z0, z1, z2, z3)[r][...] = parts[scal[2] ^ r]
+        (far if r % 2 else near)[r // 2] = parts[scal[2] ^ r]
 
 
 def finish_rows_kernel(scal, x, cot, bias, r0, r1, r2, r3, block_output, input_grad):
@@ -743,51 +774,64 @@
         input_grad[q] = cot[q].astype(jnp.float32) + piece[1].astype(jnp.float32)
 
 
-def gram_kernel(counts, place, own, a, b, c, momenta, *refs):
-    sums = len(counts)
-    grads, grams = refs[-2 - sums], refs[-1 - sums]
-
-    @pl.when(pl.program_id(0) == 0)
-    def _():
-        add_up(grouped(refs, counts, refs[len(refs) - sums :]))
-
-    total = own[...].astype(jnp.float32) + a[...].astype(jnp.float32)
-    total = total + b[...].astype(jnp.float32) + c[...].astype(jnp.float32)
+def gram_of_piece(total, momenta, grads, grams):
     short = total.astype(jnp.bfloat16)
-    grads[...] = short
-    update = 1.95 * short[0].astype(jnp.float32) + 0.9025 * momenta[0]
+    grads[0] = short
+    update = 1.95 * short.astype(jnp.float32) + 0.9025 * momenta[0]
     gram = dot(update, update, TN, lax.Precision.HIGHEST)
     for j in range(4):
         cut = slice(j * HD, (j + 1) * HD)
         grams[0, j] = gram[cut, cut]
 
 
-def gram_of(own, a, b, c, momenta, place, sums, after=()):
-    chunks = own.shape[0]
+def unit_gram_kernel(place, own, in_came, down_came, momenta, near, came, *refs):
+    grads, grams, first, second = refs[-4:]
+
+    @pl.when(pl.program_id(0) == 0)
+    def _():
+        add_up([((near, came), [first, second])])
+
+    a = in_came[0].astype(jnp.float32)
+    b = down_came[0].astype(jnp.float32)
+    other = jnp.where(pl.program_id(0) == 0, a, b)
+    gram_of_piece(own[0].astype(jnp.float32) + other, momenta, grads, grams)
+
+
+def head_gram_kernel(place, own, a, b, c, momenta, *refs):
+    grads, grams, totals = refs[-3:]
+    values = [part[...].astype(jnp.float32) for part in (own, a, b, c)]
+    total = (values[0] + values[1]) + (values[2] + values[3])
+    gram_of_piece(total[0:512], momenta, grads, grams)
+    sums = [v[512:576] + v[576:640] for v in values]
+    totals[...] = ((sums[0] + sums[1]) + (sums[2] + sums[3])).reshape(8, 8, 256)
+
+
+def gram_of(kernel, first, others, momenta, place, more, shapes, after=()):
+    chunks = momenta.shape[0] // 4
     piece = pl.BlockSpec((1, 512, 256), lambda i, s: (i, 0, 0))
-    flat = [part for group in sums for part in group]
-    targets = [jax.ShapeDtypeStruct(group[0].shape, group[0].dtype) for group in sums]
+    block = pl.BlockSpec((1, 512, 256), lambda i, s: (4 * i + s[1], 0, 0))
     return pl.pallas_call(
-        functools.partial(gram_kernel, [len(group) for group in sums]),
+        kernel,
         grid_spec=pltpu.PrefetchScalarGridSpec(
             num_scalar_prefetch=1,
             grid=(chunks,),
-            in_specs=[piece] * 4
-            + [pl.BlockSpec((1, 512, 256), lambda i, s: (4 * i + s[1], 0, 0))]
-            + [full(part) for part in flat]
+            in_specs=[piece if first.ndim == 3 else full(first)]
+            + [full(other) for other in others]
+            + [block]
+            + [full(part) for part in more]
             + [corner(a) for a in after],
             out_specs=[piece, pl.BlockSpec((1, 4, HD, HD), lambda i, s: (i, 0, 0, 0))]
-            + [full(target) for target in targets],
+            + [full(shape) for shape in shapes],
         ),
         out_shape=[
             jax.ShapeDtypeStruct((chunks, 512, 256), jnp.bfloat16),
             jax.ShapeDtypeStruct((chunks, 4, HD, HD), jnp.float32),
-            *targets,
+            *map(out_hbm, shapes),
         ],
         compiler_params=limits(20),
         cost_estimate=takes(2.5),
         name="gram",
-    )(place, own, a, b, c, momenta, *flat, *after)
+    )(place, *map(in_hbm, [first, *others, momenta, *more, *after]))
 
 
 def newton_kernel(counts, mine, theirs, *refs):
@@ -973,12 +1017,12 @@
     head_weights, mine = relayout(scal, matrices, bf16, 0, 1, mine=True)
     first_hop = hop(mine, 4)
     other_heads = spread(first_hop)
-    (piled_heads,) = relayout(scal, momenta, f32, 0, 1, after=(mine,))
-    (piled_units,) = relayout(scal, momenta, f32, 1, 2, after=(mine,))
-    unit_weights, mine = relayout(
-        scal, matrices, bf16, 1, 2, mine=True, after=(first_hop, piled_heads, piled_units, cosine, sine)
-    )
-    other_units = spread(hop(mine, 4))
+    unit_weights, mine_units = relayout(scal, matrices, bf16, 1, 2, mine=True, after=(mine,))
+    (piled_heads,) = relayout(scal, momenta, f32, 0, 1, after=(mine_units,))
+    first_hop, mine_units, cosine, sine, _ = lax.optimization_barrier(
+        (first_hop, mine_units, cosine, sine, piled_heads)
+    )
+    other_units = spread(hop(mine_units, 4))
     x_beside = hop(x, 1)
     cot_beside = hop(cot, 1)
 
@@ -990,6 +1034,7 @@
         "project",
     )
     arrived = lax.all_to_all(send, both, split_axis=0, concat_axis=0, tiled=True)
+    (piled_units,) = relayout(scal, momenta, f32, 1, 2, after=(send,))
     documents = lax.dynamic_index_in_dim(segments, blk_at, 0, keepdims=False)
     length = documents.shape[0]
     attended = launch(
@@ -1029,7 +1074,7 @@
         cost=2,
         after=(unit_sums,),
     )
-    unit_grads = launch(
+    in_keep, in_send, down_keep, down_send = launch(
         unit_grads_kernel,
         [scal, x, x_beside, cot, cot_beside, norms, unit_keep, hop(unit_send, 1)],
         [shaped((2, 512, 256), bf16)] * 4,
@@ -1038,48 +1083,58 @@
         after=(qkv_sums,),
     )
     sums = [norm_two, cot_sums, unit_sums, qkv_sums]
-    *quarters, totals = launch(
+    near, far, totals = launch(
         gather_kernel,
         [scal, x, norms, head_keep, head_send, head_weights, *other_heads, ff_branch, ff_part, *sums],
-        [shaped((2, 64, width), bf16)] * 4 + [shaped((7, 8, 256), f32)],
+        [shaped((2, 2, 64, width), bf16)] * 2 + [shaped((8, 8, 256), f32)],
         "gather",
-        after=(unit_grads[0],),
+        after=(in_keep,),
         scratch_shapes=[pltpu.VMEM((4, 2, 64, width), bf16)],
     )
-    *head_grads, totals = launch(
+    head_grads = launch(
         head_grads_kernel,
         [scal, x, x_beside, cot, cot_beside, norms, head_keep, hop(head_send, 1), totals, hop(totals, 1)],
-        [shaped((1, 512, 256), bf16)] * 4 + [shaped((7, 8, 256), f32)],
+        [shaped((640, 256), bf16)] * 4,
         "head_grads",
         cost=4,
     )
-
-    def reduced(grads):
-        return grads[0], hop(grads[1], 4), hop(grads[2], 2), hop(grads[3], 6)
-
-    unit_reduced = reduced(unit_grads)
-    head_reduced = reduced(head_grads)
-    spread_totals = [totals, hop(totals, 4), hop(totals, 2), hop(totals, 6)]
-    unit_sum, unit_grams, near, far = gram_of(
-        *unit_reduced,
+    operands = [in_keep, hop(in_send, 4), down_keep, hop(down_send, 2)]
+    own, in_send, down_send = launch(
+        combine_kernel,
+        operands,
+        [shaped((2, 512, 256), bf16)] + [shaped((1, 512, 256), bf16)] * 2,
+        "combine",
+        specs=[full(a) for a in operands],
+        cost=2,
+        after=(head_grads[0],),
+    )
+    unit_sum, unit_grams, kept, passed = gram_of(
+        unit_gram_kernel,
+        own,
+        [hop(in_send, 2), hop(down_send, 4)],
         piled_units,
         scal,
-        [(quarters[0], hop_tp(quarters[1], 1)), (quarters[2], hop_tp(quarters[3], 1))],
-        after=(head_grads[0],),
+        [near, hop_tp(far, 1)],
+        [shaped((2, 64, width), bf16)] * 2,
     )
     unit_pieces = spread(unit_sum)
-    unit_mix, total, totals = newton(
-        unit_grams, hop(unit_grams, 4), [(near, hop_tp(far, 2)), spread_totals]
-    )
+    unit_mix, total = newton(unit_grams, hop(unit_grams, 4), [(kept, hop_tp(passed, 2))])
     head_sum, head_grams, totals = gram_of(
-        *head_reduced, piled_heads, scal, [(totals, hop_tp(totals, 1))], after=(unit_mix,)
+        head_gram_kernel,
+        head_grads[0],
+        [hop(head_grads[1], 4), hop(head_grads[2], 2), hop(head_grads[3], 6)],
+        piled_heads,
+        scal,
+        [],
+        [shaped((8, 8, 256), f32)],
     )
     head_pieces = spread(head_sum)
+    head_mix, totals = newton(
+        head_grams, hop(head_grams, 4), [(totals, hop_tp(totals, 1))], after=(unit_mix,)
+    )
     before = update(1, scal, unit_pieces, spread(unit_mix), piled_units, momenta, matrices)
-    head_mix, totals = newton(
-        head_grams, hop(head_grams, 4), [(totals, hop_tp(totals, 2))], after=(before[0],)
-    )
     outs = update(0, scal, head_pieces, spread(head_mix), piled_heads, momenta, matrices, before)
+    totals = totals + hop_tp(totals, 2)
 
     beside = hop_tp(total, 2)
     block_output, input_grad = launch(
@@ -1105,8 +1160,8 @@
             totals[:2].reshape(-1),
             cot_total,
             cot_total,
-            totals[3:, :4, : 3 * HD].reshape(-1),
-            totals[3:, 4:].reshape(-1),
+            totals[3:7, :4, : 3 * HD].reshape(-1),
+            totals[3:7, 4:].reshape(-1),
         ]
     )
     return (

time: 194 us -> 195 us (level)
  Pallas kernels: 66.2 us -> 87.9 us
  local copies, waits for them, and re-layouts: 21.5 us -> 4.45 us
  starting transfers between devices: 47.3 us -> 43.9 us
    pallas_call x16 -> x17, Pallas kernels: 61.9 us -> 81.5 us  [launch(): pl.pallas_call(body, in_specs=list(specs) + [corner(a) for a in after], o...]
    unnamed x79 -> x41, local copies, waits for them, and re-layouts: 21 us -> 3.34 us
    ppermute x36 -> x34, starting transfers between devices: 29.2 us -> 22.5 us  [hop(): return lax.ppermute(values, both, [(i, i ^ by) for i in range(8)])]
    ppermute x36 -> x34, waiting for transfers between devices: 35.1 us -> 30.3 us  [hop(): return lax.ppermute(values, both, [(i, i ^ by) for i in range(8)])]
    ppermute x8 -> x7, waiting for transfers between devices: 12.1 us -> 16.9 us  [hop_tp(): return lax.ppermute(values, 'tp', [(i, i ^ by) for i in range(4)])]
    ppermute x8 -> x7, starting transfers between devices: 11 us -> 14.2 us  [hop_tp(): return lax.ppermute(values, 'tp', [(i, i ^ by) for i in range(4)])]
    all_to_all x1, waiting for transfers between devices: 7.1 us -> 5 us  [whole_device(): lax.all_to_all(send, both, split_axis=0, concat_axis=0, tiled=True)]
    pallas_call x2, Pallas kernels: 4.28 us -> 6.37 us  [gram_of(): pl.pallas_call(kernel, grid_spec=pltpu.PrefetchScalarGridSpec(num_scalar_...]
  transfers between devices with their start and end apart: 46 -> 43, of which waited for: 14 -> 13; matrix products, arithmetic and copies ran while one was open for 1% -> 3% of each run, Pallas kernels for 27% -> 38%
where the time goes in v4:
time: 195 us; the launch traced here: 193 us
  Pallas kernels  87.9 us (45%)
  waiting for transfers between devices  53.9 us (28%)
  starting transfers between devices  43.9 us (23%)
  local copies, waits for them, and re-layouts  4.45 us (2%)
  other arithmetic  2.19 us (1%)
    pallas_call x17, Pallas kernels, launch(): pl.pallas_call(body, in_specs=list(specs) + [corner(a) for a in after], o...  81.5 us
    ppermute x34, waiting for transfers between devices, hop(): return lax.ppermute(values, both, [(i, i ^ by) for i in range(8)])  30.3 us
    ppermute x34, starting transfers between devices, hop(): return lax.ppermute(values, both, [(i, i ^ by) for i in range(8)])  22.5 us
    ppermute x7, waiting for transfers between devices, hop_tp(): return lax.ppermute(values, 'tp', [(i, i ^ by) for i in range(4)])  16.9 us
    ppermute x7, starting transfers between devices, hop_tp(): return lax.ppermute(values, 'tp', [(i, i ^ by) for i in range(4)])  14.2 us
    pallas_call x2, Pallas kernels, gram_of(): pl.pallas_call(kernel, grid_spec=pltpu.PrefetchScalarGridSpec(num_scalar_...  6.37 us
    all_to_all x1, waiting for transfers between devices, whole_device(): lax.all_to_all(send, both, split_axis=0, concat_axis=0, tiled=True)  5 us
  transfers between devices with their start and end apart: 43, of which 13 were waited for; matrix products, arithmetic and copies ran while one was open for 3% of the time, Pallas kernels for 38%

profile of v4, /device:TPU:0, one launch (start us, length us, event | category | flops | bytes accessed | tf_op | source)
XLA Modules:
  0.0 193.4 jit_solution(5586095740019507209)
XLA Ops:
  0.7 4.0 %relayout.4 = (bf16[4,512,256]{2,1,0:T(8,128)(2,1)}, bf16[1,512,256]{2,1,0:T(8,128)(2,1)S(1)}) custom-call(s32[3]{0:T(128)S(1)} %pad_add_fusion.scal.refs_0_.place, f32[6,2048,128]{2,1,0:T(8,128)} %bitcast.73), custom_call_target="tpu_custom_call" | custom-call | flops 1495000064 | bytes 1000000 | tf_op jit(solution)/shard_map/relayout/pallas_call | solution.py:475
  7.7 6.9 %relayout.5 = (bf16[8,512,256]{2,1,0:T(8,128)(2,1)}, bf16[2,512,256]{2,1,0:T(8,128)(2,1)S(1)}) custom-call(s32[3]{0:T(128)S(1)} %pad_add_fusion.scal.refs_0_.place, f32[6,2048,128]{2,1,0:T(8,128)} %bitcast.74, bf16[1,512,256]{2,1,0:T(8,128)(2,1)S(1)} %get-tuple-element.59.refs_2_), custom_call_target="tpu_custom_call" | custom-call | flops 2990000128 | bytes 1000000 | tf_op jit(solution)/shard_map/relayout/pallas_call | solution.py:475
  14.7 4.3 %relayout.6.momenta = f32[4,512,256]{2,1,0:T(8,128)} custom-call(s32[3]{0:T(128)S(1)} %pad_add_fusion.scal.refs_0_.place, f32[6,2048,128]{2,1,0:T(8,128)} %bitcast.77, bf16[2,512,256]{2,1,0:T(8,128)(2,1)S(1)} %get-tuple-element.62.refs_2_), custom_call_target="tpu_custom_call" | custom-call | flops 1495000064 | bytes 1000000 | tf_op jit(solution)/shard_map/relayout/pallas_call | solution.py:475
  21.7 5.8 %collective-permute-done.8.refs_8_ = bf16[1,512,256]{2,1,0:T(8,128)(2,1)S(1)} collective-permute-done((bf16[1,512,256]{2,1,0:T(8,128)(2,1)S(1)}, bf16[1,512,256]{2,1,0:T(8,128)(2,1)S(1)}, u32[]{:S(2)}, u32[]{:S(2)}) %collective-permute-start.8) | collective-permute-done | bytes 262176 | tf_op jit(solution)/shard_map/ppermute | solution.py:993
  27.7 5.4 %collective-permute-done.3.refs_6_ = bf16[2,512,256]{2,1,0:T(8,128)(2,1)} collective-permute-done((bf16[2,512,256]{2,1,0:T(8,128)(2,1)S(1)}, bf16[2,512,256]{2,1,0:T(8,128)(2,1)}, u32[]{:S(2)}, u32[]{:S(2)}) %collective-permute-start.3) | collective-permute-done | bytes 524320 | tf_op jit(solution)/shard_map/ppermute | solution.py:993
  34.7 3.8 %project.1.refs_2_ = bf16[8,128,256]{2,1,0:T(8,128)(2,1)} custom-call(s32[3]{0:T(128)S(1)} %pad_add_fusion.scal.refs_0_.place, bf16[256,1024]{1,0:T(8,128)(2,1)S(1)} %bitcast.56, bf16[256,1024]{1,0:T(8,128)(2,1)S(1)} %bitcast.63, f32[4,1024]{1,0:T(4,128)S(1)} %slice.34.norms.refs_3_.refs_5_.refs_2_, f32[4,256]{1,0:T(4,128)S(1)} %pad.4.bias, ...), custom_call_target="tpu_custom_call" | custom-call | flops 3449999872 | bytes 1000000 | tf_op jit(solution)/shard_map/project/pallas_call | solution.py:475
  38.6 3.5 %all-to-all-start = ((bf16[8,128,256]{2,1,0:T(8,128)(2,1)}), bf16[8,128,256]{2,1,0:T(8,128)(2,1)S(1)}, u32[]{:S(2)}, u32[]{:S(2)}) async-start(bf16[8,128,256]{2,1,0:T(8,128)(2,1)} %project.1.refs_2_), calls=%async_computation | async-start | bytes 1048576 | tf_op jit(solution)/shard_map/all_to_all | solution.py:1036
  43.3 3.4 %collective-permute-done.5.refs_8_ = bf16[2,512,256]{2,1,0:T(8,128)(2,1)} collective-permute-done((bf16[2,512,256]{2,1,0:T(8,128)(2,1)}, bf16[2,512,256]{2,1,0:T(8,128)(2,1)}, u32[]{:S(2)}, u32[]{:S(2)}) %collective-permute-start.5) | collective-permute-done | bytes 524320 | tf_op jit(solution)/shard_map/ppermute | solution.py:993
  46.8 5.0 %all-to-all-done = bf16[8,128,256]{2,1,0:T(8,128)(2,1)S(1)} async-done(((bf16[8,128,256]{2,1,0:T(8,128)(2,1)}), bf16[8,128,256]{2,1,0:T(8,128)(2,1)S(1)}, u32[]{:S(2)}, u32[]{:S(2)}) %all-to-all-start) | async-done | bytes 524320 | tf_op jit(solution)/shard_map/all_to_all | solution.py:1036
  51.8 6.0 %attention.1.refs_10_ = bf16[1024,256]{1,0:T(8,128)(2,1)} custom-call(bf16[1024,256]{1,0:T(8,128)(2,1)S(1)} %bitcast.54, s32[1024,1]{1,0:T(8,128)S(1)} %copy.21.seg), custom_call_target="tpu_custom_call" | custom-call | flops 6899999744 | bytes 1000000 | tf_op jit(solution)/shard_map/attention/pallas_call | solution.py:475
  57.7 3.7 %all-to-all-start.1 = ((bf16[8,128,256]{2,1,0:T(8,128)(2,1)}), bf16[8,128,256]{2,1,0:T(8,128)(2,1)S(1)}, u32[]{:S(2)}, u32[]{:S(2)}) async-start(bf16[8,128,256]{2,1,0:T(8,128)(2,1)} %bitcast.23), calls=%async_computation.1 | async-start | bytes 1048576 | tf_op jit(solution)/shard_map/all_to_all | solution.py:1049
  61.4 6.7 %feed_forward.1 = (f32[256,1024]{1,0:T(8,128)}, f32[256,1024]{1,0:T(8,128)}, bf16[2,2,256,256]{3,2,1,0:T(8,128)(2,1)S(1)}, bf16[2,2,256,256]{3,2,1,0:T(8,128)(2,...) custom-call(s32[3]{0:T(128)S(1)} %pad_add_fusion.scal.refs_0_.place, ...), custom_call_target="tpu_custom_call" | custom-call | flops 6325000192 | bytes 1000000 | tf_op jit(solution)/shard_map/feed_forward/pallas_call | solution.py:475
  77.4 3.9 %gather.1 = (bf16[2,2,64,1024]{3,2,1,0:T(8,128)(2,1)S(1)}, bf16[2,2,64,1024]{3,2,1,0:T(8,128)(2,1)S(1)}, f32[8,8,256]{2,1,0:T(8,128)S(1)}) custom-call(s32[3]{0:T(128)S(1)} %pad_add_fusion.scal.refs_0_.place, bf16[256,1024]{1,0:T(8,128)(2,1)S(1)} %bitcast.60, f32[4,1024]{1,0:T(4,128)S(1)} %slice.34.norms.refs_3_.refs_5_.refs_2_, ...), custom_call_target="tpu_custom_call" | custom-call | flops 3449999872 | bytes 1000000 | tf_op jit(solution)/shard_map/gather/pallas_call | solution.py:475
  96.2 7.4 %relayout.7.momenta = f32[8,512,256]{2,1,0:T(8,128)} custom-call(s32[3]{0:T(128)S(1)} %pad_add_fusion.scal.refs_0_.place, f32[6,2048,128]{2,1,0:T(8,128)} %bitcast.78, bf16[8,128,256]{2,1,0:T(8,128)(2,1)} %project.1.refs_2_), custom_call_target="tpu_custom_call" | custom-call | flops 2990000128 | bytes 1000000 | tf_op jit(solution)/shard_map/relayout/pallas_call | solution.py:475
  103.7 5.7 %collective-permute-done.15.in_came = bf16[1,512,256]{2,1,0:T(8,128)(2,1)S(1)} collective-permute-done((bf16[1,512,256]{2,1,0:T(8,128)(2,1)S(1)}, bf16[1,512,256]{2,1,0:T(8,128)(2,1)S(1)}, u32[]{:S(2)}, u32[]{:S(2)}) %collective-permute-start.15) | collective-permute-done | bytes 262176 | tf_op jit(solution)/shard_map/ppermute | solution.py:993
  110.1 3.8 %gram.2 = (bf16[2,512,256]{2,1,0:T(8,128)(2,1)S(1)}, f32[2,4,64,64]{3,2,1,0:T(8,128)S(1)}, bf16[2,64,1024]{2,1,0:T(8,128)(2,1)S(1)}, bf16[2,64,1024]{2,1,0:T(8,128)(2,1)S(1)}) custom-call(s32[3]{0:T(128)S(1)} %pad_add_fusion.scal.refs_0_.place, bf16[2,512,256]{2,1,0:T(8,128)(2,1)S(1)} %get-tuple-element.82.own, ...), custom_call_target="tpu_custom_call" | custom-call | flops 2875000064 | bytes 1000000 | tf_op jit(solution)/shard_map/gram/pallas_call | solution.py:813
  122.8 5.9 %collective-permute-done.19.refs_1_ = bf16[2,64,1024]{2,1,0:T(8,128)(2,1)S(1)} collective-permute-done((bf16[2,64,1024]{2,1,0:T(8,128)(2,1)S(1)}, bf16[2,64,1024]{2,1,0:T(8,128)(2,1)S(1)}, u32[]{:S(2)}, u32[]{:S(2)}) %collective-permute-start.19) | collective-permute-done | bytes 262176 | tf_op jit(solution)/shard_map/ppermute | solution.py:996
  128.6 4.7 %newton.2 = (bf16[2,4,64,128]{3,2,1,0:T(8,128)(2,1)S(1)}, bf16[2,64,1024]{2,1,0:T(8,128)(2,1)}) custom-call(f32[2,4,64,64]{3,2,1,0:T(8,128)S(1)} %get-tuple-element.87.mine, f32[2,4,64,64]{3,2,1,0:T(8,128)S(1)} %collective-permute-done.18.theirs, bf16[2,64,1024]{2,1,0:T(8,128)(2,1)S(1)} %get-tuple-element.88.refs_0_, ...), custom_call_target="tpu_custom_call" | custom-call | flops 4024999936 | bytes 1000000 | tf_op jit(solution)/shard_map/newton/pallas_call | solution.py:475
  146.1 3.7 %collective-permute-start.20 = (bf16[2,64,1024]{2,1,0:T(8,128)(2,1)}, bf16[2,64,1024]{2,1,0:T(8,128)(2,1)S(1)}, u32[]{:S(2)}, u32[]{:S(2)}) collective-permute-start(bf16[2,64,1024]{2,1,0:T(8,128)(2,1)} %get-tuple-element.90.r0), channel_id=1, source_target_pairs={{0,1},{1,0},{2,3},{3,2},{4,5},{5,4},{6,7},{7,6},{8,9},{9,8},{10,11... | collective-permute-start | bytes 786440 | tf_op jit(solution)/shard_map/ppermute | solution.py:996
  149.8 6.5 %collective-permute-done.35.g2 = bf16[2,512,256]{2,1,0:T(8,128)(2,1)S(1)} collective-permute-done((bf16[2,512,256]{2,1,0:T(8,128)(2,1)S(1)}, bf16[2,512,256]{2,1,0:T(8,128)(2,1)S(1)}, u32[]{:S(2)}, u32[]{:S(2)}) %collective-permute-start.35) | collective-permute-done | bytes 524320 | tf_op jit(solution)/shard_map/ppermute | solution.py:993
  156.4 4.7 %collective-permute-start.22 = (bf16[2,64,1024]{2,1,0:T(8,128)(2,1)}, bf16[2,64,1024]{2,1,0:T(8,128)(2,1)S(1)}, u32[]{:S(2)}, u32[]{:S(2)}) collective-permute-start(bf16[2,64,1024]{2,1,0:T(8,128)(2,1)} %collective-permute-done.21.r2), channel_id=1, source_target_pairs={{0,1},{1,0},{2,3},{3,2},{4,5},{5,4},{6,7},{7,6},{8,9},{9,8},{10,11... | collective-permute-start | bytes 786440 | tf_op jit(solution)/shard_map/ppermute | solution.py:996
  163.7 4.5 %collective-permute-done.22.r3 = bf16[2,64,1024]{2,1,0:T(8,128)(2,1)S(1)} collective-permute-done((bf16[2,64,1024]{2,1,0:T(8,128)(2,1)}, bf16[2,64,1024]{2,1,0:T(8,128)(2,1)S(1)}, u32[]{:S(2)}, u32[]{:S(2)}) %collective-permute-start.22) | collective-permute-done | bytes 262176 | tf_op jit(solution)/shard_map/ppermute | solution.py:996
  171.9 13.8 %update.2 = (f32[6,2048,128]{2,1,0:T(8,128)}, f32[6,2048,128]{2,1,0:T(8,128)}, f32[6,2048,128]{2,1,0:T(8,128)}) custom-call(s32[3]{0:T(128)S(1)} %pad_add_fusion.scal.refs_0_.place, bf16[2,512,256]{2,1,0:T(8,128)(2,1)S(1)} %get-tuple-element.101.g0, bf16[2,512,256]{2,1,0:T(8,128)(2,1)S(1)} %collective-permute-done.34.g1, ...), custom_call_target="tpu_custom_call" | custom-call | flops 12650000384 | bytes 1000000 | tf_op jit(solution)/shard_map/update/pallas_call | solution.py:475
  185.8 7.6 %update.3 = (f32[6,2048,128]{2,1,0:T(8,128)}, f32[6,2048,128]{2,1,0:T(8,128)}, f32[6,2048,128]{2,1,0:T(8,128)}) custom-call(s32[3]{0:T(128)S(1)} %pad_add_fusion.scal.refs_0_.place, bf16[1,512,256]{2,1,0:T(8,128)(2,1)S(1)} %get-tuple-element.96.g0, ...), custom_call_target="tpu_custom_call", output_to_operand_aliasing={{0}: (12, {}), {1}: (13, {}), {2}: (14, {})} | custom-call | flops 6325000192 | bytes 1000000 | tf_op jit(solution)/shard_map/update/pallas_call | solution.py:475
  (143 shorter events, 61.4 us)
Async XLA Ops:
  4.8 14.8 %collective-permute-start.2 = (bf16[1,512,256]{2,1,0:T(8,128)(2,1)S(1)}, bf16[1,512,256]{2,1,0:T(8,128)(2,1)S(1)}, u32[]{:S(2)}, u32[]{:S(2)}) collective-permute-start(bf16[1,512,256]{2,1,0:T(8,128)(2,1)S(1)} %get-tuple-element.59.refs_2_), channel_id=1, source_target_pairs={{0,16},{4,20},{8,24},{12,28},{16,0},{20,4},{24,8},{28,12},{1,17},{... | collective-permute-start | bytes 786440 | tf_op jit(solution)/shard_map/ppermute | solution.py:993
  33.2 13.6 %collective-permute-start.5 = (bf16[2,512,256]{2,1,0:T(8,128)(2,1)}, bf16[2,512,256]{2,1,0:T(8,128)(2,1)}, u32[]{:S(2)}, u32[]{:S(2)}) collective-permute-start(bf16[2,512,256]{2,1,0:T(8,128)(2,1)} %collective-permute-done.3.refs_6_), channel_id=1, source_target_pairs={{0,8},{4,12},{8,0},{12,4},{16,24},{20,28},{24,16},{28,20},{1,9},{5... | collective-permute-start | bytes 1572872 | tf_op jit(solution)/shard_map/ppermute | solution.py:993
  42.1 29.8 %collective-permute-start = (bf16[256,1024]{1,0:T(8,128)(2,1)S(1)}, bf16[256,1024]{1,0:T(8,128)(2,1)S(1)}, u32[]{:S(2)}, u32[]{:S(2)}) collective-permute-start(bf16[256,1024]{1,0:T(8,128)(2,1)S(1)} %bitcast.57), channel_id=1, source_target_pairs={{0,4},{4,0},{8,12},{12,8},{16,20},{20,16},{24,28},{28,24},{1,5},{5... | collective-permute-start | bytes 1572872 | tf_op jit(solution)/shard_map/ppermute | solution.py:993
  42.5 29.4 %collective-permute-start.1 = (bf16[256,1024]{1,0:T(8,128)(2,1)S(1)}, bf16[256,1024]{1,0:T(8,128)(2,1)S(1)}, u32[]{:S(2)}, u32[]{:S(2)}) collective-permute-start(bf16[256,1024]{1,0:T(8,128)(2,1)S(1)} %bitcast.64), channel_id=1, source_target_pairs={{0,4},{4,0},{8,12},{12,8},{16,20},{20,16},{24,28},{28,24},{1,5},{5... | collective-permute-start | bytes 1572872 | tf_op jit(solution)/shard_map/ppermute | solution.py:993
  42.9 18.5 %collective-permute-start.4 = (bf16[2,512,256]{2,1,0:T(8,128)(2,1)}, bf16[2,512,256]{2,1,0:T(8,128)(2,1)}, u32[]{:S(2)}, u32[]{:S(2)}) collective-permute-start(bf16[2,512,256]{2,1,0:T(8,128)(2,1)} %collective-permute-done.3.refs_6_), channel_id=1, source_target_pairs={{0,4},{4,0},{8,12},{12,8},{16,20},{20,16},{24,28},{28,24},{1,5},{5... | collective-permute-start | bytes 1572872 | tf_op jit(solution)/shard_map/ppermute | solution.py:993
  46.8 14.7 %collective-permute-start.6 = (bf16[2,512,256]{2,1,0:T(8,128)(2,1)}, bf16[2,512,256]{2,1,0:T(8,128)(2,1)}, u32[]{:S(2)}, u32[]{:S(2)}) collective-permute-start(bf16[2,512,256]{2,1,0:T(8,128)(2,1)} %collective-permute-done.5.refs_8_), channel_id=1, source_target_pairs={{0,4},{4,0},{8,12},{12,8},{16,20},{20,16},{24,28},{28,24},{1,5},{5... | collective-permute-start | bytes 1572872 | tf_op jit(solution)/shard_map/ppermute | solution.py:993
  75.1 14.8 %collective-permute-start.11 = (bf16[2,512,256]{2,1,0:T(8,128)(2,1)S(1)}, bf16[2,512,256]{2,1,0:T(8,128)(2,1)S(1)}, u32[]{:S(2)}, u32[]{:S(2)}) collective-permute-start(bf16[2,512,256]{2,1,0:T(8,128)(2,1)S(1)} %get-tuple-element.71), channel_id=1, source_target_pairs={{0,16},{4,20},{8,24},{12,28},{16,0},{20,4},{24,8},{28,12},{1,17},{... | collective-permute-start | bytes 1572872 | tf_op jit(solution)/shard_map/ppermute | solution.py:993
  75.9 15.7 %collective-permute-start.12 = (bf16[2,512,256]{2,1,0:T(8,128)(2,1)S(1)}, bf16[2,512,256]{2,1,0:T(8,128)(2,1)S(1)}, u32[]{:S(2)}, u32[]{:S(2)}) collective-permute-start(bf16[2,512,256]{2,1,0:T(8,128)(2,1)S(1)} %get-tuple-element.73), channel_id=1, source_target_pairs={{0,8},{4,12},{8,0},{12,4},{16,24},{20,28},{24,16},{28,20},{1,9},{5... | collective-permute-start | bytes 1572872 | tf_op jit(solution)/shard_map/ppermute | solution.py:993
  81.4 14.3 %collective-permute-start.17 = (bf16[2,2,64,1024]{3,2,1,0:T(8,128)(2,1)S(1)}, bf16[2,2,64,1024]{3,2,1,0:T(8,128)(2,1)S(1)}, u32[]{:S(2)}, u32[]{:S(2)}) collective-permute-start(bf16[2,2,64,1024]{3,2,1,0:T(8,128)(2,1)S(1)} %get-tuple-element.86), channel_id=1, source_target_pairs={{0,1},{1,0},{2,3},{3,2},{4,5},{5,4},{6,7},{7,6},{8,9},{9,8},{10,11... | collective-permute-start | bytes 1572872 | tf_op jit(solution)/shard_map/ppermute | solution.py:996
  85.4 31.9 %collective-permute-start.23 = (bf16[640,256]{1,0:T(8,128)(2,1)S(1)}, bf16[640,256]{1,0:T(8,128)(2,1)S(1)}, u32[]{:S(2)}, u32[]{:S(2)}) collective-permute-start(bf16[640,256]{1,0:T(8,128)(2,1)S(1)} %get-tuple-element.93), channel_id=1, source_target_pairs={{0,16},{4,20},{8,24},{12,28},{16,0},{20,4},{24,8},{28,12},{1,17},{... | collective-permute-start | bytes 983048 | tf_op jit(solution)/shard_map/ppermute | solution.py:993
  86.1 31.3 %collective-permute-start.24 = (bf16[640,256]{1,0:T(8,128)(2,1)S(1)}, bf16[640,256]{1,0:T(8,128)(2,1)S(1)}, u32[]{:S(2)}, u32[]{:S(2)}) collective-permute-start(bf16[640,256]{1,0:T(8,128)(2,1)S(1)} %get-tuple-element.94), channel_id=1, source_target_pairs={{0,8},{4,12},{8,0},{12,4},{16,24},{20,28},{24,16},{28,20},{1,9},{5... | collective-permute-start | bytes 983048 | tf_op jit(solution)/shard_map/ppermute | solution.py:993
  89.9 27.5 %collective-permute-start.25 = (bf16[640,256]{1,0:T(8,128)(2,1)S(1)}, bf16[640,256]{1,0:T(8,128)(2,1)S(1)}, u32[]{:S(2)}, u32[]{:S(2)}) collective-permute-start(bf16[640,256]{1,0:T(8,128)(2,1)S(1)} %get-tuple-element.95), channel_id=1, source_target_pairs={{0,24},{4,28},{8,16},{12,20},{16,8},{20,12},{24,0},{28,4},{1,25},{... | collective-permute-start | bytes 983048 | tf_op jit(solution)/shard_map/ppermute | solution.py:993
  91.9 17.5 %collective-permute-start.15 = (bf16[1,512,256]{2,1,0:T(8,128)(2,1)S(1)}, bf16[1,512,256]{2,1,0:T(8,128)(2,1)S(1)}, u32[]{:S(2)}, u32[]{:S(2)}) collective-permute-start(bf16[1,512,256]{2,1,0:T(8,128)(2,1)S(1)} %get-tuple-element.83), channel_id=1, source_target_pairs={{0,8},{4,12},{8,0},{12,4},{16,24},{20,28},{24,16},{28,20},{1,9},{5... | collective-permute-start | bytes 786440 | tf_op jit(solution)/shard_map/ppermute | solution.py:993
  95.7 14.4 %collective-permute-start.16 = (bf16[1,512,256]{2,1,0:T(8,128)(2,1)S(1)}, bf16[1,512,256]{2,1,0:T(8,128)(2,1)S(1)}, u32[]{:S(2)}, u32[]{:S(2)}) collective-permute-start(bf16[1,512,256]{2,1,0:T(8,128)(2,1)S(1)} %get-tuple-element.84), channel_id=1, source_target_pairs={{0,16},{4,20},{8,24},{12,28},{16,0},{20,4},{24,8},{28,12},{1,17},{... | collective-permute-start | bytes 786440 | tf_op jit(solution)/shard_map/ppermute | solution.py:993
  114.7 13.9 %collective-permute-start.19 = (bf16[2,64,1024]{2,1,0:T(8,128)(2,1)S(1)}, bf16[2,64,1024]{2,1,0:T(8,128)(2,1)S(1)}, u32[]{:S(2)}, u32[]{:S(2)}) collective-permute-start(bf16[2,64,1024]{2,1,0:T(8,128)(2,1)S(1)} %get-tuple-element.89), channel_id=1, source_target_pairs={{0,2},{1,3},{2,0},{3,1},{4,6},{5,7},{6,4},{7,5},{8,10},{9,11},{10,... | collective-permute-start | bytes 786440 | tf_op jit(solution)/shard_map/ppermute | solution.py:996
  137.6 18.7 %collective-permute-start.35 = (bf16[2,512,256]{2,1,0:T(8,128)(2,1)S(1)}, bf16[2,512,256]{2,1,0:T(8,128)(2,1)S(1)}, u32[]{:S(2)}, u32[]{:S(2)}) collective-permute-start(bf16[2,512,256]{2,1,0:T(8,128)(2,1)S(1)} %get-tuple-element.101.g0), channel_id=1, source_target_pairs={{0,8},{4,12},{8,0},{12,4},{16,24},{20,28},{24,16},{28,20},{1,9},{5... | collective-permute-start | bytes 1572872 | tf_op jit(solution)/shard_map/ppermute | solution.py:993
  138.7 33.2 %collective-permute-start.34 = (bf16[2,512,256]{2,1,0:T(8,128)(2,1)S(1)}, bf16[2,512,256]{2,1,0:T(8,128)(2,1)S(1)}, u32[]{:S(2)}, u32[]{:S(2)}) collective-permute-start(bf16[2,512,256]{2,1,0:T(8,128)(2,1)S(1)} %get-tuple-element.101.g0), channel_id=1, source_target_pairs={{0,4},{4,0},{8,12},{12,8},{16,20},{20,16},{24,28},{28,24},{1,5},{5... | collective-permute-start | bytes 1572872 | tf_op jit(solution)/shard_map/ppermute | solution.py:993
  138.7 23.9 %collective-permute-start.38 = (bf16[2,4,64,128]{3,2,1,0:T(8,128)(2,1)S(1)}, bf16[2,4,64,128]{3,2,1,0:T(8,128)(2,1)}, u32[]{:S(2)}, u32[]{:S(2)}) collective-permute-start(bf16[2,4,64,128]{3,2,1,0:T(8,128)(2,1)S(1)} %get-tuple-element.99.refs_4_.q0), channel_id=1, source_target_pairs={{0,8},{4,12},{8,0},{12,4},{16,24},{20,28},{24,16},{28,20},{1,9},{5... | collective-permute-start | bytes 393224 | tf_op jit(solution)/shard_map/ppermute | solution.py:993
  146.1 16.7 %collective-permute-start.20 = (bf16[2,64,1024]{2,1,0:T(8,128)(2,1)}, bf16[2,64,1024]{2,1,0:T(8,128)(2,1)S(1)}, u32[]{:S(2)}, u32[]{:S(2)}) collective-permute-start(bf16[2,64,1024]{2,1,0:T(8,128)(2,1)} %get-tuple-element.90.r0), channel_id=1, source_target_pairs={{0,1},{1,0},{2,3},{3,2},{4,5},{5,4},{6,7},{7,6},{8,9},{9,8},{10,11... | collective-permute-start | bytes 786440 | tf_op jit(solution)/shard_map/ppermute | solution.py:996
  156.4 15.6 %collective-permute-start.36 = (bf16[2,512,256]{2,1,0:T(8,128)(2,1)S(1)}, bf16[2,512,256]{2,1,0:T(8,128)(2,1)S(1)}, u32[]{:S(2)}, u32[]{:S(2)}) collective-permute-start(bf16[2,512,256]{2,1,0:T(8,128)(2,1)S(1)} %collective-permute-done.35.g2), channel_id=1, source_target_pairs={{0,4},{4,0},{8,12},{12,8},{16,20},{20,16},{24,28},{28,24},{1,5},{5... | collective-permute-start | bytes 1572872 | tf_op jit(solution)/shard_map/ppermute | solution.py:993
  170.8 14.9 %collective-permute-start.26 = (bf16[1,512,256]{2,1,0:T(8,128)(2,1)S(1)}, bf16[1,512,256]{2,1,0:T(8,128)(2,1)S(1)}, u32[]{:S(2)}, u32[]{:S(2)}) collective-permute-start(bf16[1,512,256]{2,1,0:T(8,128)(2,1)S(1)} %get-tuple-element.96.g0), channel_id=1, source_target_pairs={{0,4},{4,0},{8,12},{12,8},{16,20},{20,16},{24,28},{28,24},{1,5},{5... | collective-permute-start | bytes 786440 | tf_op jit(solution)/shard_map/ppermute | solution.py:993
  171.3 14.4 %collective-permute-start.28 = (bf16[1,512,256]{2,1,0:T(8,128)(2,1)S(1)}, bf16[1,512,256]{2,1,0:T(8,128)(2,1)S(1)}, u32[]{:S(2)}, u32[]{:S(2)}) collective-permute-start(bf16[1,512,256]{2,1,0:T(8,128)(2,1)S(1)} %collective-permute-done.27.g2), channel_id=1, source_target_pairs={{0,4},{4,0},{8,12},{12,8},{16,20},{20,16},{24,28},{28,24},{1,5},{5... | collective-permute-start | bytes 786440 | tf_op jit(solution)/shard_map/ppermute | solution.py:993
  171.4 14.3 %collective-permute-start.31 = (bf16[1,4,64,128]{3,2,1,0:T(8,128)(2,1)S(1)}, bf16[1,4,64,128]{3,2,1,0:T(8,128)(2,1)S(1)}, u32[]{:S(2)}, u32[]{:S(2)}) collective-permute-start(bf16[1,4,64,128]{3,2,1,0:T(8,128)(2,1)S(1)} %get-tuple-element.100.q0), channel_id=1, source_target_pairs={{0,4},{4,0},{8,12},{12,8},{16,20},{20,16},{24,28},{28,24},{1,5},{5... | collective-permute-start | bytes 196616 | tf_op jit(solution)/shard_map/ppermute | solution.py:993
  171.8 13.9 %collective-permute-start.33 = (bf16[1,4,64,128]{3,2,1,0:T(8,128)(2,1)S(1)}, bf16[1,4,64,128]{3,2,1,0:T(8,128)(2,1)S(1)}, u32[]{:S(2)}, u32[]{:S(2)}) collective-permute-start(bf16[1,4,64,128]{3,2,1,0:T(8,128)(2,1)S(1)} %collective-permute-done.32.q2), channel_id=1, source_target_pairs={{0,4},{4,0},{8,12},{12,8},{16,20},{20,16},{24,28},{28,24},{1,5},{5... | collective-permute-start | bytes 196616 | tf_op jit(solution)/shard_map/ppermute | solution.py:993
  (36 other events, 366.4 us)

commit v5 on v4

--- a/solution.py
+++ b/solution.py
@@ -447,13 +447,13 @@
 
 
 def in_hbm(array):
-    if array.size * array.dtype.itemsize < 1 << 20:
+    if array.size * array.dtype.itemsize < 1 << 21:
         return array
     return pltpu.with_memory_space_constraint(array, pltpu.HBM)
 
 
 def out_hbm(shape):
-    if shape.size * shape.dtype.itemsize < 1 << 20:
+    if shape.size * shape.dtype.itemsize < 1 << 21:
         return shape
     return pltpu.HBM(shape.shape, shape.dtype)
 
@@ -483,7 +483,7 @@
     )(*map(in_hbm, operands), *map(in_hbm, after))
 
 
-def relayout_kernel(n, head, scal, src, out, *refs):
+def relayout_kernel(n, head, scal, lower, upper, out, *refs):
     scratch = refs[-1]
     low = low_lanes(n)
     place_of = members_of(head)
@@ -493,7 +493,7 @@
             pair = []
             for j in (2 * half, 2 * half + 1):
                 group, line = place_of(piece, j)
-                pair.append(src[group, pl.ds(line, n, stride=8), :])
+                pair.append((lower, upper)[group][0, pl.ds(line, n, stride=8), :])
             a, b = pair
             scratch[k, pl.ds(0, n, stride=2), :] = jnp.where(low, a, pltpu.roll(b, 64, 1))
             scratch[k, pl.ds(1, n, stride=2), :] = jnp.where(low, pltpu.roll(a, 64, 1), b)
@@ -510,12 +510,13 @@
         specs.append(pl.BlockSpec((1, 2 * n, 256), lambda k, i: (k, i, 0)))
     return launch(
         functools.partial(relayout_kernel, n, first == 0),
-        [scal, native_view(array)],
+        [scal, native_view(array), native_view(array)],
         shapes,
         "relayout",
         specs=[
             mem(pltpu.SMEM),
-            pl.BlockSpec((2, 8 * n, 128), lambda k, i: (first + k, i, 0)),
+            pl.BlockSpec((1, 8 * n, 128), lambda k, i: (2 * first + 2 * k, i, 0)),
+            pl.BlockSpec((1, 8 * n, 128), lambda k, i: (2 * first + 2 * k + 1, i, 0)),
         ],
         after=after,
         cost=1.3 * count,
@@ -717,9 +718,9 @@
 
 
 def head_grads_kernel(
-    scal, x, x_beside, cot, cot_beside, norms, keep, came, totals, totals_came, *outs
+    scal, x, x_beside, cot, cot_beside, norms, keep, came, totals, *outs
 ):
-    both = (totals[...] + totals_came[...]).reshape(64, 256)
+    both = totals[...].reshape(64, 256)
     coarse = both.astype(jnp.bfloat16)
     fine = (both - coarse.astype(jnp.float32)).astype(jnp.bfloat16)
     sides = both_cores(scal, x, x_beside, cot, cot_beside, norms, 0)
@@ -728,10 +729,23 @@
         pre_grad, attended = split_last(piece)
         for side, (h, c) in enumerate(sides):
             grad = dot(h, pre_grad, TN) + dot(c, attended, TN)
-            target = outs[2 * far + side]
-            target[0:512] = grad.astype(jnp.bfloat16)
-            target[512:576] = coarse
-            target[576:640] = fine
+            outs[side][far, 0:512] = grad.astype(jnp.bfloat16)
+            outs[side][far, 512:576] = coarse
+            outs[side][far, 576:640] = fine
+
+
+def combine_heads_kernel(keep, came, own, send):
+    for target, at in ((own, 0), (send, 1)):
+        total = keep[at].astype(jnp.float32) + came[at].astype(jnp.float32)
+        target[0:512] = total[0:512].astype(jnp.bfloat16)
+        tail = total[512:576] + total[576:640]
+        coarse = tail.astype(jnp.bfloat16)
+        target[512:576] = coarse
+        target[576:640] = (tail - coarse.astype(jnp.float32)).astype(jnp.bfloat16)
+
+
+def add_kernel(near, came, kept, passed):
+    add_up([((near, came), [kept, passed])])
 
 
 def gather_kernel(
@@ -784,12 +798,12 @@
         grams[0, j] = gram[cut, cut]
 
 
-def unit_gram_kernel(place, own, in_came, down_came, momenta, near, came, *refs):
-    grads, grams, first, second = refs[-4:]
+def unit_gram_kernel(place, own, in_came, down_came, momenta, kept, came, *refs):
+    grads, grams, total = refs[-3:]
 
     @pl.when(pl.program_id(0) == 0)
     def _():
-        add_up([((near, came), [first, second])])
+        add_up([((kept, came), total)])
 
     a = in_came[0].astype(jnp.float32)
     b = down_came[0].astype(jnp.float32)
@@ -797,13 +811,11 @@
     gram_of_piece(own[0].astype(jnp.float32) + other, momenta, grads, grams)
 
 
-def head_gram_kernel(place, own, a, b, c, momenta, *refs):
+def head_gram_kernel(place, own, came, momenta, *refs):
     grads, grams, totals = refs[-3:]
-    values = [part[...].astype(jnp.float32) for part in (own, a, b, c)]
-    total = (values[0] + values[1]) + (values[2] + values[3])
+    total = own[...].astype(jnp.float32) + came[...].astype(jnp.float32)
     gram_of_piece(total[0:512], momenta, grads, grams)
-    sums = [v[512:576] + v[576:640] for v in values]
-    totals[...] = ((sums[0] + sums[1]) + (sums[2] + sums[3])).reshape(8, 8, 256)
+    totals[...] = (total[512:576] + total[576:640]).reshape(8, 8, 256)
 
 
 def gram_of(kernel, first, others, momenta, place, more, shapes, after=()):
@@ -878,7 +890,8 @@
         mix = s[1] * s[2]
         coarse = mix.astype(jnp.bfloat16)
         fine = (mix - coarse.astype(jnp.float32)).astype(jnp.bfloat16)
-        out[i, j] = jnp.concatenate([coarse, fine], axis=1)
+        rows, lanes = slice(64 * (j // 2), 64 * (j // 2) + 64), slice(128 * (j % 2), 128 * (j % 2) + 128)
+        out[i, rows, lanes] = jnp.concatenate([coarse, fine], axis=1)
 
 
 def newton(mine, theirs, sums, after=()):
@@ -887,7 +900,7 @@
     return launch(
         functools.partial(newton_kernel, [len(group) for group in sums]),
         operands,
-        [jax.ShapeDtypeStruct((*mine.shape[:-1], 2 * HD), jnp.bfloat16)]
+        [jax.ShapeDtypeStruct((mine.shape[0], 2 * HD, 256), jnp.bfloat16)]
         + [jax.ShapeDtypeStruct(group[0].shape, group[0].dtype) for group in sums],
         "newton",
         cost=3.5,
@@ -910,7 +923,8 @@
     def _():
         for r, q in enumerate((q0, q1, q2, q3)):
             for j in range(4):
-                wide = q[0, j].astype(jnp.float32)
+                at = slice(HD * (j // 2), HD * (j // 2) + HD), slice(128 * (j % 2), 128 * (j % 2) + 128)
+                wide = q[(0,) * (len(q.shape) - 2) + at].astype(jnp.float32)
                 other = pltpu.roll(wide, HD, 1)
                 below = low_lanes(HD) == (j % 2 == 0)
                 rows = slice(j * HD, (j + 1) * HD)
@@ -923,7 +937,7 @@
     low = low_lanes(n)
     for r, piece in enumerate((g0, g1, g2, g3)):
         place = scal[1] ^ r
-        grad = piece[0].astype(jnp.float32)
+        grad = piece[(0,) * (len(piece.shape) - 2)].astype(jnp.float32)
         update = 1.95 * grad + 0.9025 * momenta[place]
         coarse = update.astype(jnp.bfloat16)
         fine = (update - coarse.astype(jnp.float32)).astype(jnp.bfloat16)
@@ -947,19 +961,26 @@
     weights[...] = weight - muon_rate * (4.0 * steps[...] + weight_decay * weight)
 
 
-def update(first, scal, grads, mixes, momenta, native_momenta, native, before=(), after=(), n=64):
-    chunks = grads[0].shape[0]
+def update(
+    first, scal, own, far, mix, mix_far, beside, momenta, native_momenta, native, before=(), after=(), n=64
+):
+    chunks = own.shape[0]
     block = pl.BlockSpec((2, 8 * n, 128), lambda k, i: (first + k, i, 0))
     piece = pl.BlockSpec((1, 2 * n, 256), lambda k, i: (k, i, 0))
-    mix = pl.BlockSpec((1, 4, HD, 2 * HD), lambda k, i: (k, 0, 0, 0))
+    factor = pl.BlockSpec((1, 2 * HD, 256), lambda k, i: (k, 0, 0))
+    pieces, factors = [piece, None, piece, None], [factor, None, factor, None]
+    for r in (0, 1):
+        pieces[2 * r + 1] = pl.BlockSpec((1, 1, 2 * n, 256), lambda k, i, r=r: (r, k, i, 0))
+        factors[2 * r + 1] = pl.BlockSpec((1, 1, 2 * HD, 256), lambda k, i, r=r: (r, k, 4, 0))
+    grads, mixes = [own, beside, far, beside], [mix, beside, mix_far, beside]
     return launch(
         functools.partial(update_kernel, n, first == 0),
         [scal, *grads, *mixes, momenta, native_view(native_momenta), native_view(native), *before],
         [jax.ShapeDtypeStruct((6, 2048, 128), jnp.float32)] * 3,
         "update",
         specs=[mem(pltpu.SMEM)]
-        + [piece] * 4
-        + [mix] * 4
+        + pieces
+        + factors
         + [pl.BlockSpec((4, 2 * n, 256), lambda k, i: (k, i, 0)), block, block]
         + [mem(pl.ANY)] * len(before),
         after=after,
@@ -994,6 +1015,9 @@
 
     def hop_tp(values, by):
         return lax.ppermute(values, "tp", [(i, i ^ by) for i in range(4)])
+
+    def tied(values, *results):
+        return lax.optimization_barrier((values, *results))[0]
 
     def spread(piece):
         c = hop(piece, 2)
@@ -1018,11 +1042,8 @@
     first_hop = hop(mine, 4)
     other_heads = spread(first_hop)
     unit_weights, mine_units = relayout(scal, matrices, bf16, 1, 2, mine=True, after=(mine,))
-    (piled_heads,) = relayout(scal, momenta, f32, 0, 1, after=(mine_units,))
-    first_hop, mine_units, cosine, sine, _ = lax.optimization_barrier(
-        (first_hop, mine_units, cosine, sine, piled_heads)
-    )
-    other_units = spread(hop(mine_units, 4))
+    (piled_heads,) = relayout(scal, momenta, f32, 0, 1, after=(mine_units, first_hop))
+    units_near = hop(tied(mine_units, first_hop), 4)
     x_beside = hop(x, 1)
     cot_beside = hop(cot, 1)
 
@@ -1035,6 +1056,9 @@
     )
     arrived = lax.all_to_all(send, both, split_axis=0, concat_axis=0, tiled=True)
     (piled_units,) = relayout(scal, momenta, f32, 1, 2, after=(send,))
+    units_near = tied(units_near, send)
+    units_far = hop(units_near, 2)
+    units_beside = hop(units_near, 1)
     documents = lax.dynamic_index_in_dim(segments, blk_at, 0, keepdims=False)
     length = documents.shape[0]
     attended = launch(
@@ -1050,6 +1074,8 @@
         attended.reshape(8, local_rows, 256), both, split_axis=0, concat_axis=0, tiled=True
     )
 
+    units_far = tied(units_far, attended)
+    other_units = [units_near, units_beside, units_far, hop(units_far, 1)]
     ff_branch, ff_part, unit_keep, unit_send, unit_sums, norm_two, cot_sums = launch(
         feed_forward_kernel,
         [scal, x, cot, norms, unit_bias, unit_weights, *other_units],
@@ -1091,13 +1117,15 @@
         after=(in_keep,),
         scratch_shapes=[pltpu.VMEM((4, 2, 64, width), bf16)],
     )
-    head_grads = launch(
+    heads_keep, heads_send = launch(
         head_grads_kernel,
-        [scal, x, x_beside, cot, cot_beside, norms, head_keep, hop(head_send, 1), totals, hop(totals, 1)],
-        [shaped((640, 256), bf16)] * 4,
+        [scal, x, x_beside, cot, cot_beside, norms, head_keep, hop(head_send, 1), totals],
+        [shaped((2, 640, 256), bf16)] * 2,
         "head_grads",
         cost=4,
     )
+    came = hop_tp(far, 1)
+    heads_came = hop(heads_send, 4)
     operands = [in_keep, hop(in_send, 4), down_keep, hop(down_send, 2)]
     own, in_send, down_send = launch(
         combine_kernel,
@@ -1106,37 +1134,80 @@
         "combine",
         specs=[full(a) for a in operands],
         cost=2,
-        after=(head_grads[0],),
-    )
-    unit_sum, unit_grams, kept, passed = gram_of(
+        after=(heads_keep,),
+    )
+    in_came, down_came = hop(in_send, 2), hop(down_send, 4)
+    kept, passed = launch(
+        add_kernel,
+        [near, came],
+        [shaped((2, 64, width), bf16)] * 2,
+        "add",
+        specs=[full(near)] * 2,
+        after=(in_send,),
+    )
+    passed = hop_tp(passed, 2)
+    heads_own, heads_send = launch(
+        combine_heads_kernel,
+        [heads_keep, heads_came],
+        [shaped((640, 256), bf16)] * 2,
+        "combine_heads",
+        specs=[full(heads_keep)] * 2,
+        after=(kept,),
+    )
+    heads_came = hop(heads_send, 2)
+    unit_sum, unit_grams, total = gram_of(
         unit_gram_kernel,
         own,
-        [hop(in_send, 2), hop(down_send, 4)],
+        [in_came, down_came],
         piled_units,
         scal,
-        [near, hop_tp(far, 1)],
-        [shaped((2, 64, width), bf16)] * 2,
-    )
-    unit_pieces = spread(unit_sum)
-    unit_mix, total = newton(unit_grams, hop(unit_grams, 4), [(kept, hop_tp(passed, 2))])
+        [kept, passed],
+        [shaped((2, 64, width), bf16)],
+        after=(heads_own,),
+    )
+    unit_theirs = hop(unit_grams, 4)
+    unit_far = hop(unit_sum, 2)
+    total_far = hop_tp(total, 2)
     head_sum, head_grams, totals = gram_of(
         head_gram_kernel,
-        head_grads[0],
-        [hop(head_grads[1], 4), hop(head_grads[2], 2), hop(head_grads[3], 6)],
+        heads_own,
+        [heads_came],
         piled_heads,
         scal,
         [],
         [shaped((8, 8, 256), f32)],
-    )
-    head_pieces = spread(head_sum)
+        after=(unit_sum,),
+    )
+    head_theirs = hop(head_grams, 4)
+    head_far = hop(head_sum, 2)
+    (unit_mix,) = newton(unit_grams, unit_theirs, [], after=(head_sum,))
+    unit_mix_far = hop(unit_mix, 2)
     head_mix, totals = newton(
-        head_grams, hop(head_grams, 4), [(totals, hop_tp(totals, 1))], after=(unit_mix,)
-    )
-    before = update(1, scal, unit_pieces, spread(unit_mix), piled_units, momenta, matrices)
-    outs = update(0, scal, head_pieces, spread(head_mix), piled_heads, momenta, matrices, before)
+        head_grams,
+        head_theirs,
+        [(totals, hop(totals, 1))],
+        after=(unit_mix, unit_far, total_far),
+    )
+    head_mix_far = hop(head_mix, 2)
+
+    def to_beside(*pieces):
+        return hop(jnp.stack([jnp.concatenate(pair, axis=1) for pair in pieces]), 1)
+
+    beside = to_beside((unit_sum, unit_mix), (unit_far, tied(unit_mix_far, head_mix)))
+    totals_came = hop_tp(totals, 1)
+    before = update(
+        1, scal, unit_sum, unit_far, unit_mix, unit_mix_far, beside, piled_units, momenta, matrices,
+        after=(head_mix,),
+    )
+    beside = to_beside((head_sum, head_mix), (head_far, head_mix_far))
+    outs = update(
+        0, scal, head_sum, head_far, head_mix, head_mix_far, beside, piled_heads, momenta, matrices,
+        before,
+    )
+    total_beside = hop_tp(tied(jnp.stack([total, total_far]), head_mix), 1)
+    totals = tied(totals + totals_came, before[0])
     totals = totals + hop_tp(totals, 2)
 
-    beside = hop_tp(total, 2)
     block_output, input_grad = launch(
         finish_rows_kernel,
         [
@@ -1145,13 +1216,14 @@
             cot.reshape(4, 64, width),
             (small[4 * width : 5 * width] + small[5 * width : 6 * width]).reshape(1, width),
             total,
-            hop_tp(total, 1),
-            beside,
-            hop_tp(beside, 1),
+            total_beside[0],
+            total_far,
+            total_beside[1],
         ],
         [shaped((4, 64, width), f32)] * 2,
         "finish_rows",
         cost=2,
+        after=(before[0],),
     )
 
     cot_total = totals[2, :4].reshape(-1) * 0.25

time: 195 us -> 183 us (0.938)
  waiting for transfers between devices: 53.9 us -> 48.4 us
  starting transfers between devices: 43.9 us -> 40.8 us
    ppermute x7 -> x6, waiting for transfers between devices: 16.9 us -> 5.4 us  [hop_tp(): return lax.ppermute(values, 'tp', [(i, i ^ by) for i in range(4)])]
    ppermute x34 -> x27, waiting for transfers between devices: 30.3 us -> 41.6 us  [hop(): return lax.ppermute(values, both, [(i, i ^ by) for i in range(8)])]
    ppermute x7 -> x6, starting transfers between devices: 14.2 us -> 9.46 us  [hop_tp(): return lax.ppermute(values, 'tp', [(i, i ^ by) for i in range(4)])]
    all_to_all x1, waiting for transfers between devices: 5 us -> 0.92 us  [whole_device(): lax.all_to_all(send, both, split_axis=0, concat_axis=0, tiled=True)]
    pallas_call x17 -> x19, Pallas kernels: 81.5 us -> 79.8 us  [launch(): pl.pallas_call(body, in_specs=list(specs) + [corner(a) for a in after], o...]
    ppermute x34 -> x27, starting transfers between devices: 22.5 us -> 23.8 us  [hop(): return lax.ppermute(values, both, [(i, i ^ by) for i in range(8)])]
  transfers between devices with their start and end apart: 43 -> 35, of which waited for: 13 -> 14; matrix products, arithmetic and copies ran while one was open for 3% -> 1% of each run, Pallas kernels for 38% -> 46%
where the time goes in v5:
time: 183 us; the launch traced here: 182 us
  Pallas kernels  86 us (47%)
  waiting for transfers between devices  48.4 us (26%)
  starting transfers between devices  40.8 us (22%)
  local copies, waits for them, and re-layouts  4.12 us (2%)
    pallas_call x19, Pallas kernels, launch(): pl.pallas_call(body, in_specs=list(specs) + [corner(a) for a in after], o...  79.8 us
    ppermute x27, waiting for transfers between devices, hop(): return lax.ppermute(values, both, [(i, i ^ by) for i in range(8)])  41.6 us
    ppermute x27, starting transfers between devices, hop(): return lax.ppermute(values, both, [(i, i ^ by) for i in range(8)])  23.8 us
    ppermute x6, starting transfers between devices, hop_tp(): return lax.ppermute(values, 'tp', [(i, i ^ by) for i in range(4)])  9.46 us
    pallas_call x2, Pallas kernels, gram_of(): pl.pallas_call(kernel, grid_spec=pltpu.PrefetchScalarGridSpec(num_scalar_...  6.22 us
    ppermute x6, waiting for transfers between devices, hop_tp(): return lax.ppermute(values, 'tp', [(i, i ^ by) for i in range(4)])  5.4 us
    all_to_all x1, starting transfers between devices, whole_device(): lax.all_to_all(attended.reshape(8, local_rows, 256), both, split_axis=0,...  4.09 us
  transfers between devices with their start and end apart: 35, of which 14 were waited for; matrix products, arithmetic and copies ran while one was open for 1% of the time, Pallas kernels for 46%

profile of v5, /device:TPU:0, one launch (start us, length us, event | category | flops | bytes accessed | tf_op | source)
XLA Modules:
  0.0 182.2 jit_solution(18090018686934274279)
XLA Ops:
  6.8 6.3 %collective-permute-done.2.refs_6_.refs_4_ = bf16[1,512,256]{2,1,0:T(8,128)(2,1)S(1)} collective-permute-done((bf16[1,512,256]{2,1,0:T(8,128)(2,1)S(1)}, bf16[1,512,256]{2,1,0:T(8,128)(2,1)S(1)}, u32[]{:S(2)}, u32[]{:S(2)}) %collective-permute-start.2) | collective-permute-done | bytes 262176 | tf_op jit(solution)/shard_map/ppermute | solution.py:1014
  15.6 5.0 %collective-permute-done.5.refs_8_ = bf16[1,512,256]{2,1,0:T(8,128)(2,1)S(1)} collective-permute-done((bf16[1,512,256]{2,1,0:T(8,128)(2,1)S(1)}, bf16[1,512,256]{2,1,0:T(8,128)(2,1)S(1)}, u32[]{:S(2)}, u32[]{:S(2)}) %collective-permute-start.5) | collective-permute-done | bytes 262176 | tf_op jit(solution)/shard_map/ppermute | solution.py:1014
  20.6 6.9 %relayout.5 = (bf16[8,512,256]{2,1,0:T(8,128)(2,1)}, bf16[2,512,256]{2,1,0:T(8,128)(2,1)S(1)}) custom-call(s32[3]{0:T(128)S(1)} %pad_add_fusion.scal.refs_0_.place, f32[6,2048,128]{2,1,0:T(8,128)} %bitcast.84, f32[6,2048,128]{2,1,0:T(8,128)} %bitcast.85, bf16[1,512,256]{2,1,0:T(8,128)(2,1)S(1)} %get-tuple-element.61.refs_3_), custom_call_target="tpu_custom_call" | custom-call | flops 2990000128 | bytes 1000000 | tf_op jit(solution)/shard_map/relayout/pallas_call | solution.py:475
  28.9 3.8 %project.1.refs_3_ = bf16[8,128,256]{2,1,0:T(8,128)(2,1)} custom-call(s32[3]{0:T(128)S(1)} %pad_add_fusion.scal.refs_0_.place, bf16[256,1024]{1,0:T(8,128)(2,1)} %bitcast.6.x.refs_1_, bf16[256,1024]{1,0:T(8,128)(2,1)} %bitcast.7.cot.refs_2_.refs_3_, f32[4,1024]{1,0:T(4,128)S(1)} %slice.40.norms.refs_3_.refs_5_.refs_2_, f32[4,256]{1,0:T(4,128)S(1)} %pad.4.bias, ...), custom_call_target="tpu_custom_call" | custom-call | flops 3449999872 | bytes 1000000 | tf_op jit(solution)/shard_map/project/pallas_call | solution.py:475
  33.3 3.5 %all-to-all-start = ((bf16[8,128,256]{2,1,0:T(8,128)(2,1)}), bf16[8,128,256]{2,1,0:T(8,128)(2,1)S(1)}, u32[]{:S(2)}, u32[]{:S(2)}) async-start(bf16[8,128,256]{2,1,0:T(8,128)(2,1)} %project.1.refs_3_), calls=%async_computation | async-start | bytes 1048576 | tf_op jit(solution)/shard_map/all_to_all | solution.py:1057
  37.1 5.5 %collective-permute-done.3.refs_6_ = bf16[2,512,256]{2,1,0:T(8,128)(2,1)} collective-permute-done((bf16[2,512,256]{2,1,0:T(8,128)(2,1)S(1)}, bf16[2,512,256]{2,1,0:T(8,128)(2,1)}, u32[]{:S(2)}, u32[]{:S(2)}) %collective-permute-start.3) | collective-permute-done | bytes 524320 | tf_op jit(solution)/shard_map/ppermute | solution.py:1014
  42.6 3.9 %collective-permute-start.8 = (bf16[2,512,256]{2,1,0:T(8,128)(2,1)}, bf16[2,512,256]{2,1,0:T(8,128)(2,1)}, u32[]{:S(2)}, u32[]{:S(2)}) collective-permute-start(bf16[2,512,256]{2,1,0:T(8,128)(2,1)} %collective-permute-done.3.refs_6_), channel_id=1, source_target_pairs={{0,8},{4,12},{8,0},{12,4},{16,24},{20,28},{24,16},{28,20},{1,9},{5... | collective-permute-start | bytes 1572872 | tf_op jit(solution)/shard_map/ppermute | solution.py:1014
  47.4 6.0 %attention.1.refs_10_ = bf16[1024,256]{1,0:T(8,128)(2,1)} custom-call(bf16[1024,256]{1,0:T(8,128)(2,1)S(1)} %bitcast.68, s32[1024,1]{1,0:T(8,128)S(1)} %copy.21.seg), custom_call_target="tpu_custom_call" | custom-call | flops 6899999744 | bytes 1000000 | tf_op jit(solution)/shard_map/attention/pallas_call | solution.py:475
  53.3 6.0 %collective-permute-done.8.refs_8_ = bf16[2,512,256]{2,1,0:T(8,128)(2,1)} collective-permute-done((bf16[2,512,256]{2,1,0:T(8,128)(2,1)}, bf16[2,512,256]{2,1,0:T(8,128)(2,1)}, u32[]{:S(2)}, u32[]{:S(2)}) %collective-permute-start.8) | collective-permute-done | bytes 524320 | tf_op jit(solution)/shard_map/ppermute | solution.py:1014
  59.9 4.1 %all-to-all-start.1 = ((bf16[8,128,256]{2,1,0:T(8,128)(2,1)}), bf16[8,128,256]{2,1,0:T(8,128)(2,1)S(1)}, u32[]{:S(2)}, u32[]{:S(2)}) async-start(bf16[8,128,256]{2,1,0:T(8,128)(2,1)} %bitcast.20), calls=%async_computation.1 | async-start | bytes 1048576 | tf_op jit(solution)/shard_map/all_to_all | solution.py:1073
  64.0 6.1 %feed_forward.1 = (f32[256,1024]{1,0:T(8,128)S(1)}, f32[256,1024]{1,0:T(8,128)S(1)}, bf16[2,2,256,256]{3,2,1,0:T(8,128)(2,1)S(1)}, bf16[2,2,256,256]{3,2,1,0:T(8...) custom-call(s32[3]{0:T(128)S(1)} %pad_add_fusion.scal.refs_0_.place, ...), custom_call_target="tpu_custom_call" | custom-call | flops 6325000192 | bytes 1000000 | tf_op jit(solution)/shard_map/feed_forward/pallas_call | solution.py:475
  75.2 3.6 %unit_grads.1 = (bf16[2,512,256]{2,1,0:T(8,128)(2,1)S(1)}, bf16[2,512,256]{2,1,0:T(8,128)(2,1)S(1)}, bf16[2,512,256]{2,1,0:T(8,128)(2,1)S(1)}, bf16[2,512,256]{2,1,0:T(8,128)(2,1)S(1)}) custom-call(s32[3]{0:T(128)S(1)} %pad_add_fusion.scal.refs_0_.place, bf16[256,1024]{1,0:T(8,128)(2,1)} %bitcast.6.x.refs_1_, ...), custom_call_target="tpu_custom_call" | custom-call | flops 4024999936 | bytes 1000000 | tf_op jit(solution)/shard_map/unit_grads/pallas_call | solution.py:475
  82.3 3.1 %gather.1 = (bf16[2,2,64,1024]{3,2,1,0:T(8,128)(2,1)S(1)}, bf16[2,2,64,1024]{3,2,1,0:T(8,128)(2,1)S(1)}, f32[8,8,256]{2,1,0:T(8,128)S(1)}) custom-call(s32[3]{0:T(128)S(1)} %pad_add_fusion.scal.refs_0_.place, bf16[256,1024]{1,0:T(8,128)(2,1)} %bitcast.6.x.refs_1_, f32[4,1024]{1,0:T(4,128)S(1)} %slice.40.norms.refs_3_.refs_5_.refs_2_, ...), custom_call_target="tpu_custom_call" | custom-call | flops 3449999872 | bytes 1000000 | tf_op jit(solution)/shard_map/gather/pallas_call | solution.py:475
  87.1 3.3 %head_grads.1 = (bf16[2,640,256]{2,1,0:T(8,128)(2,1)S(1)}, bf16[2,640,256]{2,1,0:T(8,128)(2,1)S(1)}) custom-call(s32[3]{0:T(128)S(1)} %pad_add_fusion.scal.refs_0_.place, bf16[256,1024]{1,0:T(8,128)(2,1)} %bitcast.6.x.refs_1_, bf16[256,1024]{1,0:T(8,128)(2,1)S(1)} %copy-done.3, bf16[256,1024]{1,0:T(8,128)(2,1)} %bitcast.7.cot.refs_2_.refs_3_, ...), custom_call_target="tpu_custom_call" | custom-call | flops 4600000000 | bytes 1000000 | tf_op jit(solution)/shard_map/head_grads/pallas_call | solution.py:475
  91.0 4.2 %relayout.7.momenta = f32[4,512,256]{2,1,0:T(8,128)} custom-call(s32[3]{0:T(128)S(1)} %pad_add_fusion.scal.refs_0_.place, f32[6,2048,128]{2,1,0:T(8,128)} %bitcast.76, f32[6,2048,128]{2,1,0:T(8,128)} %bitcast.77, bf16[2,512,256]{2,1,0:T(8,128)(2,1)S(1)} %get-tuple-element.64.refs_3_, bf16[1,512,256]{2,1,0:T(8,128)(2,1)S(1)} %collective-permute-done.2.refs_6_.refs_4_), custom_call_target="tpu_custom_call" | custom-call | flops 1495000064 | bytes 1000000 | tf_op jit(solution)/shard_map/relayout/pallas_call | solution.py:475
  101.7 6.4 %collective-permute-done.18.refs_1_ = bf16[2,640,256]{2,1,0:T(8,128)(2,1)S(1)} collective-permute-done((bf16[2,640,256]{2,1,0:T(8,128)(2,1)S(1)}, bf16[2,640,256]{2,1,0:T(8,128)(2,1)S(1)}, u32[]{:S(2)}, u32[]{:S(2)}) %collective-permute-start.18) | collective-permute-done | bytes 655392 | tf_op jit(solution)/shard_map/ppermute | solution.py:1014
  109.9 7.4 %relayout.6.momenta.refs_9_ = f32[8,512,256]{2,1,0:T(8,128)} custom-call(s32[3]{0:T(128)S(1)} %pad_add_fusion.scal.refs_0_.place, f32[6,2048,128]{2,1,0:T(8,128)} %bitcast.78, f32[6,2048,128]{2,1,0:T(8,128)} %bitcast.79, bf16[8,128,256]{2,1,0:T(8,128)(2,1)} %project.1.refs_3_), custom_call_target="tpu_custom_call" | custom-call | flops 2990000128 | bytes 1000000 | tf_op jit(solution)/shard_map/relayout/pallas_call | solution.py:475
  117.2 3.7 %gram.2 = (bf16[2,512,256]{2,1,0:T(8,128)(2,1)S(1)}, f32[2,4,64,64]{3,2,1,0:T(8,128)S(1)}, bf16[2,64,1024]{2,1,0:T(8,128)(2,1)S(1)}) custom-call(s32[3]{0:T(128)S(1)} %pad_add_fusion.scal.refs_0_.place, bf16[2,512,256]{2,1,0:T(8,128)(2,1)S(1)} %get-tuple-element.84.own, bf16[1,512,256]{2,1,0:T(8,128)(2,1)S(1)} %collective-permute-done.14.in_came, ...), custom_call_target="tpu_custom_call" | custom-call | flops 2875000064 | bytes 1000000 | tf_op jit(solution)/shard_map/gram/pallas_call | solution.py:825
  131.4 4.0 %newton.2.refs_4_.refs_5_ = bf16[2,128,256]{2,1,0:T(8,128)(2,1)S(1)} custom-call(f32[2,4,64,64]{3,2,1,0:T(8,128)S(1)} %get-tuple-element.98.refs_0_, f32[2,4,64,64]{3,2,1,0:T(8,128)S(1)} %collective-permute-done.23.refs_1_, bf16[1,512,256]{2,1,0:T(8,128)(2,1)S(1)} %get-tuple-element.99.refs_2_.g0), custom_call_target="tpu_custom_call" | custom-call | flops 4024999936 | bytes 1000000 | tf_op jit(solution)/shard_map/newton/pallas_call | solution.py:475
  137.3 3.1 %newton.3 = (bf16[1,128,256]{2,1,0:T(8,128)(2,1)S(1)}, f32[8,8,256]{2,1,0:T(8,128)S(1)}) custom-call(f32[1,4,64,64]{3,2,1,0:T(8,128)S(1)} %get-tuple-element.96.refs_0_, f32[1,4,64,64]{3,2,1,0:T(8,128)S(1)} %collective-permute-done.21.refs_1_, f32[8,8,256]{2,1,0:T(8,128)S(1)} %get-tuple-element.97.refs_2_, f32[8,8,256]{2,1,0:T(8,128)S(1)} %collective-permute-done.22.refs_3_, ...), custom_call_target="tpu_custom_call" | custom-call | flops 4024999936 | bytes 1000000 | tf_op jit(solution)/shard_map/newton/pallas_call | solution.py:475
  145.0 6.8 %collective-permute-done.28.g2 = bf16[1,512,256]{2,1,0:T(8,128)(2,1)S(1)} collective-permute-done((bf16[1,512,256]{2,1,0:T(8,128)(2,1)S(1)}, bf16[1,512,256]{2,1,0:T(8,128)(2,1)S(1)}, u32[]{:S(2)}, u32[]{:S(2)}) %collective-permute-start.28) | collective-permute-done | bytes 262176 | tf_op jit(solution)/shard_map/ppermute | solution.py:1014
  152.6 4.0 %collective-permute-done.31 = f32[8,8,256]{2,1,0:T(8,128)S(1)} collective-permute-done((f32[8,8,256]{2,1,0:T(8,128)S(1)}, f32[8,8,256]{2,1,0:T(8,128)S(1)}, u32[]{:S(2)}, u32[]{:S(2)}) %collective-permute-start.31) | collective-permute-done | bytes 65568 | tf_op jit(solution)/shard_map/ppermute | solution.py:1017
  156.7 13.8 %update.2 = (f32[6,2048,128]{2,1,0:T(8,128)}, f32[6,2048,128]{2,1,0:T(8,128)}, f32[6,2048,128]{2,1,0:T(8,128)}) custom-call(s32[3]{0:T(128)S(1)} %pad_add_fusion.scal.refs_0_.place, bf16[2,512,256]{2,1,0:T(8,128)(2,1)S(1)} %get-tuple-element.95.refs_0_.refs_1_, bf16[2,2,640,256]{3,2,1,0:T(8,128)(2,1)S(1)} %collective-permute-done.27.refs_2_.refs_4_.refs_6_.refs_8_, ...), custom_call_target="tpu_custom_call" | custom-call | flops 12650000384 | bytes 1000000 | tf_op jit(solution)/shard_map/update/pallas_call | solution.py:475
  173.7 7.6 %update.3 = (f32[6,2048,128]{2,1,0:T(8,128)}, f32[6,2048,128]{2,1,0:T(8,128)}, f32[6,2048,128]{2,1,0:T(8,128)}) custom-call(s32[3]{0:T(128)S(1)} %pad_add_fusion.scal.refs_0_.place, bf16[1,512,256]{2,1,0:T(8,128)(2,1)S(1)} %get-tuple-element.99.refs_2_.g0, ...), custom_call_target="tpu_custom_call", output_to_operand_aliasing={{0}: (12, {}), {1}: (13, {}), {2}: (14, {})} | custom-call | flops 6325000192 | bytes 1000000 | tf_op jit(solution)/shard_map/update/pallas_call | solution.py:475
  (144 shorter events, 53.3 us)
Async XLA Ops:
  15.5 13.3 %collective-permute-start.4 = (bf16[1,512,256]{2,1,0:T(8,128)(2,1)S(1)}, bf16[1,512,256]{2,1,0:T(8,128)(2,1)S(1)}, u32[]{:S(2)}, u32[]{:S(2)}) collective-permute-start(bf16[1,512,256]{2,1,0:T(8,128)(2,1)S(1)} %collective-permute-done.2.refs_6_.refs_4_), channel_id=1, source_target_pairs={{0,4},{4,0},{8,12},{12,8},{16,20},{20,16},{24,28},{28,24},{1,5},{5... | collective-permute-start | bytes 786440 | tf_op jit(solution)/shard_map/ppermute | solution.py:1014
  27.4 15.1 %collective-permute-start.3 = (bf16[2,512,256]{2,1,0:T(8,128)(2,1)S(1)}, bf16[2,512,256]{2,1,0:T(8,128)(2,1)}, u32[]{:S(2)}, u32[]{:S(2)}) collective-permute-start(bf16[2,512,256]{2,1,0:T(8,128)(2,1)S(1)} %get-tuple-element.64.refs_3_), channel_id=1, source_target_pairs={{0,16},{4,20},{8,24},{12,28},{16,0},{20,4},{24,8},{28,12},{1,17},{... | collective-permute-start | bytes 1572872 | tf_op jit(solution)/shard_map/ppermute | solution.py:1014
  33.3 14.0 %all-to-all-start = ((bf16[8,128,256]{2,1,0:T(8,128)(2,1)}), bf16[8,128,256]{2,1,0:T(8,128)(2,1)S(1)}, u32[]{:S(2)}, u32[]{:S(2)}) async-start(bf16[8,128,256]{2,1,0:T(8,128)(2,1)} %project.1.refs_3_), calls=%async_computation | async-start | bytes 1048576 | tf_op jit(solution)/shard_map/all_to_all | solution.py:1057
  42.6 21.4 %collective-permute-start.7 = (bf16[2,512,256]{2,1,0:T(8,128)(2,1)}, bf16[2,512,256]{2,1,0:T(8,128)(2,1)}, u32[]{:S(2)}, u32[]{:S(2)}) collective-permute-start(bf16[2,512,256]{2,1,0:T(8,128)(2,1)} %collective-permute-done.3.refs_6_), channel_id=1, source_target_pairs={{0,4},{4,0},{8,12},{12,8},{16,20},{20,16},{24,28},{28,24},{1,5},{5... | collective-permute-start | bytes 1572872 | tf_op jit(solution)/shard_map/ppermute | solution.py:1014
  42.6 16.8 %collective-permute-start.8 = (bf16[2,512,256]{2,1,0:T(8,128)(2,1)}, bf16[2,512,256]{2,1,0:T(8,128)(2,1)}, u32[]{:S(2)}, u32[]{:S(2)}) collective-permute-start(bf16[2,512,256]{2,1,0:T(8,128)(2,1)} %collective-permute-done.3.refs_6_), channel_id=1, source_target_pairs={{0,8},{4,12},{8,0},{12,4},{16,24},{20,28},{24,16},{28,20},{1,9},{5... | collective-permute-start | bytes 1572872 | tf_op jit(solution)/shard_map/ppermute | solution.py:1014
  59.4 15.3 %collective-permute-start = (bf16[256,1024]{1,0:T(8,128)(2,1)}, bf16[256,1024]{1,0:T(8,128)(2,1)S(1)}, u32[]{:S(2)}, u32[]{:S(2)}) collective-permute-start(bf16[256,1024]{1,0:T(8,128)(2,1)} %bitcast.6.x.refs_1_), channel_id=1, source_target_pairs={{0,4},{4,0},{8,12},{12,8},{16,20},{20,16},{24,28},{28,24},{1,5},{5... | collective-permute-start | bytes 1572872 | tf_op jit(solution)/shard_map/ppermute | solution.py:1014
  59.9 14.8 %collective-permute-start.1 = (bf16[256,1024]{1,0:T(8,128)(2,1)}, bf16[256,1024]{1,0:T(8,128)(2,1)}, u32[]{:S(2)}, u32[]{:S(2)}) collective-permute-start(bf16[256,1024]{1,0:T(8,128)(2,1)} %bitcast.7.cot.refs_2_.refs_3_), channel_id=1, source_target_pairs={{0,4},{4,0},{8,12},{12,8},{16,20},{20,16},{24,28},{28,24},{1,5},{5... | collective-permute-start | bytes 1572872 | tf_op jit(solution)/shard_map/ppermute | solution.py:1014
  59.9 13.8 %all-to-all-start.1 = ((bf16[8,128,256]{2,1,0:T(8,128)(2,1)}), bf16[8,128,256]{2,1,0:T(8,128)(2,1)S(1)}, u32[]{:S(2)}, u32[]{:S(2)}) async-start(bf16[8,128,256]{2,1,0:T(8,128)(2,1)} %bitcast.20), calls=%async_computation.1 | async-start | bytes 1048576 | tf_op jit(solution)/shard_map/all_to_all | solution.py:1073
  74.6 12.5 %collective-permute-start.13 = (bf16[2,256,256]{2,1,0:T(8,128)(2,1)S(1)}, bf16[2,256,256]{2,1,0:T(8,128)(2,1)S(1)}, u32[]{:S(2)}, u32[]{:S(2)}) collective-permute-start(bf16[2,256,256]{2,1,0:T(8,128)(2,1)S(1)} %get-tuple-element.77.refs_4_), channel_id=1, source_target_pairs={{0,4},{4,0},{8,12},{12,8},{16,20},{20,16},{24,28},{28,24},{1,5},{5... | collective-permute-start | bytes 786440 | tf_op jit(solution)/shard_map/ppermute | solution.py:1014
  78.9 16.3 %collective-permute-start.11 = (bf16[2,512,256]{2,1,0:T(8,128)(2,1)S(1)}, bf16[2,512,256]{2,1,0:T(8,128)(2,1)S(1)}, u32[]{:S(2)}, u32[]{:S(2)}) collective-permute-start(bf16[2,512,256]{2,1,0:T(8,128)(2,1)S(1)} %get-tuple-element.73), channel_id=1, source_target_pairs={{0,16},{4,20},{8,24},{12,28},{16,0},{20,4},{24,8},{28,12},{1,17},{... | collective-permute-start | bytes 1572872 | tf_op jit(solution)/shard_map/ppermute | solution.py:1014
  80.8 14.3 %collective-permute-start.12 = (bf16[2,512,256]{2,1,0:T(8,128)(2,1)S(1)}, bf16[2,512,256]{2,1,0:T(8,128)(2,1)S(1)}, u32[]{:S(2)}, u32[]{:S(2)}) collective-permute-start(bf16[2,512,256]{2,1,0:T(8,128)(2,1)S(1)} %get-tuple-element.75), channel_id=1, source_target_pairs={{0,8},{4,12},{8,0},{12,4},{16,24},{20,28},{24,16},{28,20},{1,9},{5... | collective-permute-start | bytes 1572872 | tf_op jit(solution)/shard_map/ppermute | solution.py:1014
  85.4 13.5 %collective-permute-start.16 = (bf16[2,2,64,1024]{3,2,1,0:T(8,128)(2,1)S(1)}, bf16[2,2,64,1024]{3,2,1,0:T(8,128)(2,1)S(1)}, u32[]{:S(2)}, u32[]{:S(2)}) collective-permute-start(bf16[2,2,64,1024]{3,2,1,0:T(8,128)(2,1)S(1)} %get-tuple-element.88), channel_id=1, source_target_pairs={{0,1},{1,0},{2,3},{3,2},{4,5},{5,4},{6,7},{7,6},{8,9},{9,8},{10,11... | collective-permute-start | bytes 1572872 | tf_op jit(solution)/shard_map/ppermute | solution.py:1017
  90.3 17.7 %collective-permute-start.18 = (bf16[2,640,256]{2,1,0:T(8,128)(2,1)S(1)}, bf16[2,640,256]{2,1,0:T(8,128)(2,1)S(1)}, u32[]{:S(2)}, u32[]{:S(2)}) collective-permute-start(bf16[2,640,256]{2,1,0:T(8,128)(2,1)S(1)} %get-tuple-element.91), channel_id=1, source_target_pairs={{0,16},{4,20},{8,24},{12,28},{16,0},{20,4},{24,8},{28,12},{1,17},{... | collective-permute-start | bytes 1966088 | tf_op jit(solution)/shard_map/ppermute | solution.py:1014
  95.4 21.8 %collective-permute-start.14 = (bf16[1,512,256]{2,1,0:T(8,128)(2,1)S(1)}, bf16[1,512,256]{2,1,0:T(8,128)(2,1)S(1)}, u32[]{:S(2)}, u32[]{:S(2)}) collective-permute-start(bf16[1,512,256]{2,1,0:T(8,128)(2,1)S(1)} %get-tuple-element.85.refs_2_), channel_id=1, source_target_pairs={{0,8},{4,12},{8,0},{12,4},{16,24},{20,28},{24,16},{28,20},{1,9},{5... | collective-permute-start | bytes 786440 | tf_op jit(solution)/shard_map/ppermute | solution.py:1014
  96.3 20.9 %collective-permute-start.15 = (bf16[1,512,256]{2,1,0:T(8,128)(2,1)S(1)}, bf16[1,512,256]{2,1,0:T(8,128)(2,1)S(1)}, u32[]{:S(2)}, u32[]{:S(2)}) collective-permute-start(bf16[1,512,256]{2,1,0:T(8,128)(2,1)S(1)} %get-tuple-element.86), channel_id=1, source_target_pairs={{0,16},{4,20},{8,24},{12,28},{16,0},{20,4},{24,8},{28,12},{1,17},{... | collective-permute-start | bytes 786440 | tf_op jit(solution)/shard_map/ppermute | solution.py:1014
  99.0 18.2 %collective-permute-start.17 = (bf16[2,64,1024]{2,1,0:T(8,128)(2,1)S(1)}, bf16[2,64,1024]{2,1,0:T(8,128)(2,1)S(1)}, u32[]{:S(2)}, u32[]{:S(2)}) collective-permute-start(bf16[2,64,1024]{2,1,0:T(8,128)(2,1)S(1)} %get-tuple-element.90), channel_id=1, source_target_pairs={{0,2},{1,3},{2,0},{3,1},{4,6},{5,7},{6,4},{7,5},{8,10},{9,11},{10,... | collective-permute-start | bytes 786440 | tf_op jit(solution)/shard_map/ppermute | solution.py:1017
  108.3 17.4 %collective-permute-start.20 = (bf16[640,256]{1,0:T(8,128)(2,1)S(1)}, bf16[640,256]{1,0:T(8,128)(2,1)S(1)}, u32[]{:S(2)}, u32[]{:S(2)}) collective-permute-start(bf16[640,256]{1,0:T(8,128)(2,1)S(1)} %get-tuple-element.94), channel_id=1, source_target_pairs={{0,8},{4,12},{8,0},{12,4},{16,24},{20,28},{24,16},{28,20},{1,9},{5... | collective-permute-start | bytes 983048 | tf_op jit(solution)/shard_map/ppermute | solution.py:1014
  121.0 14.5 %collective-permute-start.19 = (bf16[2,64,1024]{2,1,0:T(8,128)(2,1)S(1)}, bf16[2,64,1024]{2,1,0:T(8,128)(2,1)S(1)}, u32[]{:S(2)}, u32[]{:S(2)}) collective-permute-start(bf16[2,64,1024]{2,1,0:T(8,128)(2,1)S(1)} %get-tuple-element.93.refs_4_), channel_id=1, source_target_pairs={{0,2},{1,3},{2,0},{3,1},{4,6},{5,7},{6,4},{7,5},{8,10},{9,11},{10,... | collective-permute-start | bytes 786440 | tf_op jit(solution)/shard_map/ppermute | solution.py:1017
  125.1 12.2 %collective-permute-start.24 = (bf16[2,512,256]{2,1,0:T(8,128)(2,1)S(1)}, bf16[2,512,256]{2,1,0:T(8,128)(2,1)S(1)}, u32[]{:S(2)}, u32[]{:S(2)}) collective-permute-start(bf16[2,512,256]{2,1,0:T(8,128)(2,1)S(1)} %get-tuple-element.95.refs_0_.refs_1_), channel_id=1, source_target_pairs={{0,8},{4,12},{8,0},{12,4},{16,24},{20,28},{24,16},{28,20},{1,9},{5... | collective-permute-start | bytes 1572872 | tf_op jit(solution)/shard_map/ppermute | solution.py:1014
  140.6 16.0 %collective-permute-start.27 = (bf16[2,2,640,256]{3,2,1,0:T(8,128)(2,1)S(1)}, bf16[2,2,640,256]{3,2,1,0:T(8,128)(2,1)S(1)}, u32[]{:S(2)}, u32[]{:S(2)}) collective-permute-start(bf16[2,2,640,256]{3,2,1,0:T(8,128)(2,1)S(1)} %pad_maximum_fusion), channel_id=1, source_target_pairs={{0,4},{4,0},{8,12},{12,8},{16,20},{20,16},{24,28},{28,24},{1,5},{5... | collective-permute-start | bytes 3932168 | tf_op jit(solution)/shard_map/ppermute | solution.py:1014
  140.8 15.8 %collective-permute-start.25 = (bf16[2,2,64,1024]{3,2,1,0:T(8,128)(2,1)S(1)}, bf16[2,2,64,1024]{3,2,1,0:T(8,128)(2,1)S(1)}, u32[]{:S(2)}, u32[]{:S(2)}) collective-permute-start(bf16[2,2,64,1024]{3,2,1,0:T(8,128)(2,1)S(1)} %pad_maximum_fusion.2), channel_id=1, source_target_pairs={{0,1},{1,0},{2,3},{3,2},{4,5},{5,4},{6,7},{7,6},{8,9},{9,8},{10,11... | collective-permute-start | bytes 1572872 | tf_op jit(solution)/shard_map/ppermute | solution.py:1017
  144.6 12.0 %collective-permute-start.31 = (f32[8,8,256]{2,1,0:T(8,128)S(1)}, f32[8,8,256]{2,1,0:T(8,128)S(1)}, u32[]{:S(2)}, u32[]{:S(2)}) collective-permute-start(f32[8,8,256]{2,1,0:T(8,128)S(1)} %get-tuple-element.111), channel_id=1, source_target_pairs={{0,1},{1,0},{2,3},{3,2},{4,5},{5,4},{6,7},{7,6},{8,9},{9,8},{10,11... | collective-permute-start | bytes 196616 | tf_op jit(solution)/shard_map/ppermute | solution.py:1017
  152.5 21.1 %collective-permute-start.30 = (bf16[2,1,640,256]{3,2,1,0:T(8,128)(2,1)S(1)}, bf16[2,1,640,256]{3,2,1,0:T(8,128)(2,1)S(1)}, u32[]{:S(2)}, u32[]{:S(2)}) collective-permute-start(bf16[2,1,640,256]{3,2,1,0:T(8,128)(2,1)S(1)} %pad_maximum_fusion.1), channel_id=1, source_target_pairs={{0,4},{4,0},{8,12},{12,8},{16,20},{20,16},{24,28},{28,24},{1,5},{5... | collective-permute-start | bytes 1966088 | tf_op jit(solution)/shard_map/ppermute | solution.py:1014
  170.5 10.8 %collective-permute-start.32 = (f32[8,8,256]{2,1,0:T(8,128)S(1)}, f32[8,8,256]{2,1,0:T(8,128)S(1)}, u32[]{:S(2)}, u32[]{:S(2)}) collective-permute-start(f32[8,8,256]{2,1,0:T(8,128)S(1)} %add.69), channel_id=1, source_target_pairs={{0,2},{1,3},{2,0},{3,1},{4,6},{5,7},{6,4},{7,5},{8,10},{9,11},{10,... | collective-permute-start | bytes 196616 | tf_op jit(solution)/shard_map/ppermute | solution.py:1017
  (31 other events, 219.5 us)
